TPU v7x, 128 devices: a whole 4x4x4 slice. The times are simulated.
128 devices in a mesh: prow: 8 (over y, x_lo), pcol: 16 (over z, x_hi, core).
Axes of the slice: x: 4 (x_hi: 2, x_lo: 2; x = x_hi * 2 + x_lo), y: 4, z: 4, core: 2. Of those that a mesh axis runs over, the one named last changes fastest.
Arguments:
- inverse_anc: bfloat16 [8192, 8192], P('prow', 'pcol')
- factor_one: bfloat16 [8192, 4096], P('prow', 'pcol'), may hold values from -0.75 to 0.75
- factor_zero: bfloat16 [8192, 8192], P('prow', 'pcol'), may hold values from -0.75 to 0.75
- factor_parent: bfloat16 [256, 8192], replicated, may hold values from -0.75 to 0.75
- dinv_one: float32 [256, 4096], P(None, 'pcol'), may hold values from -6 to 6
- dinv_zero: float32 [256, 8192], P(None, 'pcol'), may hold values from -6 to 6
- struct_one: int32 [16, 16], replicated, may hold values from 0 to 31, all different within a row
- select_zero: int32 [32, 8], replicated, may hold values from 0 to 15, all different within a row
- parent: int32 [32], replicated, may hold values from 0 to 15
Outputs:
- upper_one: bfloat16 [8192, 4096], P('prow', 'pcol')
- diag_one: float32 [256, 4096], P(None, 'pcol')
- upper_zero: bfloat16 [8192, 8192], P('prow', 'pcol')
- upper_parent: bfloat16 [256, 8192], P(None, 'pcol')
- diag_zero: float32 [256, 8192], P(None, 'pcol')
Inputs may be any that keep to these rules, and one draw needn't show every extreme that they name: `struct_one`: each row names 16 different ancestor blocks. `select_zero`: each row names 8 different positions.
All inputs are finite; a program needn't handle non-finite values.
Results may differ from a plain program's by a relative error of at most 0.0034.
The roundings to bfloat16 on the way count: a program that leaves them out, or rounds other values in their place, can miss the bound.
Values may be sent and summed in bfloat16 or wider, within the bound.
No kernel may reach another device: no remote copies, remote signals or barrier semaphores. Data moves between devices by JAX's collectives and lax.ppermute only.
A program may use at most 192 MiB of HBM per device.

v0:
```python
import jax
import jax.numpy as jnp
from jax import lax
from jax.sharding import PartitionSpec as P


def block_mask(blocks, first_block, block_count, blk_width):
    wanted = first_block + jnp.arange(block_count, dtype=jnp.int32)
    matched = jnp.any(blocks[:, :, None] == wanted[None, None, :], axis=1)
    return jnp.repeat(jnp.repeat(matched.T, blk_width, axis=0), blk_width, axis=1)


def child_ancestors(struct_one, select_zero, parent):
    parent_rows = jnp.take(struct_one, parent, axis=0)
    return jnp.take_along_axis(parent_rows, select_zero, axis=1)


def block_products(left_side, right_side, group_count, blk_width):
    row_total = left_side.shape[0]
    return jnp.einsum(
        "nik,nil->kil",
        left_side.reshape(row_total, group_count, blk_width),
        right_side.reshape(row_total, group_count, blk_width),
        preferred_element_type=jnp.float32,
    ).reshape(blk_width, group_count * blk_width)


def shards(
    inverse_anc,
    factor_one,
    factor_zero,
    factor_parent,
    dinv_one,
    dinv_zero,
    struct_one,
    select_zero,
    parent,
):
    blk_width = factor_parent.shape[0]
    local_rows = inverse_anc.shape[0]
    row_blocks = local_rows // blk_width
    grid_cols = lax.axis_size("pcol")
    row_index = lax.axis_index("prow")
    col_index = lax.axis_index("pcol")
    sup_total = struct_one.shape[0]
    kid_total = parent.shape[0]
    own_sups = sup_total // grid_cols
    own_kids = kid_total // grid_cols
    zero_half = jnp.zeros((), jnp.bfloat16)
    ancestors = child_ancestors(struct_one, select_zero, parent)
    sup_struct = lax.dynamic_slice_in_dim(struct_one, col_index * own_sups, own_sups, 0)
    kid_struct = lax.dynamic_slice_in_dim(ancestors, col_index * own_kids, own_kids, 0)
    mask_one = block_mask(sup_struct, row_index * row_blocks, row_blocks, blk_width)
    mask_zero = block_mask(kid_struct, row_index * row_blocks, row_blocks, blk_width)
    low_one = jnp.where(mask_one, factor_one, zero_half)
    low_zero = jnp.where(mask_zero, factor_zero, zero_half)
    kid_parent = lax.dynamic_slice_in_dim(
        factor_parent, col_index * own_kids * blk_width, own_kids * blk_width, 1
    )
    kid_parents = lax.dynamic_slice_in_dim(parent, col_index * own_kids, own_kids, 0)
    inv_rows = lax.all_gather(inverse_anc, "pcol", axis=1, tiled=True)
    full_one, full_zero = (
        lax.all_gather(low_one, "prow", axis=0, tiled=True),
        lax.all_gather(low_zero, "prow", axis=0, tiled=True),
    )
    first_term = jnp.dot(inv_rows, full_one, preferred_element_type=jnp.float32)
    upper_one = jnp.where(mask_one, -first_term, 0.0).astype(jnp.bfloat16)
    diag_one = dinv_one - lax.psum(block_products(low_one, upper_one, own_sups, blk_width), "prow")
    diag_half = diag_one.astype(jnp.bfloat16)
    blocks_up, blocks_diag = (
        lax.all_gather(upper_one, "pcol", axis=1, tiled=True),
        lax.all_gather(diag_half, "pcol", axis=1, tiled=True),
    )
    up_pick = jnp.take(blocks_up.reshape(local_rows, sup_total, blk_width), kid_parents, axis=1)
    kid_blocks = kid_parent.reshape(blk_width, own_kids, blk_width)
    second = jnp.einsum(
        "rcj,jcl->rcl", up_pick, kid_blocks, preferred_element_type=jnp.float32
    ).reshape(local_rows, own_kids * blk_width)
    total_sum = jnp.dot(inv_rows, full_zero, preferred_element_type=jnp.float32) + second
    upper_zero = jnp.where(mask_zero, -total_sum, 0.0).astype(jnp.bfloat16)
    picked = jnp.einsum(
        "rcj,rcl->jcl",
        up_pick,
        low_zero.reshape(local_rows, own_kids, blk_width),
        preferred_element_type=jnp.float32,
    )
    cross_sum = lax.psum(picked, "prow")
    diag_pick = jnp.take(blocks_diag.reshape(blk_width, sup_total, blk_width), kid_parents, axis=1)
    diag_term = jnp.einsum(
        "icj,jcl->icl", diag_pick, kid_blocks, preferred_element_type=jnp.float32
    )
    upper_parent = (
        (-(cross_sum + diag_term)).reshape(blk_width, own_kids * blk_width).astype(jnp.bfloat16)
    )
    diag_sum = lax.psum(block_products(low_zero, upper_zero, own_kids, blk_width), "prow")
    own_term = jnp.einsum(
        "jck,jcl->kcl",
        kid_parent.reshape(blk_width, own_kids, blk_width),
        upper_parent.reshape(blk_width, own_kids, blk_width),
        preferred_element_type=jnp.float32,
    ).reshape(blk_width, own_kids * blk_width)
    diag_zero = dinv_zero - diag_sum - own_term
    return (upper_one, diag_one, upper_zero, upper_parent, diag_zero)


def solution(mesh):
    in_specs = (
        P("prow", "pcol"),
        P("prow", "pcol"),
        P("prow", "pcol"),
        P(),
        P(None, "pcol"),
        P(None, "pcol"),
        P(),
        P(),
        P(),
    )
    out_specs = (
        P("prow", "pcol"),
        P(None, "pcol"),
        P("prow", "pcol"),
        P(None, "pcol"),
        P(None, "pcol"),
    )
    return jax.shard_map(shards, mesh=mesh, in_specs=in_specs, out_specs=out_specs, check_vma=False)
```

profile of v0, /device:TPU:0, one launch (start us, length us, event | category | flops | bytes accessed | tf_op | source)
XLA Modules:
  0.0 640.5 jit_solution(1563731308044970730)
XLA Ops:
  7.2 0.0 copy-start
  7.2 0.0 all-gather.6.cloned.1.call-start
  7.2 0.6 copy-done
  7.9 0.2 compare_reduce_fusion.1
  8.1 0.1 broadcast_in_dim.70
  8.2 2.0 broadcast_select_fusion.1
  10.2 0.0 all-gather.6.cloned.1.call-update
  10.2 0.0 all-gather.8.cloned.1.call-start
  10.3 0.7 all-gather.8.cloned.1.call-update
  11.0 0.0 copy-start.9
  11.0 0.0 copy-start.10
  11.0 0.0 all-gather.12.cloned.1.call-start
  11.0 92.5 %all-gather.6.cloned.1.call-done = bf16[8192,256]{1,0:T(8,128)(2,1)} async-done(((bf16[1024,256]{1,0:T(8,128)(2,1)}), bf16[8192,256]{1,0:T(8,128)(2,1)}) %all-gather.6.cloned.1.call-update) | async-done | bytes 4194320 | tf_op jit(solution)/shard_map/all_gather | solution.py:63
  103.6 121.4 %all-gather.8.cloned.1.call-done = bf16[1024,8192]{1,0:T(8,128)(2,1)} async-done(((bf16[1024,512]{1,0:T(8,128)(2,1)}), bf16[1024,8192]{1,0:T(8,128)(2,1)}) %all-gather.8.cloned.1.call-update) | async-done | bytes 16777232 | tf_op jit(solution)/shard_map/all_gather | solution.py:61
  225.0 12.4 %fusion.3 = bf16[256,1024]{1,0:T(8,128)(2,1)} fusion(bf16[8192,256]{1,0:T(8,128)(2,1)} %all-gather.6.cloned.1.call-done, bf16[1024,8192]{1,0:T(8,128)(2,1)} %all-gather.8.cloned.1.call-done, pred[1024]{0:T(1024)(128)(4,1)S(1)} %broadcast_in_dim.71), kind=kOutput, calls=%fused_computation.11 | convolution fusion | flops 4295753728 | bytes 21496832 | tf_op jit(solution)/shard_map/dot_general | solution.py:66
  237.4 0.0 all-gather.12.cloned.1.call-update
  237.4 0.0 all-gather.10.cloned.1.call-start
  237.5 0.0 copy-done.9
  237.5 0.1 copy.43
  237.6 0.1 reshape.181
  237.7 0.6 gather_fusion
  238.3 0.1 broadcast_select_fusion.4
  238.4 1.9 gather_fusion.3
  240.3 0.0 copy-start.3
  240.3 0.0 copy-start.4
  240.3 0.1 reshape.184
  240.5 0.2 compare_reduce_fusion
  240.7 0.1 broadcast_bitcast_fusion
  240.8 0.5 copy.46
  241.3 1.0 bitcast_select_fusion.1
  242.3 0.0 all-gather.10.cloned.1.call-update
  242.4 0.2 all-reduce.3.cloned.1.call-start
  242.6 1.0 constant_dynamic-slice_fusion
  243.6 0.1 copy.47
  243.7 0.1 compare_and_fusion
  243.8 1.0 convolution_bitcast_fusion.2
  244.8 63.0 %all-gather.12.cloned.1.call-done = bf16[1024,4096]{0,1:T(8,128)(2,1)} async-done(((bf16[1024,256]{0,1:T(8,128)(2,1)}), bf16[1024,4096]{0,1:T(8,128)(2,1)}) %all-gather.12.cloned.1.call-update) | async-done | bytes 8388624 | tf_op jit(solution)/shard_map/all_gather | solution.py:71
  307.8 12.4 %copy.48 = bf16[1024,16,256]{2,0,1:T(8,128)(2,1)} copy(bf16[1024,16,256]{0,2,1:T(8,128)(2,1)} %bitcast.79) | data formatting | bytes 16777216 | tf_op jit(solution)/shard_map/reshape | solution.py:74
  320.2 4.0 gather_fusion.1
  324.2 1.3 convolution_bitcast_fusion
  325.5 1.9 fusion.8
  327.4 148.5 %all-gather.10.cloned.1.call-done = bf16[8192,512]{0,1:T(8,128)(2,1)} async-done(((bf16[1024,512]{0,1:T(8,128)(2,1)}), bf16[8192,512]{0,1:T(8,128)(2,1)}) %all-gather.10.cloned.1.call-update) | async-done | bytes 8388624 | tf_op jit(solution)/shard_map/all_gather | solution.py:64
  475.9 15.2 %fusion = bf16[1024,512]{0,1:T(8,128)(2,1)S(1)} fusion(f32[2,256,1024]{2,1,0:T(8,128)} %fusion.8, bf16[8192,512]{0,1:T(8,128)(2,1)} %all-gather.10.cloned.1.call-done, bf16[1024,8192]{1,0:T(8,128)(2,1)} %all-gather.8.cloned.1.call-done, pred[1024,2]{0,1:T(4,128)(4,1)S(1)} %bitcast.91), kind=kOutput, calls=%fused_computation.6 | convolution fusion | flops 8592031744 | bytes 28313600 | tf_op jit(solution)/shard_map/dot_general | solution.py:79
  491.1 0.5 fusion.19
  491.6 1.0 copy.51
  492.6 0.0 all-reduce.3.cloned.1.call-update
  492.6 0.0 all-gather.14.cloned.1.call-start
  492.6 1.1 copy.42
  493.7 83.5 %all-reduce.3.cloned.1.call-done = (f32[256,256]{0,1:T(8,128)}, f32[256,2,256]{0,2,1:T(8,128)}, f32[256,512]{1,0:T(8,128)}) async-done(((f32[256,256]{0,1:T(8,128)}, f32[256,2,256]{0,2,1:T(8,128)}, f32[256,512]{1,0:T(8,128)}), (f32[256,256]{0,1:T(8,128)}, f32[256,2,256]{0,2,1:T(8,128)}, f32[256,512]{1,0:T(8,128)})) %all-reduce.3.cloned.1.call-update) | async-done | bytes 1310736 | tf_op jit(solution)/shard_map/psum | solution.py:68
  577.3 1.7 fusion.18
  578.9 0.0 all-gather.14.cloned.1.call-update
  579.0 1.0 copy.54
  580.0 1.3 copy.56
  581.3 0.8 copy.55
  582.1 45.4 %all-gather.14.cloned.1.call-done = bf16[256,4096]{0,1:T(8,128)(2,1)} async-done(((bf16[256,256]{0,1:T(8,128)(2,1)}), bf16[256,4096]{0,1:T(8,128)(2,1)}) %all-gather.14.cloned.1.call-update) | async-done | bytes 2097168 | tf_op jit(solution)/shard_map/all_gather | solution.py:72
  627.5 2.9 copy.49
  630.4 0.6 gather_fusion.2
  631.0 0.0 copy-start.7
  631.0 0.3 fusion.6
  631.3 0.3 fusion.20
  631.6 0.2 copy.53
  631.8 0.8 copy.57
  632.7 0.9 subtract_subtract_fusion
  633.6 0.0 copy-done.1
  (24 shorter events, 0.1 us)
Async XLA Ops:
  7.2 0.7 copy-start
  7.2 96.4 %all-gather.6.cloned.1.call-start = ((), (), s32[]{:S(2)}) async-start(), calls=%async_computation | async-start | bytes 4718592 | tf_op jit(solution)/shard_map/all_gather | solution.py:63
  10.2 214.8 %all-gather.8.cloned.1.call-start = ((), (), s32[]{:S(2)}) async-start(), calls=%async_computation.1 | async-start | bytes 17825792 | tf_op jit(solution)/shard_map/all_gather | solution.py:61
  11.0 226.5 %copy-start.9 = (s32[32,8]{0,1:T(8,128)S(1)}, s32[32,8]{0,1:T(8,128)}, u32[]{:S(2)}) copy-start(s32[32,8]{0,1:T(8,128)} %param.16) | copy-start | bytes 3076
  11.0 226.7 %copy-start.10 = (s32[32]{0:T(128)S(1)}, s32[32]{0:T(128)}, u32[]{:S(2)}) copy-start(s32[32]{0:T(128)} %param.17) | copy-start | bytes 388
  11.0 296.8 %all-gather.12.cloned.1.call-start = ((), (), s32[]{:S(2)}) async-start(), calls=%async_computation.3 | async-start | bytes 8912896 | tf_op jit(solution)/shard_map/all_gather | solution.py:71
  237.4 238.5 %all-gather.10.cloned.1.call-start = ((), (), s32[]{:S(2)}) async-start(), calls=%async_computation.2 | async-start | bytes 9437184 | tf_op jit(solution)/shard_map/all_gather | solution.py:64
  238.4 2.4 copy-start.5
  240.3 3.5 copy-start.3
  240.3 3.5 copy-start.4
  242.4 334.9 %all-reduce.3.cloned.1.call-start = ((), (), s32[]{:S(2)}) async-start(), calls=%async_computation.5 | async-start | bytes 2621440 | tf_op jit(solution)/shard_map/psum | solution.py:68
  307.8 16.4 %copy-start.2 = (bf16[1024,512]{0,1:T(8,128)(2,1)S(1)}, bf16[1024,512]{0,1:T(8,128)(2,1)}, u32[]{:S(2)}) copy-start(bf16[1024,512]{0,1:T(8,128)(2,1)} %bitcast_select_fusion.1) | copy-start | bytes 3145732
  492.6 134.9 %all-gather.14.cloned.1.call-start = ((), (), s32[]{:S(2)}) async-start(), calls=%async_computation.4 | async-start | bytes 2228224 | tf_op jit(solution)/shard_map/all_gather | solution.py:72
  579.0 52.0 %copy-start.6 = (f32[256,2,256]{0,2,1:T(8,128)S(1)}, f32[256,2,256]{0,2,1:T(8,128)}, u32[]{:S(2)}) copy-start(f32[256,2,256]{0,2,1:T(8,128)} %get-tuple-element.21) | copy-start | bytes 1572868
  627.5 6.1 copy-start.1
  631.0 1.7 copy-start.7
  631.0 1.7 copy-start.8
Sparse Core Ops, SparseCore 0:
  10.3 93.1 all-gather.5
  105.9 119.0 all-gather.7
  237.6 70.2 all-gather.11
  309.9 166.0 all-gather.9
  492.7 84.5 all-reduce.2
  580.2 47.3 all-gather.13
where the time goes:
time: 642 us; the launch traced here: 640 us
  waiting for transfers between devices  555 us (86%)
  matrix products  32.9 us (5%)
  local copies, waits for them, and re-layouts  31.3 us (5%)
  between operations  14.4 us (2%)
    all_gather x1, waiting for transfers between devices, shards(): lax.all_gather(low_zero, 'prow', axis=0, tiled=True)  148 us
    all_gather x1, waiting for transfers between devices, shards(): inv_rows = lax.all_gather(inverse_anc, 'pcol', axis=1, tiled=True)  121 us
    all_gather x1, waiting for transfers between devices, shards(): lax.all_gather(low_one, 'prow', axis=0, tiled=True)  92.5 us
    psum x1, waiting for transfers between devices, shards(): lax.psum(block_products(low_one, upper_one, own_sups, blk_width), 'prow')  83.5 us
    all_gather x1, waiting for transfers between devices, shards(): lax.all_gather(upper_one, 'pcol', axis=1, tiled=True)  63 us
    all_gather x1, waiting for transfers between devices, shards(): lax.all_gather(diag_half, 'pcol', axis=1, tiled=True)  45.4 us
    dot_general x1, matrix products, shards(): jnp.dot(inv_rows, full_zero, preferred_element_type=jnp.float32) + second  15.2 us
  transfers between devices with their start and end apart: 6, of which 6 were waited for; matrix products, arithmetic and copies ran while one was open for 5% of the time, Pallas kernels for 0%

commit v1 on v0

v1 whole, which is shorter than its diff:
```python
import jax
import jax.numpy as jnp
from jax import lax
from jax.experimental import pallas as pl
from jax.experimental.pallas import tpu as pltpu
from jax.sharding import PartitionSpec as P

MESH_AXES = ("prow", "pcol")
BF = jnp.bfloat16
F32 = jnp.float32
B = 256
LOC = 1024
PIECES = ((0, 0), (0, 1), (-1, 0), (1, 0), (-1, 1), (1, 1), (2, 0), (2, 1))
SLICES = ((0, 0), (0, 1), (-1, 0), (1, 0), (-1, 1), (1, 1), (2, 0), (2, 1))


def moves(dy=0, dxl=0, dz=0, dxh=0, dcore=0):
    pairs = []
    for y in range(4):
        for xl in range(2):
            for z in range(4):
                for xh in range(2):
                    for core in range(2):
                        src = (y * 2 + xl) * 16 + z * 4 + xh * 2 + core
                        dst = (((y + dy) % 4) * 2 + (xl ^ dxl)) * 16
                        dst += ((z + dz) % 4) * 4 + (xh ^ dxh) * 2 + (core ^ dcore)
                        pairs.append((src, dst))
    return pairs


X_HI = moves(dxh=1)
X_LO = moves(dxl=1)
Z_UP = moves(dz=1)
Z_DOWN = moves(dz=-1)
Y_UP = moves(dy=1)
Y_DOWN = moves(dy=-1)
SIBLING = moves(dcore=1)


def send(block, pairs):
    return lax.ppermute(block, MESH_AXES, pairs)


def ring_gather(own, swap, up, down):
    half = own.shape[0] // 2
    other = send(own, swap)
    below, above = send(own, up), send(own, down)
    other_below, other_above = send(other, up), send(other, down)
    far = (send(below[:half], up), send(above[half:], down))
    other_far = (send(other_below[:half], up), send(other_above[half:], down))
    return [(own,), (other,), (below,), (above,), (other_below,), (other_above,), far, other_far]


def dot(left, right):
    return jnp.dot(left, right, preferred_element_type=F32)


def dot_t(left, right):
    return lax.dot_general(left, right, (((0,), (0,)), ((), ())), preferred_element_type=F32)


VMEM = pl.BlockSpec(memory_space=pltpu.VMEM)
SMEM = pl.BlockSpec(memory_space=pltpu.SMEM)
ANY = pl.BlockSpec(memory_space=pl.ANY)


def call(body, out_shape, in_specs, scratch=(), limit=32):
    outs = [VMEM] * len(out_shape) if isinstance(out_shape, list) else VMEM
    return pl.pallas_call(
        body,
        out_shape=out_shape,
        in_specs=in_specs,
        out_specs=outs,
        scratch_shapes=list(scratch),
        compiler_params=pltpu.CompilerParams(vmem_limit_bytes=limit * 2**20),
    )


SLOT_AT = 0
SLICE_AT = 96
ROW_AT = 104
PAR_AT = 116


def halves(refs):
    if len(refs) == 1:
        return [(refs[0], 0), (refs[0], LOC // 2)]
    return [(refs[0], 0), (refs[1], 0)]


def level_one_body(counts, tab, *refs):
    inv_counts, low_counts = counts
    pos = 0
    inv_refs, low_refs = [], []
    for count in inv_counts:
        inv_refs.append(refs[pos : pos + count])
        pos += count
    for count in low_counts:
        low_refs.append(refs[pos : pos + count])
        pos += count
    own_ref, up_ref, part_ref, diag_ref, inv_s, low_s, acc, inv_sem, low_sem = refs[pos:]
    low_copies = []
    for q, group in enumerate(low_refs):
        at = pl.ds(pl.multiple_of(tab[SLICE_AT + q] * 32, 32), 32)
        span = 32 // len(group)
        for h, ref in enumerate(group):
            low_copies.append(
                pltpu.make_async_copy(
                    ref, low_s.at[pl.ds(h * span, span), at, :], low_sem.at[q, h]
                )
            )
    for copy in low_copies:
        copy.start()
    half = LOC // 2
    for q, group in enumerate(inv_refs):
        for hc in range(2):
            for hr, (ref, start) in enumerate(halves(group)):
                pltpu.make_async_copy(
                    ref.at[pl.ds(start, half), pl.ds(hc * B, B)],
                    inv_s.at[2 * q + hc, pl.ds(hr * half, half), :],
                    inv_sem.at[2 * q + hc, hr],
                ).start()
    acc[...] = jnp.zeros_like(acc)
    part_ref[...] = jnp.zeros_like(part_ref)
    diag_ref[...] = jnp.zeros_like(diag_ref)
    for copy in low_copies:
        copy.wait()

    def step(b, carry):
        for hr in range(2):
            view = inv_s.at[b, pl.ds(hr * half, half), :]
            pltpu.make_async_copy(view, view, inv_sem.at[b, hr]).wait()
        slot = tab[SLOT_AT + b]

        @pl.when(slot >= 0)
        def _():
            acc[...] += dot(inv_s[b], low_s[slot])

        for e in range(2):
            kid_slot = tab[SLOT_AT + 32 * (e + 1) + b]
            for rb in range(4):

                @pl.when((kid_slot >= 0) & (tab[ROW_AT + 4 * (e + 1) + rb] > 0))
                def _():
                    rows, cols = pl.ds(rb * B, B), pl.ds(e * B, B)
                    part_ref[rows, cols] += dot(inv_s[b, rows, :], low_s[kid_slot])

        return carry

    lax.fori_loop(0, 32, step, 0)
    for rb in range(4):
        rows = pl.ds(rb * B, B)
        up_ref[rows, :] = jnp.zeros((B, B), BF)

        @pl.when(tab[ROW_AT + rb] > 0)
        def _():
            up = (-acc[rows, :]).astype(BF)
            up_ref[rows, :] = up
            diag_ref[...] += dot_t(own_ref[rows, :], up)


def level_one(tab, inv_pieces, low_pieces, factor_one):
    counts = ([len(p) for p in inv_pieces], [len(p) for p in low_pieces])
    flat = [a for p in inv_pieces for a in p] + [a for p in low_pieces for a in p]

    def body(tab_ref, *refs):
        level_one_body(counts, tab_ref, *refs)

    return call(
        body,
        [
            jax.ShapeDtypeStruct((LOC, B), BF),
            jax.ShapeDtypeStruct((LOC, 2 * B), F32),
            jax.ShapeDtypeStruct((B, B), F32),
        ],
        [SMEM] + [ANY] * len(flat) + [VMEM],
        [
            pltpu.VMEM((32, LOC, B), BF),
            pltpu.VMEM((32, B, B), BF),
            pltpu.VMEM((LOC, B), F32),
            pltpu.SemaphoreType.DMA((32, 2)),
            pltpu.SemaphoreType.DMA((8, 2)),
        ],
        limit=48,
    )(tab, *flat, factor_one)


def pack_body(parent, spread, terms, dinv, out, diag):
    total = terms[0]
    for i in range(1, 8):
        total = total + terms[i]
    value = dinv[...] - total
    diag[...] = value
    half = value.astype(BF)
    for j in range(16):
        out[j, 0:64, :] = spread[parent[2 * j]]
        out[j, 64:128, :] = spread[parent[2 * j + 1]]
        out[j, 128:160, :] = half


def level_zero_body(tab, got, part, factor, link, up_ref, sums, both):
    both[...] = jnp.zeros_like(both)
    for e in range(2):
        cols = pl.ds(e * B, B)
        for rb in range(4):
            rows = pl.ds(rb * B, B)
            present = tab[ROW_AT + 4 * (e + 1) + rb] > 0

            @pl.when(jnp.logical_not(present))
            def _():
                up_ref[rows, cols] = jnp.zeros((B, B), BF)

            @pl.when(present)
            def _():
                above = got[4 * rb : 4 * rb + 4, e * 64 : e * 64 + 64, :].reshape(B, B)
                low = factor[rows, cols]
                total = part[rows, cols] + dot(above, link[:, cols])
                up = (-total).astype(BF)
                up_ref[rows, cols] = up
                both[0, :, cols] += dot_t(above, low)
                both[1, :, cols] += dot_t(low, up)

    for i in range(8):
        sums[i, 0:32, :] = both[0, i * 32 : i * 32 + 32, :]
        sums[i, 32:64, :] = both[1, i * 32 : i * 32 + 32, :]


def parent_body(tab, sums, got, link, out):
    total = sums[0]
    for i in range(1, 8):
        total = total + sums[i]
    ups = []
    for e in range(2):
        cols = slice(e * B, e * B + B)
        half = got[tab[PAR_AT + e], 128:160, :]
        ups.append((-(total[0:32, cols] + dot(half, link[:, cols]))).astype(BF))
    up = jnp.concatenate(ups, axis=1)
    high = total[32:64].astype(BF)
    rest = (total[32:64] - high.astype(F32)).astype(BF)
    for i in range(8):
        out[i, 0:32, :] = up
        out[i, 32:64, :] = high
        out[i, 64:96, :] = rest


def last_body(got, dinv, link, up_ref, diag_ref):
    for i in range(8):
        rows = pl.ds(i * 32, 32)
        up_ref[rows, :] = got[i, 0:32, :]
        diag_ref[rows, :] = dinv[rows, :] - (
            got[i, 32:64, :].astype(F32) + got[i, 64:96, :].astype(F32)
        )
    for e in range(2):
        cols = pl.ds(e * B, B)
        diag_ref[:, cols] -= dot_t(link[:, cols], up_ref[:, cols])


def position_of(blocks, offset):
    places = jnp.where(
        blocks[:, None] == jnp.arange(32, dtype=jnp.int32)[None, :],
        jnp.arange(blocks.shape[0], dtype=jnp.int32)[:, None] + offset,
        -1,
    )
    return jnp.max(places, axis=0)


def tables(struct_one, select_zero, parent, row, col):
    own = lax.dynamic_slice_in_dim(struct_one, col, 1, 0)[0]
    parents = lax.dynamic_slice_in_dim(parent, 2 * col, 2, 0)
    picks = lax.dynamic_slice_in_dim(select_zero, 2 * col, 2, 0)
    kids = jnp.take_along_axis(jnp.take(struct_one, parents, axis=0), picks, axis=1)
    z, xh, core = col // 4, (col // 2) % 2, col % 2
    y, xl = row // 2, row % 2
    columns = []
    for dcore in range(2):
        for dz, dxh in PIECES:
            columns.append(((z + dz) % 4) * 4 + (xh ^ dxh) * 2 + (core ^ dcore))
    order = jnp.stack([2 * c + h for c in columns for h in range(2)])
    slots, rows = [], []
    for e, blocks in enumerate((own, kids[0], kids[1])):
        at = position_of(blocks, (0, 16, 24)[e])
        slots.append(jnp.take(at, order))
        rows.append(lax.dynamic_slice_in_dim(at, 4 * row, 4, 0) >= 0)
    slices = jnp.stack([((y + dy) % 4) * 2 + (xl ^ dxl) for dy, dxl in SLICES])
    tab = jnp.concatenate(
        slots + [slices] + [r.astype(jnp.int32) for r in rows] + [parents]
    ).astype(jnp.int32)
    chosen = jnp.concatenate([(b // 4) * 12 + e * 4 + b % 4 for e, b in enumerate((own, kids[0], kids[1]))])
    return tab, chosen


def shards(
    inverse_anc,
    factor_one,
    factor_zero,
    factor_parent,
    dinv_one,
    dinv_zero,
    struct_one,
    select_zero,
    parent,
):
    row = lax.axis_index("prow")
    col = lax.axis_index("pcol")
    tab, chosen = tables(struct_one, select_zero, parent, row, col)
    link = lax.dynamic_slice_in_dim(factor_parent, col * 2 * B, 2 * B, 1)
    dinv_rows = lax.dynamic_slice_in_dim(dinv_one, row * 32, 32, 0)

    pieces = ring_gather(inverse_anc, X_HI, Z_UP, Z_DOWN)
    pieces = pieces + [tuple(send(a, SIBLING) for a in p) for p in pieces]

    spread_low = jnp.concatenate(
        [
            factor_one.reshape(4, 8, 1, 32, B).transpose(1, 2, 0, 3, 4),
            factor_zero.reshape(4, 8, 32, 2, B).transpose(1, 3, 0, 2, 4),
        ],
        axis=1,
    )
    spread_low = lax.all_to_all(spread_low, "prow", 0, 0)
    mine = jnp.take(spread_low.reshape(96, 32, B), chosen, axis=0)
    low_pieces = ring_gather(mine, X_LO, Y_UP, Y_DOWN)

    upper_one, part, diag_part = level_one(tab, pieces, low_pieces, factor_one)

    spread = lax.all_to_all(upper_one.reshape(16, 64, B), "pcol", 0, 0)
    terms = lax.all_to_all(diag_part.reshape(8, 32, B), "prow", 0, 0)
    packed, diag_rows = call(
        pack_body,
        [jax.ShapeDtypeStruct((16, 160, B), BF), jax.ShapeDtypeStruct((32, B), F32)],
        [SMEM, VMEM, VMEM, VMEM],
    )(parent, spread, terms, dinv_rows)
    diag_one = lax.all_gather(diag_rows, "prow", axis=0, tiled=True)
    got = lax.all_to_all(packed, "pcol", 0, 0)
    upper_zero, sums = call(
        level_zero_body,
        [jax.ShapeDtypeStruct((LOC, 2 * B), BF), jax.ShapeDtypeStruct((8, 64, 2 * B), F32)],
        [SMEM, VMEM, VMEM, VMEM, VMEM],
        [pltpu.VMEM((2, B, 2 * B), F32)],
    )(tab, got, part, factor_zero, link)
    sums = lax.all_to_all(sums, "prow", 0, 0)
    rows_out = call(
        parent_body,
        jax.ShapeDtypeStruct((8, 96, 2 * B), BF),
        [SMEM, VMEM, VMEM, VMEM],
    )(tab, sums, got, link)
    rows_in = lax.all_to_all(rows_out, "prow", 0, 0)
    upper_parent, diag_zero = call(
        last_body,
        [jax.ShapeDtypeStruct((B, 2 * B), BF), jax.ShapeDtypeStruct((B, 2 * B), F32)],
        [VMEM, VMEM, VMEM],
    )(rows_in, dinv_zero, link)
    return upper_one, diag_one, upper_zero, upper_parent, diag_zero


def solution(mesh):
    in_specs = (
        P("prow", "pcol"),
        P("prow", "pcol"),
        P("prow", "pcol"),
        P(),
        P(None, "pcol"),
        P(None, "pcol"),
        P(),
        P(),
        P(),
    )
    out_specs = (
        P("prow", "pcol"),
        P(None, "pcol"),
        P("prow", "pcol"),
        P(None, "pcol"),
        P(None, "pcol"),
    )
    return jax.shard_map(shards, mesh=mesh, in_specs=in_specs, out_specs=out_specs, check_vma=False)
```

time: 642 us -> 261 us (0.41)
  waiting for transfers between devices: 555 us -> 89.4 us
  blocking collectives: 0 us -> 65.9 us
  starting transfers between devices: 0.42 us -> 48.7 us
  matrix products: 32.9 us -> 0 us
  Pallas kernels: 0 us -> 23.2 us
  between operations: 14.4 us -> 0.99 us
    all_gather x5 -> x0, waiting for transfers between devices: 471 us -> none  [the longest x1 148 us: shards(): lax.all_gather(low_zero, 'prow', axis=0, tiled=True)]
    psum x1 -> x0, waiting for transfers between devices: 83.5 us -> none  [shards(): lax.psum(block_products(low_one, upper_one, own_sups, blk_width), 'prow')]
    ppermute x0 -> x28, waiting for transfers between devices: none -> 51.7 us  [send(): return lax.ppermute(block, MESH_AXES, pairs)]
    all_to_all x0 -> x4, waiting for transfers between devices: none -> 37.7 us  [the longest x1 19.9 us: shards(): got = lax.all_to_all(packed, 'pcol', 0, 0)]
    all_gather x0 -> x1, blocking collectives: none -> 35.1 us  [shards(): diag_one = lax.all_gather(diag_rows, 'prow', axis=0, tiled=True)]
    dot_general x8 -> x0, matrix products: 32.9 us -> none  [the longest x1 15.2 us: shards(): jnp.dot(inv_rows, full_zero, preferred_element_type=jnp.float32) + second]
    ppermute x0 -> x28, starting transfers between devices: none -> 31.5 us  [send(): return lax.ppermute(block, MESH_AXES, pairs)]
    all_to_all x0 -> x2, blocking collectives: none -> 30.8 us  [the longest x1 18.6 us: shards(): sums = lax.all_to_all(sums, 'prow', 0, 0)]
  transfers between devices with their start and end apart: 6 -> 32, of which waited for: 6 -> 12; matrix products, arithmetic and copies ran while one was open for 5% -> 9% of each run, Pallas kernels for 0% -> 0%
where the time goes in v1:
time: 261 us; the launch traced here: 260 us
  waiting for transfers between devices  89.4 us (34%)
  blocking collectives  65.9 us (25%)
  starting transfers between devices  48.7 us (19%)
  local copies, waits for them, and re-layouts  28.7 us (11%)
  Pallas kernels  23.2 us (9%)
  other arithmetic  3.17 us (1%)
    ppermute x28, waiting for transfers between devices, send(): return lax.ppermute(block, MESH_AXES, pairs)  51.7 us
    all_gather x1, blocking collectives, shards(): diag_one = lax.all_gather(diag_rows, 'prow', axis=0, tiled=True)  35.1 us
    ppermute x28, starting transfers between devices, send(): return lax.ppermute(block, MESH_AXES, pairs)  31.5 us
    all_to_all x1, waiting for transfers between devices, shards(): got = lax.all_to_all(packed, 'pcol', 0, 0)  19.9 us
    all_to_all x1, blocking collectives, shards(): sums = lax.all_to_all(sums, 'prow', 0, 0)  18.6 us
    pallas_call x1, Pallas kernels, level_one(): call(body, [jax.ShapeDtypeStruct((LOC, B), BF), jax.ShapeDtypeStruct((LOC...  18.3 us
    all_to_all x1, waiting for transfers between devices, shards(): spread = lax.all_to_all(upper_one.reshape(16, 64, B), 'pcol', 0, 0)  12.3 us
    all_to_all x1, blocking collectives, shards(): terms = lax.all_to_all(diag_part.reshape(8, 32, B), 'prow', 0, 0)  12.2 us
  transfers between devices with their start and end apart: 32, of which 12 were waited for; matrix products, arithmetic and copies ran while one was open for 9% of the time, Pallas kernels for 0%

profile of v1, /device:TPU:0, one launch (start us, length us, event | category | flops | bytes accessed | tf_op | source)
XLA Modules:
  0.0 260.0 jit_solution(737912257846535702)
XLA Ops:
  0.7 3.2 %collective-permute-start = (bf16[1024,512]{1,0:T(8,128)(2,1)}, bf16[1024,512]{1,0:T(8,128)(2,1)}, u32[]{:S(2)}, u32[]{:S(2)}) collective-permute-start(bf16[1024,512]{1,0:T(8,128)(2,1)} %refs_0_.1), channel_id=1, source_target_pairs={{0,2},{1,3},{2,0},{3,1},{4,6},{5,7},{6,4},{7,5},{8,10},{9,11},{10,... | collective-permute-start | bytes 3145736 | tf_op jit(solution)/shard_map/ppermute | solution.py:41
  3.8 1.9 collective-permute-start.1
  5.8 2.1 collective-permute-start.2
  7.9 1.3 reshape.174
  9.2 1.0 copy.24
  10.3 2.2 pad_maximum_fusion
  12.5 1.5 copy.25
  14.0 4.6 %all-to-all-start = ((bf16[8,3,4,32,256]{4,3,2,1,0:T(8,128)(2,1)}), bf16[8,3,4,32,256]{4,3,2,1,0:T(8,128)(2,1)S(1)}, u32[]{:S(2)}, u32[]{:S(2)}) async-start(bf16[8,3,4,32,256]{4,3,2,1,0:T(8,128)(2,1)} %copy.25), calls=%async_computation | async-start | bytes 3145728 | tf_op jit(solution)/shard_map/all_to_all | solution.py:319
  18.9 0.6 gather_fusion
  19.7 0.7 gather_fusion.2
  20.6 10.5 %collective-permute-done.1.refs_2_ = bf16[1024,512]{1,0:T(8,128)(2,1)} collective-permute-done((bf16[1024,512]{1,0:T(8,128)(2,1)}, bf16[1024,512]{1,0:T(8,128)(2,1)}, u32[]{:S(2)}, u32[]{:S(2)}) %collective-permute-start.1) | collective-permute-done | bytes 1048608 | tf_op jit(solution)/shard_map/ppermute | solution.py:41
  31.1 1.9 slice.54
  33.0 1.9 slice.55
  34.9 3.2 %collective-permute-start.6 = (bf16[512,512]{1,0:T(8,128)(2,1)}, bf16[512,512]{1,0:T(8,128)(2,1)S(1)}, u32[]{:S(2)}, u32[]{:S(2)}) collective-permute-start(bf16[512,512]{1,0:T(8,128)(2,1)} %slice.55), channel_id=1, source_target_pairs={{0,12},{1,13},{2,14},{3,15},{4,0},{5,1},{6,2},{7,3},{8,4},{9,5},{1... | collective-permute-start | bytes 1572872 | tf_op jit(solution)/shard_map/ppermute | solution.py:41
  38.1 3.2 %collective-permute-start.4 = (bf16[1024,512]{1,0:T(8,128)(2,1)}, bf16[1024,512]{1,0:T(8,128)(2,1)}, u32[]{:S(2)}, u32[]{:S(2)}) collective-permute-start(bf16[1024,512]{1,0:T(8,128)(2,1)} %collective-permute-done.refs_1_), channel_id=1, source_target_pairs={{0,12},{1,13},{2,14},{3,15},{4,0},{5,1},{6,2},{7,3},{8,4},{9,5},{1... | collective-permute-start | bytes 3145736 | tf_op jit(solution)/shard_map/ppermute | solution.py:41
  41.3 5.5 %all-to-all-done = bf16[8,3,4,32,256]{4,3,2,1,0:T(8,128)(2,1)S(1)} async-done(((bf16[8,3,4,32,256]{4,3,2,1,0:T(8,128)(2,1)}), bf16[8,3,4,32,256]{4,3,2,1,0:T(8,128)(2,1)S(1)}, u32[]{:S(2)}, u32[]{:S(2)}) %all-to-all-start) | async-done | bytes 1572896 | tf_op jit(solution)/shard_map/all_to_all | solution.py:319
  46.8 0.6 gather_fusion.1
  47.6 1.6 collective-permute-done.5.refs_6_
  49.3 1.6 collective-permute-start.20
  50.8 3.0 %collective-permute-start.21 = (bf16[32,32,256]{2,1,0:T(8,128)(2,1)S(1)}, bf16[32,32,256]{2,1,0:T(8,128)(2,1)S(1)}, u32[]{:S(2)}, u32[]{:S(2)}) collective-permute-start(bf16[32,32,256]{2,1,0:T(8,128)(2,1)S(1)} %broadcast_select_fusion.refs_20_), channel_id=1, source_target_pairs={{0,96},{1,97},{2,98},{3,99},{4,100},{5,101},{6,102},{7,103},{8,104... | collective-permute-start | bytes 1572872 | tf_op jit(solution)/shard_map/ppermute | solution.py:41
  53.8 6.7 %collective-permute-done.19.refs_21_ = bf16[32,32,256]{2,1,0:T(8,128)(2,1)} collective-permute-done((bf16[32,32,256]{2,1,0:T(8,128)(2,1)S(1)}, bf16[32,32,256]{2,1,0:T(8,128)(2,1)}, u32[]{:S(2)}, u32[]{:S(2)}) %collective-permute-start.19) | collective-permute-done | bytes 524320 | tf_op jit(solution)/shard_map/ppermute | solution.py:41
  60.5 1.2 collective-permute-done.20.refs_22_
  62.2 7.5 %collective-permute-done.3.refs_4_ = bf16[1024,512]{1,0:T(8,128)(2,1)} collective-permute-done((bf16[1024,512]{1,0:T(8,128)(2,1)}, bf16[1024,512]{1,0:T(8,128)(2,1)}, u32[]{:S(2)}, u32[]{:S(2)}) %collective-permute-start.3) | collective-permute-done | bytes 1048608 | tf_op jit(solution)/shard_map/ppermute | solution.py:41
  69.8 1.1 collective-permute-done.4.refs_5_
  70.9 1.6 collective-permute-start.22
  72.6 1.0 slice.59
  73.6 1.6 collective-permute-start.24
  75.3 1.7 collective-permute-start.25
  76.9 1.4 collective-permute-start.23
  78.3 1.9 slice.56
  80.2 1.9 slice.57
  82.1 10.2 %collective-permute-done.24.refs_26_ = bf16[16,32,256]{2,1,0:T(8,128)(2,1)S(1)} collective-permute-done((bf16[16,32,256]{2,1,0:T(8,128)(2,1)S(1)}, bf16[16,32,256]{2,1,0:T(8,128)(2,1)S(1)}, u32[]{:S(2)}, u32[]{:S(2)}) %collective-permute-start.24) | collective-permute-done | bytes 262176 | tf_op jit(solution)/shard_map/ppermute | solution.py:41
  92.3 0.7 copy-done.6
  93.0 3.7 %collective-permute-start.8 = (bf16[512,512]{1,0:T(8,128)(2,1)}, bf16[512,512]{1,0:T(8,128)(2,1)}, u32[]{:S(2)}, u32[]{:S(2)}) collective-permute-start(bf16[512,512]{1,0:T(8,128)(2,1)} %slice.57), channel_id=1, source_target_pairs={{0,12},{1,13},{2,14},{3,15},{4,0},{5,1},{6,2},{7,3},{8,4},{9,5},{1... | collective-permute-start | bytes 1572872 | tf_op jit(solution)/shard_map/ppermute | solution.py:41
  96.7 0.7 copy-done.8
  97.5 0.5 collective-permute-start.14
  98.2 1.7 slice.60
  100.3 0.7 gather_fusion.5
  101.1 7.1 %collective-permute-done.8.refs_9_ = bf16[512,512]{1,0:T(8,128)(2,1)} collective-permute-done((bf16[512,512]{1,0:T(8,128)(2,1)}, bf16[512,512]{1,0:T(8,128)(2,1)}, u32[]{:S(2)}, u32[]{:S(2)}) %collective-permute-start.8) | collective-permute-done | bytes 524320 | tf_op jit(solution)/shard_map/ppermute | solution.py:41
  108.2 1.7 slice.61
  109.9 1.8 collective-permute-start.27
  111.8 0.7 gather_fusion.3
  112.5 0.7 gather_fusion.4
  113.3 5.6 %collective-permute-done.27.refs_29_ = bf16[16,32,256]{2,1,0:T(8,128)(2,1)} collective-permute-done((bf16[16,32,256]{2,1,0:T(8,128)(2,1)}, bf16[16,32,256]{2,1,0:T(8,128)(2,1)}, u32[]{:S(2)}, u32[]{:S(2)}) %collective-permute-start.27) | collective-permute-done | bytes 262176 | tf_op jit(solution)/shard_map/ppermute | solution.py:41
  119.0 0.9 copy-done.7
  119.9 0.9 copy-done.9
  120.8 18.3 %shard_map.128 = (bf16[1024,256]{1,0:T(8,128)(2,1)}, f32[1024,512]{1,0:T(8,128)}, f32[256,256]{1,0:T(8,128)S(1)}) custom-call(s32[118]{0:T(128)S(1)} %concatenate.38.tab_ref.tab, bf16[1024,512]{1,0:T(8,128)(2,1)} %refs_0_.1, bf16[1024,512]{1,0:T(8,128)(2,1)} %collective-permute-done.refs_1_, bf16[1024,512]{1,0:T(8,128)(2,1)} %collective-permute-done.1.refs_2_, ...), custom_call_target="tpu_custom_call" | custom-call | tf_op jit(solution)/shard_map/pallas_call | solution.py:169
  139.1 12.2 %all_to_all.30.terms = f32[8,32,256]{2,1,0:T(8,128)S(1)} all-to-all(f32[8,32,256]{2,1,0:T(8,128)S(1)} %bitcast.67), channel_id=1, replica_groups=mesh['prow'=8,'pcol'=16] {'prow'}, dimensions={0} | all-to-all | bytes 524288 | tf_op jit(solution)/shard_map/all_to_all | solution.py:326
  151.3 5.1 %all-to-all-start.1 = ((bf16[16,64,256]{2,1,0:T(8,128)(2,1)}), bf16[16,64,256]{2,1,0:T(8,128)(2,1)S(1)}, u32[]{:S(2)}, u32[]{:S(2)}) async-start(bf16[16,64,256]{2,1,0:T(8,128)(2,1)} %bitcast.71), calls=%async_computation.1 | async-start | bytes 1048576 | tf_op jit(solution)/shard_map/all_to_all | solution.py:325
  156.5 12.3 %all-to-all-done.1.spread = bf16[16,64,256]{2,1,0:T(8,128)(2,1)S(1)} async-done(((bf16[16,64,256]{2,1,0:T(8,128)(2,1)}), bf16[16,64,256]{2,1,0:T(8,128)(2,1)S(1)}, u32[]{:S(2)}, u32[]{:S(2)}) %all-to-all-start.1) | async-done | bytes 524320 | tf_op jit(solution)/shard_map/all_to_all | solution.py:325
  168.8 0.6 shard_map.129
  169.5 1.1 copy-done.4
  170.6 3.7 %all-to-all-start.3 = ((bf16[16,160,256]{2,1,0:T(8,128)(2,1)}), bf16[16,160,256]{2,1,0:T(8,128)(2,1)S(1)}, u32[]{:S(2)}, u32[]{:S(2)}) async-start(bf16[16,160,256]{2,1,0:T(8,128)(2,1)} %copy-done.4), calls=%async_computation.3 | async-start | bytes 2621440 | tf_op jit(solution)/shard_map/all_to_all | solution.py:333
  174.3 1.0 constant_dynamic-slice_fusion.link
  175.3 19.9 %all-to-all-done.3.got = bf16[16,160,256]{2,1,0:T(8,128)(2,1)S(1)} async-done(((bf16[16,160,256]{2,1,0:T(8,128)(2,1)}), bf16[16,160,256]{2,1,0:T(8,128)(2,1)S(1)}, u32[]{:S(2)}, u32[]{:S(2)}) %all-to-all-start.3) | async-done | bytes 1310752 | tf_op jit(solution)/shard_map/all_to_all | solution.py:333
  195.1 1.6 copy-done.3
  196.7 2.5 shard_map.130
  199.2 18.6 %all_to_all.31.sums = f32[8,64,512]{2,1,0:T(8,128)S(1)} all-to-all(f32[8,64,512]{2,1,0:T(8,128)S(1)} %get-tuple-element.21), channel_id=1, replica_groups=mesh['prow'=8,'pcol'=16] {'prow'}, dimensions={0} | all-to-all | bytes 2097152 | tf_op jit(solution)/shard_map/all_to_all | solution.py:340
  217.7 0.7 shard_map.131
  218.5 0.9 copy-done.2
  219.3 3.7 %all-to-all-start.5 = ((bf16[8,96,512]{2,1,0:T(8,128)(2,1)}), bf16[8,96,512]{2,1,0:T(8,128)(2,1)S(1)}, u32[]{:S(2)}, u32[]{:S(2)}) async-start(bf16[8,96,512]{2,1,0:T(8,128)(2,1)} %copy-done.2), calls=%async_computation.5 | async-start | bytes 1572864 | tf_op jit(solution)/shard_map/all_to_all | solution.py:346
  223.0 35.1 %all_gather.3 = f32[256,256]{1,0:T(8,128)S(1)} all-gather(f32[32,256]{1,0:T(8,128)S(1)} %get-tuple-element.17), channel_id=1, replica_groups=mesh['prow'=8,'pcol'=16] {'prow'}, dimensions={0}, use_global_device_ids=true | all-gather | bytes 294912 | tf_op jit(solution)/shard_map/all_gather | solution.py:332
  258.2 1.1 shard_map.132
  259.3 0.7 copy.28
  (91 shorter events, 2.7 us)
Async XLA Ops:
  0.6 155.9 %copy-start = (f32[256,256]{1,0:T(8,128)S(1)}, f32[256,256]{1,0:T(8,128)}, u32[]{:S(2)}) copy-start(f32[256,256]{1,0:T(8,128)} %param.15) | copy-start | bytes 786436
  0.6 8.6 %copy-start.11 = (bf16[1024,256]{1,0:T(8,128)(2,1)S(1)}, bf16[1024,256]{1,0:T(8,128)(2,1)}, u32[]{:S(2)}) copy-start(bf16[1024,256]{1,0:T(8,128)(2,1)} %refs_30_.1) | copy-start | bytes 1572868
  0.7 37.4 %collective-permute-start = (bf16[1024,512]{1,0:T(8,128)(2,1)}, bf16[1024,512]{1,0:T(8,128)(2,1)}, u32[]{:S(2)}, u32[]{:S(2)}) collective-permute-start(bf16[1024,512]{1,0:T(8,128)(2,1)} %refs_0_.1), channel_id=1, source_target_pairs={{0,2},{1,3},{2,0},{3,1},{4,6},{5,7},{6,4},{7,5},{8,10},{9,11},{10,... | collective-permute-start | bytes 3145736 | tf_op jit(solution)/shard_map/ppermute | solution.py:41
  3.8 27.3 %collective-permute-start.1 = (bf16[1024,512]{1,0:T(8,128)(2,1)}, bf16[1024,512]{1,0:T(8,128)(2,1)}, u32[]{:S(2)}, u32[]{:S(2)}) collective-permute-start(bf16[1024,512]{1,0:T(8,128)(2,1)} %refs_0_.1), channel_id=1, source_target_pairs={{0,4},{1,5},{2,6},{3,7},{4,8},{5,9},{6,10},{7,11},{8,12},{9,13},{1... | collective-permute-start | bytes 3145736 | tf_op jit(solution)/shard_map/ppermute | solution.py:41
  5.8 27.2 %collective-permute-start.2 = (bf16[1024,512]{1,0:T(8,128)(2,1)}, bf16[1024,512]{1,0:T(8,128)(2,1)}, u32[]{:S(2)}, u32[]{:S(2)}) collective-permute-start(bf16[1024,512]{1,0:T(8,128)(2,1)} %refs_0_.1), channel_id=1, source_target_pairs={{0,12},{1,13},{2,14},{3,15},{4,0},{5,1},{6,2},{7,3},{8,4},{9,5},{1... | collective-permute-start | bytes 3145736 | tf_op jit(solution)/shard_map/ppermute | solution.py:41
  7.9 39.7 %collective-permute-start.9 = (bf16[1024,512]{1,0:T(8,128)(2,1)}, bf16[1024,512]{1,0:T(8,128)(2,1)}, u32[]{:S(2)}, u32[]{:S(2)}) collective-permute-start(bf16[1024,512]{1,0:T(8,128)(2,1)} %refs_0_.1), channel_id=1, source_target_pairs={{0,1},{1,0},{2,3},{3,2},{4,5},{5,4},{6,7},{7,6},{8,9},{9,8},{10,11... | collective-permute-start | bytes 3145736 | tf_op jit(solution)/shard_map/ppermute | solution.py:41
  14.0 4.6 %copy-start.10 = (s32[32]{0:T(128)S(1)}, s32[32]{0:T(128)}, u32[]{:S(2)}) copy-start(s32[32]{0:T(128)} %parent.1) | copy-start | bytes 388
  14.0 4.7 %copy-start.15 = (s32[32,8]{0,1:T(8,128)S(1)}, s32[32,8]{0,1:T(8,128)}, u32[]{:S(2)}) copy-start(s32[32,8]{0,1:T(8,128)} %param.18) | copy-start | bytes 3076
  14.0 4.9 %copy-start.14 = (s32[16,16]{1,0:T(8,128)S(1)}, s32[16,16]{1,0:T(8,128)}, u32[]{:S(2)}) copy-start(s32[16,16]{1,0:T(8,128)} %param.17) | copy-start | bytes 3076
  14.0 32.8 %all-to-all-start = ((bf16[8,3,4,32,256]{4,3,2,1,0:T(8,128)(2,1)}), bf16[8,3,4,32,256]{4,3,2,1,0:T(8,128)(2,1)S(1)}, u32[]{:S(2)}, u32[]{:S(2)}) async-start(bf16[8,3,4,32,256]{4,3,2,1,0:T(8,128)(2,1)} %copy.25), calls=%async_computation | async-start | bytes 3145728 | tf_op jit(solution)/shard_map/all_to_all | solution.py:319
  33.0 16.3 %collective-permute-start.5 = (bf16[512,512]{1,0:T(8,128)(2,1)}, bf16[512,512]{1,0:T(8,128)(2,1)S(1)}, u32[]{:S(2)}, u32[]{:S(2)}) collective-permute-start(bf16[512,512]{1,0:T(8,128)(2,1)} %slice.54), channel_id=1, source_target_pairs={{0,4},{1,5},{2,6},{3,7},{4,8},{5,9},{6,10},{7,11},{8,12},{9,13},{1... | collective-permute-start | bytes 1572872 | tf_op jit(solution)/shard_map/ppermute | solution.py:41
  34.9 16.0 %collective-permute-start.6 = (bf16[512,512]{1,0:T(8,128)(2,1)}, bf16[512,512]{1,0:T(8,128)(2,1)S(1)}, u32[]{:S(2)}, u32[]{:S(2)}) collective-permute-start(bf16[512,512]{1,0:T(8,128)(2,1)} %slice.55), channel_id=1, source_target_pairs={{0,12},{1,13},{2,14},{3,15},{4,0},{5,1},{6,2},{7,3},{8,4},{9,5},{1... | collective-permute-start | bytes 1572872 | tf_op jit(solution)/shard_map/ppermute | solution.py:41
  38.1 31.7 %collective-permute-start.3 = (bf16[1024,512]{1,0:T(8,128)(2,1)}, bf16[1024,512]{1,0:T(8,128)(2,1)}, u32[]{:S(2)}, u32[]{:S(2)}) collective-permute-start(bf16[1024,512]{1,0:T(8,128)(2,1)} %collective-permute-done.refs_1_), channel_id=1, source_target_pairs={{0,4},{1,5},{2,6},{3,7},{4,8},{5,9},{6,10},{7,11},{8,12},{9,13},{1... | collective-permute-start | bytes 3145736 | tf_op jit(solution)/shard_map/ppermute | solution.py:41
  38.1 32.8 %collective-permute-start.4 = (bf16[1024,512]{1,0:T(8,128)(2,1)}, bf16[1024,512]{1,0:T(8,128)(2,1)}, u32[]{:S(2)}, u32[]{:S(2)}) collective-permute-start(bf16[1024,512]{1,0:T(8,128)(2,1)} %collective-permute-done.refs_1_), channel_id=1, source_target_pairs={{0,12},{1,13},{2,14},{3,15},{4,0},{5,1},{6,2},{7,3},{8,4},{9,5},{1... | collective-permute-start | bytes 3145736 | tf_op jit(solution)/shard_map/ppermute | solution.py:41
  47.5 13.0 %collective-permute-start.19 = (bf16[32,32,256]{2,1,0:T(8,128)(2,1)S(1)}, bf16[32,32,256]{2,1,0:T(8,128)(2,1)}, u32[]{:S(2)}, u32[]{:S(2)}) collective-permute-start(bf16[32,32,256]{2,1,0:T(8,128)(2,1)S(1)} %broadcast_select_fusion.refs_20_), channel_id=1, source_target_pairs={{0,16},{1,17},{2,18},{3,19},{4,20},{5,21},{6,22},{7,23},{8,24},{9,... | collective-permute-start | bytes 1572872 | tf_op jit(solution)/shard_map/ppermute | solution.py:41
  49.3 12.5 %collective-permute-start.20 = (bf16[32,32,256]{2,1,0:T(8,128)(2,1)S(1)}, bf16[32,32,256]{2,1,0:T(8,128)(2,1)S(1)}, u32[]{:S(2)}, u32[]{:S(2)}) collective-permute-start(bf16[32,32,256]{2,1,0:T(8,128)(2,1)S(1)} %broadcast_select_fusion.refs_20_), channel_id=1, source_target_pairs={{0,32},{1,33},{2,34},{3,35},{4,36},{5,37},{6,38},{7,39},{8,40},{9,... | collective-permute-start | bytes 1572872 | tf_op jit(solution)/shard_map/ppermute | solution.py:41
  50.8 10.9 %collective-permute-start.21 = (bf16[32,32,256]{2,1,0:T(8,128)(2,1)S(1)}, bf16[32,32,256]{2,1,0:T(8,128)(2,1)S(1)}, u32[]{:S(2)}, u32[]{:S(2)}) collective-permute-start(bf16[32,32,256]{2,1,0:T(8,128)(2,1)S(1)} %broadcast_select_fusion.refs_20_), channel_id=1, source_target_pairs={{0,96},{1,97},{2,98},{3,99},{4,100},{5,101},{6,102},{7,103},{8,104... | collective-permute-start | bytes 1572872 | tf_op jit(solution)/shard_map/ppermute | solution.py:41
  60.5 14.7 %collective-permute-start.10 = (bf16[1024,512]{1,0:T(8,128)(2,1)}, bf16[1024,512]{1,0:T(8,128)(2,1)}, u32[]{:S(2)}, u32[]{:S(2)}) collective-permute-start(bf16[1024,512]{1,0:T(8,128)(2,1)} %collective-permute-done.refs_1_), channel_id=1, source_target_pairs={{0,1},{1,0},{2,3},{3,2},{4,5},{5,4},{6,7},{7,6},{8,9},{9,8},{10,11... | collective-permute-start | bytes 3145736 | tf_op jit(solution)/shard_map/ppermute | solution.py:41
  61.7 20.3 %copy-start.12 = (bf16[32,32,256]{2,1,0:T(8,128)(2,1)}, bf16[32,32,256]{2,1,0:T(8,128)(2,1)S(1)}, u32[]{:S(2)}) copy-start(bf16[32,32,256]{2,1,0:T(8,128)(2,1)S(1)} %collective-permute-done.20.refs_22_) | copy-start | bytes 1572868
  61.7 9.2 %collective-permute-start.15 = (bf16[512,512]{1,0:T(8,128)(2,1)S(1)}, bf16[512,512]{1,0:T(8,128)(2,1)S(1)}, u32[]{:S(2)}, u32[]{:S(2)}) collective-permute-start(bf16[512,512]{1,0:T(8,128)(2,1)S(1)} %collective-permute-done.5.refs_6_), channel_id=1, source_target_pairs={{0,1},{1,0},{2,3},{3,2},{4,5},{5,4},{6,7},{7,6},{8,9},{9,8},{10,11... | collective-permute-start | bytes 1572872 | tf_op jit(solution)/shard_map/ppermute | solution.py:41
  61.7 8.0 %copy-start.13 = (bf16[32,32,256]{2,1,0:T(8,128)(2,1)}, bf16[32,32,256]{2,1,0:T(8,128)(2,1)S(1)}, u32[]{:S(2)}) copy-start(bf16[32,32,256]{2,1,0:T(8,128)(2,1)S(1)} %collective-permute-done.21.refs_23_) | copy-start | bytes 1572868
  61.7 15.2 %collective-permute-start.11 = (bf16[1024,512]{1,0:T(8,128)(2,1)}, bf16[1024,512]{1,0:T(8,128)(2,1)}, u32[]{:S(2)}, u32[]{:S(2)}) collective-permute-start(bf16[1024,512]{1,0:T(8,128)(2,1)} %collective-permute-done.1.refs_2_), channel_id=1, source_target_pairs={{0,1},{1,0},{2,3},{3,2},{4,5},{5,4},{6,7},{7,6},{8,9},{9,8},{10,11... | collective-permute-start | bytes 3145736 | tf_op jit(solution)/shard_map/ppermute | solution.py:41
  69.8 12.3 %collective-permute-start.12 = (bf16[1024,512]{1,0:T(8,128)(2,1)}, bf16[1024,512]{1,0:T(8,128)(2,1)}, u32[]{:S(2)}, u32[]{:S(2)}) collective-permute-start(bf16[1024,512]{1,0:T(8,128)(2,1)} %collective-permute-done.2.refs_3_), channel_id=1, source_target_pairs={{0,1},{1,0},{2,3},{3,2},{4,5},{5,4},{6,7},{7,6},{8,9},{9,8},{10,11... | collective-permute-start | bytes 3145736 | tf_op jit(solution)/shard_map/ppermute | solution.py:41
  70.9 2.7 %collective-permute-start.16 = (bf16[512,512]{1,0:T(8,128)(2,1)S(1)}, bf16[512,512]{1,0:T(8,128)(2,1)S(1)}, u32[]{:S(2)}, u32[]{:S(2)}) collective-permute-start(bf16[512,512]{1,0:T(8,128)(2,1)S(1)} %collective-permute-done.6.refs_7_), channel_id=1, source_target_pairs={{0,1},{1,0},{2,3},{3,2},{4,5},{5,4},{6,7},{7,6},{8,9},{9,8},{10,11... | collective-permute-start | bytes 1572872 | tf_op jit(solution)/shard_map/ppermute | solution.py:41
  70.9 26.5 %collective-permute-start.22 = (bf16[32,32,256]{2,1,0:T(8,128)(2,1)}, bf16[32,32,256]{2,1,0:T(8,128)(2,1)}, u32[]{:S(2)}, u32[]{:S(2)}) collective-permute-start(bf16[32,32,256]{2,1,0:T(8,128)(2,1)} %collective-permute-done.19.refs_21_), channel_id=1, source_target_pairs={{0,32},{1,33},{2,34},{3,35},{4,36},{5,37},{6,38},{7,39},{8,40},{9,... | collective-permute-start | bytes 1572872 | tf_op jit(solution)/shard_map/ppermute | solution.py:41
  73.6 18.7 %collective-permute-start.24 = (bf16[16,32,256]{2,1,0:T(8,128)(2,1)S(1)}, bf16[16,32,256]{2,1,0:T(8,128)(2,1)S(1)}, u32[]{:S(2)}, u32[]{:S(2)}) collective-permute-start(bf16[16,32,256]{2,1,0:T(8,128)(2,1)S(1)} %slice.58), channel_id=1, source_target_pairs={{0,32},{1,33},{2,34},{3,35},{4,36},{5,37},{6,38},{7,39},{8,40},{9,... | collective-permute-start | bytes 786440 | tf_op jit(solution)/shard_map/ppermute | solution.py:41
  75.3 21.5 %collective-permute-start.25 = (bf16[16,32,256]{2,1,0:T(8,128)(2,1)S(1)}, bf16[16,32,256]{2,1,0:T(8,128)(2,1)S(1)}, u32[]{:S(2)}, u32[]{:S(2)}) collective-permute-start(bf16[16,32,256]{2,1,0:T(8,128)(2,1)S(1)} %slice.59), channel_id=1, source_target_pairs={{0,96},{1,97},{2,98},{3,99},{4,100},{5,101},{6,102},{7,103},{8,104... | collective-permute-start | bytes 786440 | tf_op jit(solution)/shard_map/ppermute | solution.py:41
  76.9 23.0 %collective-permute-start.23 = (bf16[32,32,256]{2,1,0:T(8,128)(2,1)}, bf16[32,32,256]{2,1,0:T(8,128)(2,1)}, u32[]{:S(2)}, u32[]{:S(2)}) collective-permute-start(bf16[32,32,256]{2,1,0:T(8,128)(2,1)} %collective-permute-done.19.refs_21_), channel_id=1, source_target_pairs={{0,96},{1,97},{2,98},{3,99},{4,100},{5,101},{6,102},{7,103},{8,104... | collective-permute-start | bytes 1572872 | tf_op jit(solution)/shard_map/ppermute | solution.py:41
  82.1 18.9 %collective-permute-start.7 = (bf16[512,512]{1,0:T(8,128)(2,1)}, bf16[512,512]{1,0:T(8,128)(2,1)S(1)}, u32[]{:S(2)}, u32[]{:S(2)}) collective-permute-start(bf16[512,512]{1,0:T(8,128)(2,1)} %slice.56), channel_id=1, source_target_pairs={{0,4},{1,5},{2,6},{3,7},{4,8},{5,9},{6,10},{7,11},{8,12},{9,13},{1... | collective-permute-start | bytes 1572872 | tf_op jit(solution)/shard_map/ppermute | solution.py:41
  92.3 0.7 copy-start.6
  93.0 15.2 %collective-permute-start.8 = (bf16[512,512]{1,0:T(8,128)(2,1)}, bf16[512,512]{1,0:T(8,128)(2,1)}, u32[]{:S(2)}, u32[]{:S(2)}) collective-permute-start(bf16[512,512]{1,0:T(8,128)(2,1)} %slice.57), channel_id=1, source_target_pairs={{0,12},{1,13},{2,14},{3,15},{4,0},{5,1},{6,2},{7,3},{8,4},{9,5},{1... | collective-permute-start | bytes 1572872 | tf_op jit(solution)/shard_map/ppermute | solution.py:41
  96.7 0.7 copy-start.8
  97.4 21.5 %collective-permute-start.13 = (bf16[1024,512]{1,0:T(8,128)(2,1)}, bf16[1024,512]{1,0:T(8,128)(2,1)}, u32[]{:S(2)}, u32[]{:S(2)}) collective-permute-start(bf16[1024,512]{1,0:T(8,128)(2,1)} %collective-permute-done.3.refs_4_), channel_id=1, source_target_pairs={{0,1},{1,0},{2,3},{3,2},{4,5},{5,4},{6,7},{7,6},{8,9},{9,8},{10,11... | collective-permute-start | bytes 3145736 | tf_op jit(solution)/shard_map/ppermute | solution.py:41
  97.5 21.5 %collective-permute-start.14 = (bf16[1024,512]{1,0:T(8,128)(2,1)}, bf16[1024,512]{1,0:T(8,128)(2,1)}, u32[]{:S(2)}, u32[]{:S(2)}) collective-permute-start(bf16[1024,512]{1,0:T(8,128)(2,1)} %collective-permute-done.4.refs_5_), channel_id=1, source_target_pairs={{0,1},{1,0},{2,3},{3,2},{4,5},{5,4},{6,7},{7,6},{8,9},{9,8},{10,11... | collective-permute-start | bytes 3145736 | tf_op jit(solution)/shard_map/ppermute | solution.py:41
  99.9 10.0 %collective-permute-start.26 = (bf16[16,32,256]{2,1,0:T(8,128)(2,1)}, bf16[16,32,256]{2,1,0:T(8,128)(2,1)}, u32[]{:S(2)}, u32[]{:S(2)}) collective-permute-start(bf16[16,32,256]{2,1,0:T(8,128)(2,1)} %slice.60), channel_id=1, source_target_pairs={{0,32},{1,33},{2,34},{3,35},{4,36},{5,37},{6,38},{7,39},{8,40},{9,... | collective-permute-start | bytes 786440 | tf_op jit(solution)/shard_map/ppermute | solution.py:41
  101.0 18.0 %collective-permute-start.17 = (bf16[512,512]{1,0:T(8,128)(2,1)S(1)}, bf16[512,512]{1,0:T(8,128)(2,1)}, u32[]{:S(2)}, u32[]{:S(2)}) collective-permute-start(bf16[512,512]{1,0:T(8,128)(2,1)S(1)} %collective-permute-done.7.refs_8_), channel_id=1, source_target_pairs={{0,1},{1,0},{2,3},{3,2},{4,5},{5,4},{6,7},{7,6},{8,9},{9,8},{10,11... | collective-permute-start | bytes 1572872 | tf_op jit(solution)/shard_map/ppermute | solution.py:41
  108.2 10.7 %collective-permute-start.18 = (bf16[512,512]{1,0:T(8,128)(2,1)}, bf16[512,512]{1,0:T(8,128)(2,1)}, u32[]{:S(2)}, u32[]{:S(2)}) collective-permute-start(bf16[512,512]{1,0:T(8,128)(2,1)} %collective-permute-done.8.refs_9_), channel_id=1, source_target_pairs={{0,1},{1,0},{2,3},{3,2},{4,5},{5,4},{6,7},{7,6},{8,9},{9,8},{10,11... | collective-permute-start | bytes 1572872 | tf_op jit(solution)/shard_map/ppermute | solution.py:41
  109.9 9.0 %collective-permute-start.27 = (bf16[16,32,256]{2,1,0:T(8,128)(2,1)}, bf16[16,32,256]{2,1,0:T(8,128)(2,1)}, u32[]{:S(2)}, u32[]{:S(2)}) collective-permute-start(bf16[16,32,256]{2,1,0:T(8,128)(2,1)} %slice.61), channel_id=1, source_target_pairs={{0,96},{1,97},{2,98},{3,99},{4,100},{5,101},{6,102},{7,103},{8,104... | collective-permute-start | bytes 786440 | tf_op jit(solution)/shard_map/ppermute | solution.py:41
  118.9 1.0 copy-start.7
  119.9 0.9 copy-start.9
  151.3 17.5 %all-to-all-start.1 = ((bf16[16,64,256]{2,1,0:T(8,128)(2,1)}), bf16[16,64,256]{2,1,0:T(8,128)(2,1)S(1)}, u32[]{:S(2)}, u32[]{:S(2)}) async-start(bf16[16,64,256]{2,1,0:T(8,128)(2,1)} %bitcast.71), calls=%async_computation.1 | async-start | bytes 1048576 | tf_op jit(solution)/shard_map/all_to_all | solution.py:325
  156.5 38.6 %copy-start.1 = (bf16[1024,512]{1,0:T(8,128)(2,1)S(1)}, bf16[1024,512]{1,0:T(8,128)(2,1)}, u32[]{:S(2)}) copy-start(bf16[1024,512]{1,0:T(8,128)(2,1)} %factor.1) | copy-start | bytes 3145732
  169.5 1.1 copy-start.4
  170.6 24.5 %all-to-all-start.3 = ((bf16[16,160,256]{2,1,0:T(8,128)(2,1)}), bf16[16,160,256]{2,1,0:T(8,128)(2,1)S(1)}, u32[]{:S(2)}, u32[]{:S(2)}) async-start(bf16[16,160,256]{2,1,0:T(8,128)(2,1)} %copy-done.4), calls=%async_computation.3 | async-start | bytes 2621440 | tf_op jit(solution)/shard_map/all_to_all | solution.py:333
  195.1 1.6 copy-start.3
  218.5 0.9 copy-start.2
  219.3 38.8 %copy-start.5 = (f32[256,512]{1,0:T(8,128)S(1)}, f32[256,512]{1,0:T(8,128)}, u32[]{:S(2)}) copy-start(f32[256,512]{1,0:T(8,128)} %dinv.1) | copy-start | bytes 1572868
  219.3 38.8 %all-to-all-start.5 = ((bf16[8,96,512]{2,1,0:T(8,128)(2,1)}), bf16[8,96,512]{2,1,0:T(8,128)(2,1)S(1)}, u32[]{:S(2)}, u32[]{:S(2)}) async-start(bf16[8,96,512]{2,1,0:T(8,128)(2,1)} %copy-done.2), calls=%async_computation.5 | async-start | bytes 1572864 | tf_op jit(solution)/shard_map/all_to_all | solution.py:346

commit v2 on v1

v2 whole, which is shorter than its diff:
```python
import jax
import jax.numpy as jnp
from jax import lax
from jax.experimental import pallas as pl
from jax.experimental.pallas import tpu as pltpu
from jax.sharding import PartitionSpec as P

MESH_AXES = ("prow", "pcol")
BF = jnp.bfloat16
F32 = jnp.float32
B = 256
LOC = 1024
def moves(dy=0, dxl=0, dz=0, dxh=0, dcore=0):
    pairs = []
    for y in range(4):
        for xl in range(2):
            for z in range(4):
                for xh in range(2):
                    for core in range(2):
                        src = (y * 2 + xl) * 16 + z * 4 + xh * 2 + core
                        dst = (((y + dy) % 4) * 2 + (xl ^ dxl)) * 16
                        dst += ((z + dz) % 4) * 4 + (xh ^ dxh) * 2 + (core ^ dcore)
                        pairs.append((src, dst))
    return pairs


X_HI = moves(dxh=1)
X_LO = moves(dxl=1)
Z_UP = moves(dz=1)
Z_DOWN = moves(dz=-1)
Y_UP = moves(dy=1)
Y_DOWN = moves(dy=-1)
SIBLING = moves(dcore=1)


def send(block, pairs):
    return lax.ppermute(block, MESH_AXES, pairs)


def dot(left, right):
    return jnp.dot(left, right, preferred_element_type=F32)


def dot_t(left, right):
    return lax.dot_general(left, right, (((0,), (0,)), ((), ())), preferred_element_type=F32)


VMEM = pl.BlockSpec(memory_space=pltpu.VMEM)
SMEM = pl.BlockSpec(memory_space=pltpu.SMEM)
HBM = pl.BlockSpec(memory_space=pltpu.HBM)


def call(body, out_shape, in_specs, scratch=(), limit=32, flops=0, moved=0):
    outs = [VMEM] * len(out_shape) if isinstance(out_shape, list) else VMEM
    cost = pl.CostEstimate(flops=flops, bytes_accessed=moved, transcendentals=0)
    return pl.pallas_call(
        body,
        cost_estimate=cost if flops else None,
        out_shape=out_shape,
        in_specs=in_specs,
        out_specs=outs,
        scratch_shapes=list(scratch),
        compiler_params=pltpu.CompilerParams(vmem_limit_bytes=limit * 2**20),
    )


POS_AT = 0
SLICE_AT = 32
ROW_AT = 40
PAR_AT = 52
PICK_AT = 54
TABLE = 86


def table_body(place, struct, select, parent, tab):
    row, col = place[0], place[1]
    z, xh, core = col // 4, (col // 2) % 2, col % 2
    y, xl = row // 2, row % 2
    parents = [parent[2 * col], parent[2 * col + 1]]
    blocks = [struct[col, n] for n in range(16)]
    for e in range(2):
        tab[PAR_AT + e] = parents[e]
        blocks += [struct[parents[e], select[2 * col + e, n]] for n in range(8)]
    for n, block in enumerate(blocks):
        home = block // 2
        piece = ((home // 4) + 4 - z) % 4
        piece += 4 * (((home // 2) % 2 + xh) % 2) + 8 * ((home % 2 + core) % 2)
        tab[POS_AT + n] = 2 * piece + block % 2
        group = 0 if n < 16 else (1 if n < 24 else 2)
        tab[PICK_AT + n] = (block // 4) * 12 + group * 4 + block % 4
    for group, (low, high) in enumerate(((0, 16), (16, 24), (24, 32))):
        for rb in range(4):
            found = jnp.int32(0)
            for n in range(low, high):
                found = found + (blocks[n] == 4 * row + rb).astype(jnp.int32)
            tab[ROW_AT + 4 * group + rb] = found
    for k in range(8):
        tab[SLICE_AT + k] = ((y + k % 4) % 4) * 2 + (xl + k // 4) % 2


def build_body(one, zero, out):
    for i in range(8):
        for t in range(4):
            rows = pl.ds(t * B + i * 32, 32)
            out[i, 0, t] = one[rows, :]
            out[i, 1, t] = zero[rows, 0:B]
            out[i, 2, t] = zero[rows, B : 2 * B]


def pick_body(tab, spread, out):
    for n in range(32):
        out[n] = spread[tab[PICK_AT + n]]


def load(tab, inv_refs, low_refs, first, count, inv_s, low_s, inv_sem, low_sem):
    copies = []
    for q, ref in enumerate(low_refs):
        at = pl.ds(pl.multiple_of(tab[SLICE_AT + q] * 32, 32), 32)
        copies.append(
            pltpu.make_async_copy(
                ref.at[pl.ds(first, count)], low_s.at[:, at, :], low_sem.at[q]
            )
        )
    for q, ref in enumerate(inv_refs):
        for h in range(2):
            copies.append(
                pltpu.make_async_copy(
                    ref.at[:, pl.ds(h * B, B)], inv_s.at[2 * q + h], inv_sem.at[2 * q + h]
                )
            )
    for copy in copies:
        copy.start()
    return copies


def product(tab, inv_s, low_s, first, n):
    total = dot(inv_s[tab[POS_AT + first + n]], low_s[n])
    for j in range(1, 4):
        total += dot(inv_s[tab[POS_AT + first + n + j]], low_s[n + j])
    return total


def kids_body(tab, *refs):
    inv_refs, low_refs = refs[:16], refs[16:24]
    part_ref, inv_s, low_s, inv_sem, low_sem = refs[24:]
    copies = load(tab, inv_refs, low_refs, 16, 16, inv_s, low_s, inv_sem, low_sem)
    part_ref[...] = jnp.zeros_like(part_ref)
    for copy in copies:
        copy.wait()

    def step(n, carry):
        cols = pl.ds(pl.multiple_of((n // 2) * B, B), B)
        part_ref[:, cols] += product(tab, inv_s, low_s, 16, 4 * n)
        return carry

    lax.fori_loop(0, 4, step, 0)


def level_one_body(tab, *refs):
    inv_refs, low_refs = refs[:16], refs[16:24]
    own_ref, up_ref = refs[24:26]
    diag_refs = refs[26:34]
    inv_s, low_s, acc, diag, inv_sem, low_sem = refs[34:]
    copies = load(tab, inv_refs, low_refs, 0, 16, inv_s, low_s, inv_sem, low_sem)
    acc[...] = jnp.zeros_like(acc)
    diag[...] = jnp.zeros_like(diag)
    for copy in copies:
        copy.wait()

    def own_step(n, carry):
        acc[...] += product(tab, inv_s, low_s, 0, 4 * n)
        return carry

    lax.fori_loop(0, 4, own_step, 0)
    for rb in range(4):
        rows = pl.ds(rb * B, B)
        up_ref[rows, :] = jnp.zeros((B, B), BF)

        @pl.when(tab[ROW_AT + rb] > 0)
        def _():
            up = (-acc[rows, :]).astype(BF)
            up_ref[rows, :] = up
            diag[...] += dot_t(own_ref[rows, :], up)

    for k in range(8):
        at = pl.ds(pl.multiple_of(tab[SLICE_AT + k] * 32, 32), 32)
        diag_refs[k][...] = diag[at, :]


def level_one(tab, inv_pieces, low_pieces, factor_one):
    return call(
        level_one_body,
        [
            jax.ShapeDtypeStruct((LOC, B), BF),
        ]
        + [jax.ShapeDtypeStruct((32, B), F32)] * 8,
        [SMEM] + [HBM] * 24 + [VMEM],
        [
            pltpu.VMEM((32, LOC, B), BF),
            pltpu.VMEM((16, B, B), BF),
            pltpu.VMEM((LOC, B), F32),
            pltpu.VMEM((B, B), F32),
            pltpu.SemaphoreType.DMA((32,)),
            pltpu.SemaphoreType.DMA((8,)),
        ],
        limit=30,
    )(tab, *inv_pieces, *low_pieces, factor_one)


def kids(tab, inv_pieces, low_pieces):
    return call(
        kids_body,
        jax.ShapeDtypeStruct((LOC, 2 * B), F32),
        [SMEM] + [HBM] * 24,
        [
            pltpu.VMEM((32, LOC, B), BF),
            pltpu.VMEM((16, B, B), BF),
            pltpu.SemaphoreType.DMA((32,)),
            pltpu.SemaphoreType.DMA((8,)),
        ],
        limit=56,
        flops=2 * LOC * 16 * B * B,
        moved=24 * 2**20,
    )(tab, *inv_pieces, *low_pieces)


def pack_body(parent, spread, dinv, *refs):
    terms, out, diag = refs[:8], refs[8], refs[9]
    total = terms[0][...]
    for i in range(1, 8):
        total = total + terms[i][...]
    value = dinv[...] - total
    diag[...] = value
    half = value.astype(BF)
    for j in range(16):
        out[j, 0:64, :] = spread[parent[2 * j]]
        out[j, 64:128, :] = spread[parent[2 * j + 1]]
        out[j, 128:160, :] = half


def level_zero_body(tab, got, part, factor, link, up_ref, sums, both):
    both[...] = jnp.zeros_like(both)
    for e in range(2):
        cols = pl.ds(e * B, B)
        for rb in range(4):
            rows = pl.ds(rb * B, B)
            present = tab[ROW_AT + 4 * (e + 1) + rb] > 0

            @pl.when(jnp.logical_not(present))
            def _():
                up_ref[rows, cols] = jnp.zeros((B, B), BF)

            @pl.when(present)
            def _():
                above = got[4 * rb : 4 * rb + 4, e * 64 : e * 64 + 64, :].reshape(B, B)
                low = factor[rows, cols]
                total = part[rows, cols] + dot(above, link[:, cols])
                up = (-total).astype(BF)
                up_ref[rows, cols] = up
                both[0, :, cols] += dot_t(above, low)
                both[1, :, cols] += dot_t(low, up)

    for i in range(8):
        sums[i, 0:32, :] = both[0, i * 32 : i * 32 + 32, :]
        sums[i, 32:64, :] = both[1, i * 32 : i * 32 + 32, :]


def parent_body(tab, sums, got, link, diag, out):
    total = sums[0]
    for i in range(1, 8):
        total = total + sums[i]
    ups = []
    for e in range(2):
        cols = slice(e * B, e * B + B)
        half = got[tab[PAR_AT + e], 128:160, :]
        ups.append((-(total[0:32, cols] + dot(half, link[:, cols]))).astype(BF))
    up = jnp.concatenate(ups, axis=1)
    high = total[32:64].astype(BF)
    rest = (total[32:64] - high.astype(F32)).astype(BF)
    one_high = diag[...].astype(BF)
    one_rest = (diag[...] - one_high.astype(F32)).astype(BF)
    one = jnp.concatenate([one_high, one_rest], axis=1)
    for i in range(8):
        out[i, 96:128, :] = one
        out[i, 0:32, :] = up
        out[i, 32:64, :] = high
        out[i, 64:96, :] = rest


def last_body(got, dinv, link, up_ref, diag_ref, one_ref):
    for i in range(8):
        rows = pl.ds(i * 32, 32)
        up_ref[rows, :] = got[i, 0:32, :]
        one_ref[rows, :] = got[i, 96:128, 0:B].astype(F32) + got[i, 96:128, B : 2 * B].astype(F32)
        diag_ref[rows, :] = dinv[rows, :] - (
            got[i, 32:64, :].astype(F32) + got[i, 64:96, :].astype(F32)
        )
    for e in range(2):
        cols = pl.ds(e * B, B)
        diag_ref[:, cols] -= dot_t(link[:, cols], up_ref[:, cols])


def shards(
    inverse_anc,
    factor_one,
    factor_zero,
    factor_parent,
    dinv_one,
    dinv_zero,
    struct_one,
    select_zero,
    parent,
):
    row = lax.axis_index("prow")
    col = lax.axis_index("pcol")
    tab = pl.pallas_call(
        table_body,
        out_shape=jax.ShapeDtypeStruct((TABLE,), jnp.int32),
        in_specs=[SMEM] * 4,
        out_specs=SMEM,
    )(jnp.stack([row, col]).astype(jnp.int32), struct_one, select_zero, parent)
    link = lax.dynamic_slice_in_dim(factor_parent, col * 2 * B, 2 * B, 1)
    dinv_rows = lax.dynamic_slice_in_dim(dinv_one, row * 32, 32, 0)

    barrier = lax.optimization_barrier
    below, above = send(inverse_anc, Z_UP), send(inverse_anc, Z_DOWN)
    other = send(inverse_anc, X_HI)
    spread_low = call(
        build_body, jax.ShapeDtypeStruct((8, 3, 4, 32, B), BF), [VMEM, VMEM]
    )(factor_one, factor_zero)
    spread_low = lax.all_to_all(spread_low, "prow", 0, 0)

    own, below, above = barrier((inverse_anc, below, above))
    far = send(below, Z_UP)
    sib_own, sib_below, sib_above = send(own, SIBLING), send(below, SIBLING), send(above, SIBLING)

    spread_low, other, sib_own, sib_below, sib_above = barrier(
        (spread_low, other, sib_own, sib_below, sib_above)
    )
    other_above, other_below = send(other, Z_DOWN), send(other, Z_UP)
    mine = call(pick_body, jax.ShapeDtypeStruct((32, 32, B), BF), [SMEM, VMEM])(
        tab, spread_low.reshape(96, 32, B)
    )
    low_below, low_above = send(mine, Y_UP), send(mine, Y_DOWN)
    low_other = send(mine, X_LO)
    other_far = send(far, X_HI)
    sib_far, sib_other = send(far, SIBLING), send(other, SIBLING)
    low_far = send(low_below, Y_UP)
    low_other_above, low_other_below = send(low_other, Y_DOWN), send(low_other, Y_UP)
    low_other_far = send(low_other_above, Y_DOWN)
    sib_other_below, sib_other_above = send(other_below, SIBLING), send(other_above, SIBLING)
    sib_other_far = send(other_far, SIBLING)
    pieces = [own, above, far, below, other, other_above, other_far, other_below]
    pieces += [sib_own, sib_above, sib_far, sib_below]
    pieces += [sib_other, sib_other_above, sib_other_far, sib_other_below]
    low_pieces = [mine, low_above, low_far, low_below]
    low_pieces += [low_other, low_other_above, low_other_far, low_other_below]

    upper_one, *diag_parts = level_one(tab, pieces, low_pieces, factor_one)
    part = kids(tab, pieces, low_pieces)

    spread = lax.all_to_all(upper_one.reshape(16, 64, B), "pcol", 0, 0)
    terms = [diag_parts[0]]
    for k in range(1, 8):
        terms.append(send(diag_parts[k], moves(dy=k % 4, dxl=k // 4)))
    packed, diag_rows = call(
        pack_body,
        [jax.ShapeDtypeStruct((16, 160, B), BF), jax.ShapeDtypeStruct((32, B), F32)],
        [SMEM] + [VMEM] * 10,
    )(parent, spread, dinv_rows, *terms)
    got = lax.all_to_all(packed, "pcol", 0, 0)
    upper_zero, sums = call(
        level_zero_body,
        [jax.ShapeDtypeStruct((LOC, 2 * B), BF), jax.ShapeDtypeStruct((8, 64, 2 * B), F32)],
        [SMEM, VMEM, VMEM, VMEM, VMEM],
        [pltpu.VMEM((2, B, 2 * B), F32)],
    )(tab, got, part, factor_zero, link)
    sums = lax.all_to_all(sums, "prow", 0, 0)
    rows_out = call(
        parent_body,
        jax.ShapeDtypeStruct((8, 128, 2 * B), BF),
        [SMEM, VMEM, VMEM, VMEM, VMEM],
    )(tab, sums, got, link, diag_rows)
    rows_in = lax.all_to_all(rows_out, "prow", 0, 0)
    upper_parent, diag_zero, diag_one = call(
        last_body,
        [
            jax.ShapeDtypeStruct((B, 2 * B), BF),
            jax.ShapeDtypeStruct((B, 2 * B), F32),
            jax.ShapeDtypeStruct((B, B), F32),
        ],
        [VMEM, VMEM, VMEM],
    )(rows_in, dinv_zero, link)
    return upper_one, diag_one, upper_zero, upper_parent, diag_zero


def solution(mesh):
    in_specs = (
        P("prow", "pcol"),
        P("prow", "pcol"),
        P("prow", "pcol"),
        P(),
        P(None, "pcol"),
        P(None, "pcol"),
        P(),
        P(),
        P(),
    )
    out_specs = (
        P("prow", "pcol"),
        P(None, "pcol"),
        P("prow", "pcol"),
        P(None, "pcol"),
        P(None, "pcol"),
    )
    return jax.shard_map(shards, mesh=mesh, in_specs=in_specs, out_specs=out_specs, check_vma=False)
```

time: 261 us -> 215 us (0.82)
  blocking collectives: 65.9 us -> 37.4 us
  local copies, waits for them, and re-layouts: 28.7 us -> 7.7 us
  Pallas kernels: 23.2 us -> 30.3 us
  waiting for transfers between devices: 89.4 us -> 86.3 us
    all_gather x1 -> x0, blocking collectives: 35.1 us -> none  [shards(): diag_one = lax.all_gather(diag_rows, 'prow', axis=0, tiled=True)]
    ppermute x28 -> x29, waiting for transfers between devices: 51.7 us -> 78.2 us  [send(): return lax.ppermute(block, MESH_AXES, pairs)]
    all_to_all x1, waiting for transfers between devices: 12.3 us -> 0.01 us  [shards(): spread = lax.all_to_all(upper_one.reshape(16, 64, B), 'pcol', 0, 0)]
    slice x8 -> x0, local copies, waits for them, and re-layouts: 11.8 us -> none  [the longest x4 7.07 us: ring_gather(): other_far = (send(other_below[:half], up), send(other_above[half:], down))]
    all_to_all x1, waiting for transfers between devices: 19.9 us -> 8.15 us  [shards(): got = lax.all_to_all(packed, 'pcol', 0, 0)]
    pallas_call x2 -> x6, Pallas kernels: 19 us -> 25.3 us  [the longest x1 11.7 us: kids(): call(kids_body, jax.ShapeDtypeStruct((LOC, 2 * B), F32), [SMEM] + [HBM] *...]
    all_to_all x1, waiting for transfers between devices: 5.5 us -> 0.01 us  [shards(): spread_low = lax.all_to_all(spread_low, 'prow', 0, 0)]
    all_to_all x1, blocking collectives: 12.2 us -> 17.2 us  [shards(): rows_in = lax.all_to_all(rows_out, 'prow', 0, 0)]
  transfers between devices with their start and end apart: 32 -> 32, of which waited for: 12 -> 11; matrix products, arithmetic and copies ran while one was open for 9% -> 1% of each run, Pallas kernels for 0% -> 8%
where the time goes in v2:
time: 215 us; the launch traced here: 214 us
  waiting for transfers between devices  86.3 us (40%)
  starting transfers between devices  50.8 us (24%)
  blocking collectives  37.4 us (17%)
  Pallas kernels  30.3 us (14%)
  local copies, waits for them, and re-layouts  7.7 us (4%)
    ppermute x29, waiting for transfers between devices, send(): return lax.ppermute(block, MESH_AXES, pairs)  78.2 us
    ppermute x29, starting transfers between devices, send(): return lax.ppermute(block, MESH_AXES, pairs)  34.4 us
    all_to_all x1, blocking collectives, shards(): sums = lax.all_to_all(sums, 'prow', 0, 0)  20.2 us
    all_to_all x1, blocking collectives, shards(): rows_in = lax.all_to_all(rows_out, 'prow', 0, 0)  17.2 us
    pallas_call x1, Pallas kernels, kids(): call(kids_body, jax.ShapeDtypeStruct((LOC, 2 * B), F32), [SMEM] + [HBM] *...  11.7 us
    pallas_call x1, Pallas kernels, level_one(): call(level_one_body, [jax.ShapeDtypeStruct((LOC, B), BF)] + [jax.ShapeDty...  8.21 us
    all_to_all x1, waiting for transfers between devices, shards(): got = lax.all_to_all(packed, 'pcol', 0, 0)  8.15 us
    all_to_all x1, starting transfers between devices, shards(): got = lax.all_to_all(packed, 'pcol', 0, 0)  7.31 us
  transfers between devices with their start and end apart: 32, of which 11 were waited for; matrix products, arithmetic and copies ran while one was open for 1% of the time, Pallas kernels for 8%

profile of v2, /device:TPU:0, one launch (start us, length us, event | category | flops | bytes accessed | tf_op | source)
XLA Modules:
  0.0 214.2 jit_solution(5689161762472929642)
XLA Ops:
  0.6 0.0 copy-start
  0.6 2.1 collective-permute-start
  2.7 2.2 %collective-permute-start.1 = (bf16[1024,512]{1,0:T(8,128)(2,1)}, bf16[1024,512]{1,0:T(8,128)(2,1)}, u32[]{:S(2)}, u32[]{:S(2)}) collective-permute-start(bf16[1024,512]{1,0:T(8,128)(2,1)} %refs_0_.1), channel_id=1, source_target_pairs={{0,12},{1,13},{2,14},{3,15},{4,0},{5,1},{6,2},{7,3},{8,4},{9,5},{1... | collective-permute-start | bytes 3145736 | tf_op jit(solution)/shard_map/ppermute | solution.py:37
  4.9 1.2 copy-done.4
  6.1 1.0 copy-done.21
  7.2 1.3 shard_map.129
  8.5 5.5 %all-to-all-start = ((bf16[8,3,4,32,256]{4,3,2,1,0:T(8,128)(2,1)}), bf16[8,3,4,32,256]{4,3,2,1,0:T(8,128)(2,1)S(1)}, u32[]{:S(2)}, u32[]{:S(2)}) async-start(bf16[8,3,4,32,256]{4,3,2,1,0:T(8,128)(2,1)} %shard_map.129), calls=%async_computation | async-start | bytes 3145728 | tf_op jit(solution)/shard_map/all_to_all | solution.py:331
  14.0 2.8 %collective-permute-start.3 = (bf16[1024,512]{1,0:T(8,128)(2,1)S(1)}, bf16[1024,512]{1,0:T(8,128)(2,1)}, u32[]{:S(2)}, u32[]{:S(2)}) collective-permute-start(bf16[1024,512]{1,0:T(8,128)(2,1)S(1)} %copy-done.3), channel_id=1, source_target_pairs={{0,2},{1,3},{2,0},{3,1},{4,6},{5,7},{6,4},{7,5},{8,10},{9,11},{10,... | collective-permute-start | bytes 3145736 | tf_op jit(solution)/shard_map/ppermute | solution.py:37
  16.8 11.5 %collective-permute-done.refs_3_ = bf16[1024,512]{1,0:T(8,128)(2,1)} collective-permute-done((bf16[1024,512]{1,0:T(8,128)(2,1)}, bf16[1024,512]{1,0:T(8,128)(2,1)}, u32[]{:S(2)}, u32[]{:S(2)}) %collective-permute-start) | collective-permute-done | bytes 1048608 | tf_op jit(solution)/shard_map/ppermute | solution.py:37
  28.3 0.5 collective-permute-start.4
  28.8 0.0 collective-permute-start.6
  28.8 1.3 collective-permute-start.2
  30.1 0.7 copy.14.select
  30.8 0.6 pad_add_fusion.place
  31.4 2.8 %shard_map.128.tab = s32[86]{0:T(128)} custom-call(s32[2]{0:T(128)} %pad_add_fusion.place, s32[16,16]{1,0:T(8,128)} %struct.1, s32[32,8]{1,0:T(8,128)} %copy.14.select, s32[32]{0:T(128)} %parent.3), custom_call_target="tpu_custom_call" | custom-call | tf_op jit(solution)/shard_map/pallas_call | solution.py:316
  34.2 22.4 %collective-permute-done.3.refs_4_ = bf16[1024,512]{1,0:T(8,128)(2,1)} collective-permute-done((bf16[1024,512]{1,0:T(8,128)(2,1)S(1)}, bf16[1024,512]{1,0:T(8,128)(2,1)}, u32[]{:S(2)}, u32[]{:S(2)}) %collective-permute-start.3) | collective-permute-done | bytes 1048608 | tf_op jit(solution)/shard_map/ppermute | solution.py:37
  56.6 0.0 all-to-all-done
  56.6 0.0 collective-permute-done.5.refs_11_
  56.6 0.6 copy-done.24
  57.3 0.6 shard_map.130.refs_16_
  57.8 0.0 copy-start.2
  57.9 1.2 collective-permute-start.18
  59.1 1.4 collective-permute-start.16
  60.5 1.8 collective-permute-start.15
  62.3 1.6 collective-permute-start.7
  63.9 0.5 collective-permute-start.9
  64.3 6.1 %collective-permute-done.18.refs_20_ = bf16[32,32,256]{2,1,0:T(8,128)(2,1)S(1)} collective-permute-done((bf16[32,32,256]{2,1,0:T(8,128)(2,1)S(1)}, bf16[32,32,256]{2,1,0:T(8,128)(2,1)S(1)}, u32[]{:S(2)}, u32[]{:S(2)}) %collective-permute-start.18) | collective-permute-done | bytes 524320 | tf_op jit(solution)/shard_map/ppermute | solution.py:37
  70.4 1.8 collective-permute-done.16.refs_19_
  72.2 2.0 collective-permute-start.8
  74.2 10.9 %collective-permute-done.7.refs_5_ = bf16[1024,512]{1,0:T(8,128)(2,1)S(1)} collective-permute-done((bf16[1024,512]{1,0:T(8,128)(2,1)}, bf16[1024,512]{1,0:T(8,128)(2,1)S(1)}, u32[]{:S(2)}, u32[]{:S(2)}) %collective-permute-start.7) | collective-permute-done | bytes 1048608 | tf_op jit(solution)/shard_map/ppermute | solution.py:37
  85.1 1.4 collective-permute-start.19
  86.5 0.8 collective-permute-done.9.refs_7_
  87.3 0.3 collective-permute-start.21
  87.6 10.1 %collective-permute-done.8.refs_6_ = bf16[1024,512]{1,0:T(8,128)(2,1)S(1)} collective-permute-done((bf16[1024,512]{1,0:T(8,128)(2,1)}, bf16[1024,512]{1,0:T(8,128)(2,1)S(1)}, u32[]{:S(2)}, u32[]{:S(2)}) %collective-permute-start.8) | collective-permute-done | bytes 1048608 | tf_op jit(solution)/shard_map/ppermute | solution.py:37
  97.7 0.5 collective-permute-start.13
  98.2 1.4 collective-permute-start.17
  99.7 1.8 collective-permute-start.20
  101.5 11.9 %collective-permute-done.17.refs_18_ = bf16[32,32,256]{2,1,0:T(8,128)(2,1)S(1)} collective-permute-done((bf16[32,32,256]{2,1,0:T(8,128)(2,1)S(1)}, bf16[32,32,256]{2,1,0:T(8,128)(2,1)S(1)}, u32[]{:S(2)}, u32[]{:S(2)}) %collective-permute-start.17) | collective-permute-done | bytes 524320 | tf_op jit(solution)/shard_map/ppermute | solution.py:37
  113.4 0.0 copy-start.22
  113.4 1.4 copy-done.22
  114.9 8.2 %shard_map.131 = (bf16[1024,256]{1,0:T(8,128)(2,1)}, f32[32,256]{1,0:T(8,128)S(1)}, f32[32,256]{1,0:T(8,128)S(1)}, f32[32,256]{1,0:T(8,128)S(1)}, f32[32,256]{1,...) custom-call(s32[86]{0:T(128)S(1)} %copy-done.25, ...), custom_call_target="tpu_custom_call" | custom-call | tf_op jit(solution)/shard_map/pallas_call | solution.py:191
  123.3 3.6 %all-to-all-start.1 = ((bf16[16,64,256]{2,1,0:T(8,128)(2,1)}), bf16[16,64,256]{2,1,0:T(8,128)(2,1)S(1)}, u32[]{:S(2)}, u32[]{:S(2)}) async-start(bf16[16,64,256]{2,1,0:T(8,128)(2,1)} %bitcast.5), calls=%async_computation.1 | async-start | bytes 1048576 | tf_op jit(solution)/shard_map/all_to_all | solution.py:362
  126.9 1.6 collective-permute-start.22
  128.4 2.9 %collective-permute-start.23 = (f32[32,256]{1,0:T(8,128)S(1)}, f32[32,256]{1,0:T(8,128)S(1)}, u32[]{:S(2)}, u32[]{:S(2)}) collective-permute-start(f32[32,256]{1,0:T(8,128)S(1)} %get-tuple-element.40), channel_id=1, source_target_pairs={{0,64},{1,65},{2,66},{3,67},{4,68},{5,69},{6,70},{7,71},{8,72},{9,... | collective-permute-start | bytes 98312 | tf_op jit(solution)/shard_map/ppermute | solution.py:37
  131.3 1.0 collective-permute-start.24
  132.4 1.1 collective-permute-start.25
  133.4 1.4 collective-permute-start.26
  134.8 1.0 collective-permute-start.27
  135.8 2.6 %collective-permute-start.28 = (f32[32,256]{1,0:T(8,128)S(1)}, f32[32,256]{1,0:T(8,128)S(1)}, u32[]{:S(2)}, u32[]{:S(2)}) collective-permute-start(f32[32,256]{1,0:T(8,128)S(1)} %get-tuple-element.45), channel_id=1, source_target_pairs={{0,112},{1,113},{2,114},{3,115},{4,116},{5,117},{6,118},{7,119},{8... | collective-permute-start | bytes 98312 | tf_op jit(solution)/shard_map/ppermute | solution.py:37
  138.5 1.0 collective-permute-done.26.refs_5_
  139.5 1.7 collective-permute-done.27.refs_6_
  141.2 1.7 shard_map.132
  143.0 7.3 %all-to-all-start.2 = ((bf16[16,160,256]{2,1,0:T(8,128)(2,1)}), bf16[16,160,256]{2,1,0:T(8,128)(2,1)S(1)}, u32[]{:S(2)}, u32[]{:S(2)}) async-start(bf16[16,160,256]{2,1,0:T(8,128)(2,1)} %get-tuple-element.46), calls=%async_computation.2 | async-start | bytes 2621440 | tf_op jit(solution)/shard_map/all_to_all | solution.py:371
  150.3 1.0 constant_dynamic-slice_fusion.link
  151.3 0.0 copy-start.5
  151.3 11.7 %shard_map.133.part = f32[1024,512]{1,0:T(8,128)} custom-call(s32[86]{0:T(128)} %shard_map.128.tab, bf16[1024,512]{1,0:T(8,128)(2,1)} %refs_0_.1, bf16[1024,512]{1,0:T(8,128)(2,1)} %collective-permute-done.1.refs_1_, bf16[1024,512]{1,0:T(8,128)(2,1)} %collective-permute-done.2.refs_2_, bf16[1024,512]{1,0:T(8,128)(2,1)} %collective-permute-done.refs_3_, ...), custom_call_target="tpu_custom_call" | custom-call | flops 2147483648 | bytes 25165824 | tf_op jit(solution)/shard_map/pallas_call | solution.py:211
  163.0 8.2 %all-to-all-done.2.got = bf16[16,160,256]{2,1,0:T(8,128)(2,1)S(1)} async-done(((bf16[16,160,256]{2,1,0:T(8,128)(2,1)}), bf16[16,160,256]{2,1,0:T(8,128)(2,1)S(1)}, u32[]{:S(2)}, u32[]{:S(2)}) %all-to-all-start.2) | async-done | bytes 1310752 | tf_op jit(solution)/shard_map/all_to_all | solution.py:371
  171.2 1.6 copy-done.1
  172.8 2.1 shard_map.134
  174.9 20.2 %all_to_all.25.sums = f32[8,64,512]{2,1,0:T(8,128)S(1)} all-to-all(f32[8,64,512]{2,1,0:T(8,128)S(1)} %get-tuple-element.47), channel_id=1, replica_groups=mesh['prow'=8,'pcol'=16] {'prow'}, dimensions={0} | all-to-all | bytes 2097152 | tf_op jit(solution)/shard_map/all_to_all | solution.py:378
  195.1 0.7 shard_map.135
  195.8 0.0 copy-start.23
  195.8 17.2 %all_to_all.26.got = bf16[8,128,512]{2,1,0:T(8,128)(2,1)S(1)} all-to-all(bf16[8,128,512]{2,1,0:T(8,128)(2,1)S(1)} %shard_map.135), channel_id=1, replica_groups=mesh['prow'=8,'pcol'=16] {'prow'}, dimensions={0} | all-to-all | bytes 2097152 | tf_op jit(solution)/shard_map/all_to_all | solution.py:384
  213.0 1.2 shard_map.136
  (73 shorter events, 0.2 us)
Async XLA Ops:
  0.6 137.8 %copy-start = (f32[256,256]{1,0:T(8,128)S(1)}, f32[256,256]{1,0:T(8,128)}, u32[]{:S(2)}) copy-start(f32[256,256]{1,0:T(8,128)} %param.13) | copy-start | bytes 786436
  0.6 27.7 %collective-permute-start = (bf16[1024,512]{1,0:T(8,128)(2,1)}, bf16[1024,512]{1,0:T(8,128)(2,1)}, u32[]{:S(2)}, u32[]{:S(2)}) collective-permute-start(bf16[1024,512]{1,0:T(8,128)(2,1)} %refs_0_.1), channel_id=1, source_target_pairs={{0,4},{1,5},{2,6},{3,7},{4,8},{5,9},{6,10},{7,11},{8,12},{9,13},{1... | collective-permute-start | bytes 3145736 | tf_op jit(solution)/shard_map/ppermute | solution.py:37
  2.7 25.6 %collective-permute-start.1 = (bf16[1024,512]{1,0:T(8,128)(2,1)}, bf16[1024,512]{1,0:T(8,128)(2,1)}, u32[]{:S(2)}, u32[]{:S(2)}) collective-permute-start(bf16[1024,512]{1,0:T(8,128)(2,1)} %refs_0_.1), channel_id=1, source_target_pairs={{0,12},{1,13},{2,14},{3,15},{4,0},{5,1},{6,2},{7,3},{8,4},{9,5},{1... | collective-permute-start | bytes 3145736 | tf_op jit(solution)/shard_map/ppermute | solution.py:37
  4.9 1.2 copy-start.4
  6.1 1.0 copy-start.21
  8.5 5.5 %copy-start.3 = (bf16[1024,512]{1,0:T(8,128)(2,1)S(1)}, bf16[1024,512]{1,0:T(8,128)(2,1)}, u32[]{:S(2)}) copy-start(bf16[1024,512]{1,0:T(8,128)(2,1)} %refs_0_.1) | copy-start | bytes 3145732
  8.5 21.6 %copy-start.28 = (s32[32,8]{0,1:T(8,128)S(1)}, s32[32,8]{0,1:T(8,128)}, u32[]{:S(2)}) copy-start(s32[32,8]{0,1:T(8,128)} %param.16) | copy-start | bytes 3076
  8.5 48.1 %all-to-all-start = ((bf16[8,3,4,32,256]{4,3,2,1,0:T(8,128)(2,1)}), bf16[8,3,4,32,256]{4,3,2,1,0:T(8,128)(2,1)S(1)}, u32[]{:S(2)}, u32[]{:S(2)}) async-start(bf16[8,3,4,32,256]{4,3,2,1,0:T(8,128)(2,1)} %shard_map.129), calls=%async_computation | async-start | bytes 3145728 | tf_op jit(solution)/shard_map/all_to_all | solution.py:331
  14.0 42.6 %collective-permute-start.3 = (bf16[1024,512]{1,0:T(8,128)(2,1)S(1)}, bf16[1024,512]{1,0:T(8,128)(2,1)}, u32[]{:S(2)}, u32[]{:S(2)}) collective-permute-start(bf16[1024,512]{1,0:T(8,128)(2,1)S(1)} %copy-done.3), channel_id=1, source_target_pairs={{0,2},{1,3},{2,0},{3,1},{4,6},{5,7},{6,4},{7,5},{8,10},{9,11},{10,... | collective-permute-start | bytes 3145736 | tf_op jit(solution)/shard_map/ppermute | solution.py:37
  28.3 28.3 %collective-permute-start.5 = (bf16[1024,512]{1,0:T(8,128)(2,1)}, bf16[1024,512]{1,0:T(8,128)(2,1)}, u32[]{:S(2)}, u32[]{:S(2)}) collective-permute-start(bf16[1024,512]{1,0:T(8,128)(2,1)} %collective-permute-done.refs_3_), channel_id=1, source_target_pairs={{0,1},{1,0},{2,3},{3,2},{4,5},{5,4},{6,7},{7,6},{8,9},{9,8},{10,11... | collective-permute-start | bytes 3145736 | tf_op jit(solution)/shard_map/ppermute | solution.py:37
  28.3 28.3 %collective-permute-start.4 = (bf16[1024,512]{1,0:T(8,128)(2,1)S(1)}, bf16[1024,512]{1,0:T(8,128)(2,1)}, u32[]{:S(2)}, u32[]{:S(2)}) collective-permute-start(bf16[1024,512]{1,0:T(8,128)(2,1)S(1)} %copy-done.3), channel_id=1, source_target_pairs={{0,1},{1,0},{2,3},{3,2},{4,5},{5,4},{6,7},{7,6},{8,9},{9,8},{10,11... | collective-permute-start | bytes 3145736 | tf_op jit(solution)/shard_map/ppermute | solution.py:37
  28.8 27.8 %collective-permute-start.6 = (bf16[1024,512]{1,0:T(8,128)(2,1)}, bf16[1024,512]{1,0:T(8,128)(2,1)}, u32[]{:S(2)}, u32[]{:S(2)}) collective-permute-start(bf16[1024,512]{1,0:T(8,128)(2,1)} %collective-permute-done.1.refs_1_), channel_id=1, source_target_pairs={{0,1},{1,0},{2,3},{3,2},{4,5},{5,4},{6,7},{7,6},{8,9},{9,8},{10,11... | collective-permute-start | bytes 3145736 | tf_op jit(solution)/shard_map/ppermute | solution.py:37
  28.8 35.1 %collective-permute-start.2 = (bf16[1024,512]{1,0:T(8,128)(2,1)}, bf16[1024,512]{1,0:T(8,128)(2,1)}, u32[]{:S(2)}, u32[]{:S(2)}) collective-permute-start(bf16[1024,512]{1,0:T(8,128)(2,1)} %collective-permute-done.refs_3_), channel_id=1, source_target_pairs={{0,4},{1,5},{2,6},{3,7},{4,8},{5,9},{6,10},{7,11},{8,12},{9,13},{1... | collective-permute-start | bytes 3145736 | tf_op jit(solution)/shard_map/ppermute | solution.py:37
  34.2 79.3 %copy-start.25 = (s32[86]{0:T(128)S(1)}, s32[86]{0:T(128)}, u32[]{:S(2)}) copy-start(s32[86]{0:T(128)} %shard_map.128.tab) | copy-start | bytes 1036
  56.6 0.7 copy-start.24
  57.3 84.0 %copy-start.27 = (s32[32]{0:T(128)S(1)}, s32[32]{0:T(128)}, u32[]{:S(2)}) copy-start(s32[32]{0:T(128)} %parent.3) | copy-start | bytes 388
  57.8 65.3 %copy-start.2 = (bf16[32,32,256]{2,1,0:T(8,128)(2,1)}, bf16[32,32,256]{2,1,0:T(8,128)(2,1)S(1)}, u32[]{:S(2)}) copy-start(bf16[32,32,256]{2,1,0:T(8,128)(2,1)S(1)} %shard_map.130.refs_16_) | copy-start | bytes 1572868
  57.9 12.6 %collective-permute-start.18 = (bf16[32,32,256]{2,1,0:T(8,128)(2,1)S(1)}, bf16[32,32,256]{2,1,0:T(8,128)(2,1)S(1)}, u32[]{:S(2)}, u32[]{:S(2)}) collective-permute-start(bf16[32,32,256]{2,1,0:T(8,128)(2,1)S(1)} %shard_map.130.refs_16_), channel_id=1, source_target_pairs={{0,16},{1,17},{2,18},{3,19},{4,20},{5,21},{6,22},{7,23},{8,24},{9,... | collective-permute-start | bytes 1572872 | tf_op jit(solution)/shard_map/ppermute | solution.py:37
  59.1 13.1 %collective-permute-start.16 = (bf16[32,32,256]{2,1,0:T(8,128)(2,1)S(1)}, bf16[32,32,256]{2,1,0:T(8,128)(2,1)S(1)}, u32[]{:S(2)}, u32[]{:S(2)}) collective-permute-start(bf16[32,32,256]{2,1,0:T(8,128)(2,1)S(1)} %shard_map.130.refs_16_), channel_id=1, source_target_pairs={{0,32},{1,33},{2,34},{3,35},{4,36},{5,37},{6,38},{7,39},{8,40},{9,... | collective-permute-start | bytes 1572872 | tf_op jit(solution)/shard_map/ppermute | solution.py:37
  60.5 13.7 %collective-permute-start.15 = (bf16[32,32,256]{2,1,0:T(8,128)(2,1)S(1)}, bf16[32,32,256]{2,1,0:T(8,128)(2,1)S(1)}, u32[]{:S(2)}, u32[]{:S(2)}) collective-permute-start(bf16[32,32,256]{2,1,0:T(8,128)(2,1)S(1)} %shard_map.130.refs_16_), channel_id=1, source_target_pairs={{0,96},{1,97},{2,98},{3,99},{4,100},{5,101},{6,102},{7,103},{8,104... | collective-permute-start | bytes 1572872 | tf_op jit(solution)/shard_map/ppermute | solution.py:37
  62.3 22.8 %collective-permute-start.7 = (bf16[1024,512]{1,0:T(8,128)(2,1)}, bf16[1024,512]{1,0:T(8,128)(2,1)S(1)}, u32[]{:S(2)}, u32[]{:S(2)}) collective-permute-start(bf16[1024,512]{1,0:T(8,128)(2,1)} %collective-permute-done.3.refs_4_), channel_id=1, source_target_pairs={{0,12},{1,13},{2,14},{3,15},{4,0},{5,1},{6,2},{7,3},{8,4},{9,5},{1... | collective-permute-start | bytes 3145736 | tf_op jit(solution)/shard_map/ppermute | solution.py:37
  63.9 23.4 %collective-permute-start.9 = (bf16[1024,512]{1,0:T(8,128)(2,1)}, bf16[1024,512]{1,0:T(8,128)(2,1)S(1)}, u32[]{:S(2)}, u32[]{:S(2)}) collective-permute-start(bf16[1024,512]{1,0:T(8,128)(2,1)} %collective-permute-done.3.refs_4_), channel_id=1, source_target_pairs={{0,4},{1,5},{2,6},{3,7},{4,8},{5,9},{6,10},{7,11},{8,12},{9,13},{1... | collective-permute-start | bytes 3145736 | tf_op jit(solution)/shard_map/ppermute | solution.py:37
  70.4 52.7 %copy-start.14 = (bf16[32,32,256]{2,1,0:T(8,128)(2,1)}, bf16[32,32,256]{2,1,0:T(8,128)(2,1)S(1)}, u32[]{:S(2)}) copy-start(bf16[32,32,256]{2,1,0:T(8,128)(2,1)S(1)} %collective-permute-done.18.refs_20_) | copy-start | bytes 1572868
  70.4 17.2 %collective-permute-start.11 = (bf16[1024,512]{1,0:T(8,128)(2,1)}, bf16[1024,512]{1,0:T(8,128)(2,1)S(1)}, u32[]{:S(2)}, u32[]{:S(2)}) collective-permute-start(bf16[1024,512]{1,0:T(8,128)(2,1)} %collective-permute-done.3.refs_4_), channel_id=1, source_target_pairs={{0,1},{1,0},{2,3},{3,2},{4,5},{5,4},{6,7},{7,6},{8,9},{9,8},{10,11... | collective-permute-start | bytes 3145736 | tf_op jit(solution)/shard_map/ppermute | solution.py:37
  72.2 50.9 %copy-start.15 = (bf16[32,32,256]{2,1,0:T(8,128)(2,1)}, bf16[32,32,256]{2,1,0:T(8,128)(2,1)S(1)}, u32[]{:S(2)}) copy-start(bf16[32,32,256]{2,1,0:T(8,128)(2,1)S(1)} %collective-permute-done.16.refs_19_) | copy-start | bytes 1572868
  72.2 25.5 %collective-permute-start.8 = (bf16[1024,512]{1,0:T(8,128)(2,1)}, bf16[1024,512]{1,0:T(8,128)(2,1)S(1)}, u32[]{:S(2)}, u32[]{:S(2)}) collective-permute-start(bf16[1024,512]{1,0:T(8,128)(2,1)} %collective-permute-done.2.refs_2_), channel_id=1, source_target_pairs={{0,2},{1,3},{2,0},{3,1},{4,6},{5,7},{6,4},{7,5},{8,10},{9,11},{10,... | collective-permute-start | bytes 3145736 | tf_op jit(solution)/shard_map/ppermute | solution.py:37
  74.2 48.9 %copy-start.16 = (bf16[32,32,256]{2,1,0:T(8,128)(2,1)}, bf16[32,32,256]{2,1,0:T(8,128)(2,1)S(1)}, u32[]{:S(2)}) copy-start(bf16[32,32,256]{2,1,0:T(8,128)(2,1)S(1)} %collective-permute-done.15.refs_17_) | copy-start | bytes 1572868
  74.2 23.5 %collective-permute-start.10 = (bf16[1024,512]{1,0:T(8,128)(2,1)}, bf16[1024,512]{1,0:T(8,128)(2,1)S(1)}, u32[]{:S(2)}, u32[]{:S(2)}) collective-permute-start(bf16[1024,512]{1,0:T(8,128)(2,1)} %collective-permute-done.2.refs_2_), channel_id=1, source_target_pairs={{0,1},{1,0},{2,3},{3,2},{4,5},{5,4},{6,7},{7,6},{8,9},{9,8},{10,11... | collective-permute-start | bytes 3145736 | tf_op jit(solution)/shard_map/ppermute | solution.py:37
  85.1 38.0 %copy-start.6 = (bf16[1024,512]{1,0:T(8,128)(2,1)}, bf16[1024,512]{1,0:T(8,128)(2,1)S(1)}, u32[]{:S(2)}) copy-start(bf16[1024,512]{1,0:T(8,128)(2,1)S(1)} %collective-permute-done.7.refs_5_) | copy-start | bytes 3145732
  85.1 13.1 %collective-permute-start.19 = (bf16[32,32,256]{2,1,0:T(8,128)(2,1)S(1)}, bf16[32,32,256]{2,1,0:T(8,128)(2,1)S(1)}, u32[]{:S(2)}, u32[]{:S(2)}) collective-permute-start(bf16[32,32,256]{2,1,0:T(8,128)(2,1)S(1)} %collective-permute-done.18.refs_20_), channel_id=1, source_target_pairs={{0,96},{1,97},{2,98},{3,99},{4,100},{5,101},{6,102},{7,103},{8,104... | collective-permute-start | bytes 1572872 | tf_op jit(solution)/shard_map/ppermute | solution.py:37
  87.3 35.8 %copy-start.7 = (bf16[1024,512]{1,0:T(8,128)(2,1)}, bf16[1024,512]{1,0:T(8,128)(2,1)S(1)}, u32[]{:S(2)}) copy-start(bf16[1024,512]{1,0:T(8,128)(2,1)S(1)} %collective-permute-done.9.refs_7_) | copy-start | bytes 3145732
  87.3 12.3 %collective-permute-start.21 = (bf16[32,32,256]{2,1,0:T(8,128)(2,1)S(1)}, bf16[32,32,256]{2,1,0:T(8,128)(2,1)S(1)}, u32[]{:S(2)}, u32[]{:S(2)}) collective-permute-start(bf16[32,32,256]{2,1,0:T(8,128)(2,1)S(1)} %collective-permute-done.18.refs_20_), channel_id=1, source_target_pairs={{0,32},{1,33},{2,34},{3,35},{4,36},{5,37},{6,38},{7,39},{8,40},{9,... | collective-permute-start | bytes 1572872 | tf_op jit(solution)/shard_map/ppermute | solution.py:37
  87.6 35.5 %copy-start.8 = (bf16[1024,512]{1,0:T(8,128)(2,1)}, bf16[1024,512]{1,0:T(8,128)(2,1)S(1)}, u32[]{:S(2)}) copy-start(bf16[1024,512]{1,0:T(8,128)(2,1)S(1)} %collective-permute-done.11.refs_12_) | copy-start | bytes 3145732
  87.6 25.7 %collective-permute-start.12 = (bf16[1024,512]{1,0:T(8,128)(2,1)S(1)}, bf16[1024,512]{1,0:T(8,128)(2,1)S(1)}, u32[]{:S(2)}, u32[]{:S(2)}) collective-permute-start(bf16[1024,512]{1,0:T(8,128)(2,1)S(1)} %collective-permute-done.7.refs_5_), channel_id=1, source_target_pairs={{0,1},{1,0},{2,3},{3,2},{4,5},{5,4},{6,7},{7,6},{8,9},{9,8},{10,11... | collective-permute-start | bytes 3145736 | tf_op jit(solution)/shard_map/ppermute | solution.py:37
  97.7 25.5 %copy-start.9 = (bf16[1024,512]{1,0:T(8,128)(2,1)}, bf16[1024,512]{1,0:T(8,128)(2,1)S(1)}, u32[]{:S(2)}) copy-start(bf16[1024,512]{1,0:T(8,128)(2,1)S(1)} %collective-permute-done.8.refs_6_) | copy-start | bytes 3145732
  97.7 15.7 %collective-permute-start.14 = (bf16[1024,512]{1,0:T(8,128)(2,1)S(1)}, bf16[1024,512]{1,0:T(8,128)(2,1)S(1)}, u32[]{:S(2)}, u32[]{:S(2)}) collective-permute-start(bf16[1024,512]{1,0:T(8,128)(2,1)S(1)} %collective-permute-done.9.refs_7_), channel_id=1, source_target_pairs={{0,1},{1,0},{2,3},{3,2},{4,5},{5,4},{6,7},{7,6},{8,9},{9,8},{10,11... | collective-permute-start | bytes 3145736 | tf_op jit(solution)/shard_map/ppermute | solution.py:37
  97.7 25.5 %copy-start.10 = (bf16[1024,512]{1,0:T(8,128)(2,1)}, bf16[1024,512]{1,0:T(8,128)(2,1)S(1)}, u32[]{:S(2)}) copy-start(bf16[1024,512]{1,0:T(8,128)(2,1)S(1)} %collective-permute-done.10.refs_10_) | copy-start | bytes 3145732
  97.7 15.7 %collective-permute-start.13 = (bf16[1024,512]{1,0:T(8,128)(2,1)S(1)}, bf16[1024,512]{1,0:T(8,128)(2,1)S(1)}, u32[]{:S(2)}, u32[]{:S(2)}) collective-permute-start(bf16[1024,512]{1,0:T(8,128)(2,1)S(1)} %collective-permute-done.8.refs_6_), channel_id=1, source_target_pairs={{0,1},{1,0},{2,3},{3,2},{4,5},{5,4},{6,7},{7,6},{8,9},{9,8},{10,11... | collective-permute-start | bytes 3145736 | tf_op jit(solution)/shard_map/ppermute | solution.py:37
  98.2 25.0 %copy-start.17 = (bf16[32,32,256]{2,1,0:T(8,128)(2,1)}, bf16[32,32,256]{2,1,0:T(8,128)(2,1)S(1)}, u32[]{:S(2)}) copy-start(bf16[32,32,256]{2,1,0:T(8,128)(2,1)S(1)} %collective-permute-done.19.refs_21_) | copy-start | bytes 1572868
  98.2 15.1 %collective-permute-start.17 = (bf16[32,32,256]{2,1,0:T(8,128)(2,1)S(1)}, bf16[32,32,256]{2,1,0:T(8,128)(2,1)S(1)}, u32[]{:S(2)}, u32[]{:S(2)}) collective-permute-start(bf16[32,32,256]{2,1,0:T(8,128)(2,1)S(1)} %collective-permute-done.16.refs_19_), channel_id=1, source_target_pairs={{0,32},{1,33},{2,34},{3,35},{4,36},{5,37},{6,38},{7,39},{8,40},{9,... | collective-permute-start | bytes 1572872 | tf_op jit(solution)/shard_map/ppermute | solution.py:37
  99.7 23.5 %copy-start.18 = (bf16[32,32,256]{2,1,0:T(8,128)(2,1)}, bf16[32,32,256]{2,1,0:T(8,128)(2,1)S(1)}, u32[]{:S(2)}) copy-start(bf16[32,32,256]{2,1,0:T(8,128)(2,1)S(1)} %collective-permute-done.21.refs_23_) | copy-start | bytes 1572868
  99.7 13.7 %collective-permute-start.20 = (bf16[32,32,256]{2,1,0:T(8,128)(2,1)S(1)}, bf16[32,32,256]{2,1,0:T(8,128)(2,1)S(1)}, u32[]{:S(2)}, u32[]{:S(2)}) collective-permute-start(bf16[32,32,256]{2,1,0:T(8,128)(2,1)S(1)} %collective-permute-done.19.refs_21_), channel_id=1, source_target_pairs={{0,96},{1,97},{2,98},{3,99},{4,100},{5,101},{6,102},{7,103},{8,104... | collective-permute-start | bytes 1572872 | tf_op jit(solution)/shard_map/ppermute | solution.py:37
  113.4 9.8 %copy-start.19 = (bf16[32,32,256]{2,1,0:T(8,128)(2,1)}, bf16[32,32,256]{2,1,0:T(8,128)(2,1)S(1)}, u32[]{:S(2)}) copy-start(bf16[32,32,256]{2,1,0:T(8,128)(2,1)S(1)} %collective-permute-done.17.refs_18_) | copy-start | bytes 1572868
  113.4 9.8 %copy-start.20 = (bf16[32,32,256]{2,1,0:T(8,128)(2,1)}, bf16[32,32,256]{2,1,0:T(8,128)(2,1)S(1)}, u32[]{:S(2)}) copy-start(bf16[32,32,256]{2,1,0:T(8,128)(2,1)S(1)} %collective-permute-done.20.refs_22_) | copy-start | bytes 1572868
  113.4 9.8 %copy-start.11 = (bf16[1024,512]{1,0:T(8,128)(2,1)}, bf16[1024,512]{1,0:T(8,128)(2,1)S(1)}, u32[]{:S(2)}) copy-start(bf16[1024,512]{1,0:T(8,128)(2,1)S(1)} %collective-permute-done.12.refs_13_) | copy-start | bytes 3145732
  113.4 9.8 %copy-start.12 = (bf16[1024,512]{1,0:T(8,128)(2,1)}, bf16[1024,512]{1,0:T(8,128)(2,1)S(1)}, u32[]{:S(2)}) copy-start(bf16[1024,512]{1,0:T(8,128)(2,1)S(1)} %collective-permute-done.14.refs_15_) | copy-start | bytes 3145732
  113.4 1.4 copy-start.22
  114.9 8.4 %copy-start.13 = (bf16[1024,512]{1,0:T(8,128)(2,1)}, bf16[1024,512]{1,0:T(8,128)(2,1)S(1)}, u32[]{:S(2)}) copy-start(bf16[1024,512]{1,0:T(8,128)(2,1)S(1)} %collective-permute-done.13.refs_14_) | copy-start | bytes 3145732
  123.3 18.0 %all-to-all-start.1 = ((bf16[16,64,256]{2,1,0:T(8,128)(2,1)}), bf16[16,64,256]{2,1,0:T(8,128)(2,1)S(1)}, u32[]{:S(2)}, u32[]{:S(2)}) async-start(bf16[16,64,256]{2,1,0:T(8,128)(2,1)} %bitcast.5), calls=%async_computation.1 | async-start | bytes 1048576 | tf_op jit(solution)/shard_map/all_to_all | solution.py:362
  126.9 8.0 %collective-permute-start.22 = (f32[32,256]{1,0:T(8,128)S(1)}, f32[32,256]{1,0:T(8,128)S(1)}, u32[]{:S(2)}, u32[]{:S(2)}) collective-permute-start(f32[32,256]{1,0:T(8,128)S(1)} %get-tuple-element.39), channel_id=1, source_target_pairs={{0,32},{1,33},{2,34},{3,35},{4,36},{5,37},{6,38},{7,39},{8,40},{9,... | collective-permute-start | bytes 98312 | tf_op jit(solution)/shard_map/ppermute | solution.py:37
  128.4 7.4 %collective-permute-start.23 = (f32[32,256]{1,0:T(8,128)S(1)}, f32[32,256]{1,0:T(8,128)S(1)}, u32[]{:S(2)}, u32[]{:S(2)}) collective-permute-start(f32[32,256]{1,0:T(8,128)S(1)} %get-tuple-element.40), channel_id=1, source_target_pairs={{0,64},{1,65},{2,66},{3,67},{4,68},{5,69},{6,70},{7,71},{8,72},{9,... | collective-permute-start | bytes 98312 | tf_op jit(solution)/shard_map/ppermute | solution.py:37
  131.3 7.1 %collective-permute-start.24 = (f32[32,256]{1,0:T(8,128)S(1)}, f32[32,256]{1,0:T(8,128)S(1)}, u32[]{:S(2)}, u32[]{:S(2)}) collective-permute-start(f32[32,256]{1,0:T(8,128)S(1)} %get-tuple-element.41), channel_id=1, source_target_pairs={{0,96},{1,97},{2,98},{3,99},{4,100},{5,101},{6,102},{7,103},{8,104... | collective-permute-start | bytes 98312 | tf_op jit(solution)/shard_map/ppermute | solution.py:37
  132.4 6.1 %collective-permute-start.25 = (f32[32,256]{1,0:T(8,128)S(1)}, f32[32,256]{1,0:T(8,128)S(1)}, u32[]{:S(2)}, u32[]{:S(2)}) collective-permute-start(f32[32,256]{1,0:T(8,128)S(1)} %get-tuple-element.42), channel_id=1, source_target_pairs={{0,16},{1,17},{2,18},{3,19},{4,20},{5,21},{6,22},{7,23},{8,24},{9,... | collective-permute-start | bytes 98312 | tf_op jit(solution)/shard_map/ppermute | solution.py:37
  133.4 6.1 %collective-permute-start.26 = (f32[32,256]{1,0:T(8,128)S(1)}, f32[32,256]{1,0:T(8,128)S(1)}, u32[]{:S(2)}, u32[]{:S(2)}) collective-permute-start(f32[32,256]{1,0:T(8,128)S(1)} %get-tuple-element.43), channel_id=1, source_target_pairs={{0,48},{1,49},{2,50},{3,51},{4,52},{5,53},{6,54},{7,55},{8,56},{9,... | collective-permute-start | bytes 98312 | tf_op jit(solution)/shard_map/ppermute | solution.py:37
  134.8 6.4 %collective-permute-start.27 = (f32[32,256]{1,0:T(8,128)S(1)}, f32[32,256]{1,0:T(8,128)S(1)}, u32[]{:S(2)}, u32[]{:S(2)}) collective-permute-start(f32[32,256]{1,0:T(8,128)S(1)} %get-tuple-element.44), channel_id=1, source_target_pairs={{0,80},{1,81},{2,82},{3,83},{4,84},{5,85},{6,86},{7,87},{8,88},{9,... | collective-permute-start | bytes 98312 | tf_op jit(solution)/shard_map/ppermute | solution.py:37
  135.8 5.4 %collective-permute-start.28 = (f32[32,256]{1,0:T(8,128)S(1)}, f32[32,256]{1,0:T(8,128)S(1)}, u32[]{:S(2)}, u32[]{:S(2)}) collective-permute-start(f32[32,256]{1,0:T(8,128)S(1)} %get-tuple-element.45), channel_id=1, source_target_pairs={{0,112},{1,113},{2,114},{3,115},{4,116},{5,117},{6,118},{7,119},{8... | collective-permute-start | bytes 98312 | tf_op jit(solution)/shard_map/ppermute | solution.py:37
  143.0 28.2 %all-to-all-start.2 = ((bf16[16,160,256]{2,1,0:T(8,128)(2,1)}), bf16[16,160,256]{2,1,0:T(8,128)(2,1)S(1)}, u32[]{:S(2)}, u32[]{:S(2)}) async-start(bf16[16,160,256]{2,1,0:T(8,128)(2,1)} %get-tuple-element.46), calls=%async_computation.2 | async-start | bytes 2621440 | tf_op jit(solution)/shard_map/all_to_all | solution.py:371
  151.3 19.9 %copy-start.5 = (bf16[1024,512]{1,0:T(8,128)(2,1)S(1)}, bf16[1024,512]{1,0:T(8,128)(2,1)}, u32[]{:S(2)}) copy-start(bf16[1024,512]{1,0:T(8,128)(2,1)} %factor.1) | copy-start | bytes 3145732
  151.3 19.9 %copy-start.26 = (s32[86]{0:T(128)S(1)}, s32[86]{0:T(128)}, u32[]{:S(2)}) copy-start(s32[86]{0:T(128)} %shard_map.128.tab) | copy-start | bytes 1036
  171.2 1.6 copy-start.1
  195.8 17.3 %copy-start.23 = (f32[256,512]{1,0:T(8,128)S(1)}, f32[256,512]{1,0:T(8,128)}, u32[]{:S(2)}) copy-start(f32[256,512]{1,0:T(8,128)} %dinv.1) | copy-start | bytes 1572868

commit v3 on v2

--- a/solution.py
+++ b/solution.py
@@ -65,37 +65,52 @@
 
 
 POS_AT = 0
-SLICE_AT = 32
-ROW_AT = 40
-PAR_AT = 52
-PICK_AT = 54
-TABLE = 86
+SLICE_AT = 64
+ROW_AT = 72
+PAR_AT = 88
+PICK_AT = 90
+CORE_AT = 122
+TABLE = 123
+LISTS = ((0, 16), (16, 32), (32, 40), (40, 48), (48, 56), (56, 64))
 
 
 def table_body(place, struct, select, parent, tab):
     row, col = place[0], place[1]
-    z, xh, core = col // 4, (col // 2) % 2, col % 2
-    y, xl = row // 2, row % 2
-    parents = [parent[2 * col], parent[2 * col + 1]]
-    blocks = [struct[col, n] for n in range(16)]
+    core = col & 1
+    y, xl = row >> 1, row & 1
+    sib = col ^ 1
+    blocks = [struct[col, n] for n in range(16)] + [struct[sib, n] for n in range(16)]
+    for where in (col, sib):
+        for e in range(2):
+            kid = 2 * where + e
+            home = parent[kid]
+            blocks += [struct[home, select[kid, n]] for n in range(8)]
     for e in range(2):
-        tab[PAR_AT + e] = parents[e]
-        blocks += [struct[parents[e], select[2 * col + e, n]] for n in range(8)]
+        tab[PAR_AT + e] = parent[2 * col + e]
     for n, block in enumerate(blocks):
-        home = block // 2
-        piece = ((home // 4) + 4 - z) % 4
-        piece += 4 * (((home // 2) % 2 + xh) % 2) + 8 * ((home % 2 + core) % 2)
-        tab[POS_AT + n] = 2 * piece + block % 2
+        home = block >> 1
+        apart = ((home >> 2) - (col >> 2)) & 3
+        other = (home ^ col) & 3
+        tab[POS_AT + n] = 4 * apart + 16 * (other >> 1) + 2 * (other & 1) + (block & 1)
+    for n in range(32):
+        index = n if n < 16 else n + 16
         group = 0 if n < 16 else (1 if n < 24 else 2)
-        tab[PICK_AT + n] = (block // 4) * 12 + group * 4 + block % 4
-    for group, (low, high) in enumerate(((0, 16), (16, 24), (24, 32))):
-        for rb in range(4):
-            found = jnp.int32(0)
-            for n in range(low, high):
-                found = found + (blocks[n] == 4 * row + rb).astype(jnp.int32)
-            tab[ROW_AT + 4 * group + rb] = found
+        block = blocks[index]
+        tab[PICK_AT + n] = (block >> 2) * 12 + group * 4 + (block & 3)
+    for n in range(ROW_AT, ROW_AT + 16):
+        tab[n] = 0
+    for group in range(4):
+        low, high = LISTS[group]
+        for n in range(low, high):
+            block = blocks[n]
+
+            @pl.when((block >> 2) == row)
+            def _():
+                tab[ROW_AT + 4 * group + (block & 3)] = 1
+
     for k in range(8):
-        tab[SLICE_AT + k] = ((y + k % 4) % 4) * 2 + (xl + k // 4) % 2
+        tab[SLICE_AT + k] = ((y + k) & 3) * 2 + (xl ^ (k // 4))
+    tab[CORE_AT] = core
 
 
 def build_body(one, zero, out):
@@ -112,22 +127,50 @@
         out[n] = spread[tab[PICK_AT + n]]
 
 
-def load(tab, inv_refs, low_refs, first, count, inv_s, low_s, inv_sem, low_sem):
+HALF = LOC // 2
+
+
+def collect_body(tab, *refs):
+    outs, sem = refs[8:10], refs[10]
     copies = []
-    for q, ref in enumerate(low_refs):
+    for q in range(8):
         at = pl.ds(pl.multiple_of(tab[SLICE_AT + q] * 32, 32), 32)
-        copies.append(
-            pltpu.make_async_copy(
-                ref.at[pl.ds(first, count)], low_s.at[:, at, :], low_sem.at[q]
-            )
-        )
-    for q, ref in enumerate(inv_refs):
-        for h in range(2):
+        for e in range(2):
             copies.append(
                 pltpu.make_async_copy(
-                    ref.at[:, pl.ds(h * B, B)], inv_s.at[2 * q + h], inv_sem.at[2 * q + h]
+                    refs[q].at[pl.ds(16 * e, 16)], outs[e].at[:, at, :], sem.at[2 * q + e]
                 )
             )
+    for copy in copies:
+        copy.start()
+    for copy in copies:
+        copy.wait()
+
+
+def collect(tab, pieces):
+    return call(
+        collect_body,
+        [jax.ShapeDtypeStruct((16, B, B), BF)] * 2,
+        [SMEM] + [HBM] * 8,
+        [pltpu.SemaphoreType.DMA((16,))],
+    )(tab, *pieces)
+
+
+def load(refs, groups, inv_s, low_s, inv_sem, low_sem):
+    copies = []
+    for g in range(groups):
+        copies.append(
+            pltpu.make_async_copy(refs[8 + g], low_s.at[pl.ds(16 * g, 16)], low_sem.at[g])
+        )
+    for q in range(8):
+        for d in range(2):
+            for h in range(2):
+                n = 4 * q + 2 * d + h
+                copies.append(
+                    pltpu.make_async_copy(
+                        refs[q].at[d, :, pl.ds(h * B, B)], inv_s.at[n], inv_sem.at[n]
+                    )
+                )
     for copy in copies:
         copy.start()
     return copies
@@ -140,88 +183,105 @@
     return total
 
 
-def kids_body(tab, *refs):
-    inv_refs, low_refs = refs[:16], refs[16:24]
-    part_ref, inv_s, low_s, inv_sem, low_sem = refs[24:]
-    copies = load(tab, inv_refs, low_refs, 16, 16, inv_s, low_s, inv_sem, low_sem)
-    part_ref[...] = jnp.zeros_like(part_ref)
-    for copy in copies:
-        copy.wait()
-
-    def step(n, carry):
-        cols = pl.ds(pl.multiple_of((n // 2) * B, B), B)
-        part_ref[:, cols] += product(tab, inv_s, low_s, 16, 4 * n)
-        return carry
-
-    lax.fori_loop(0, 4, step, 0)
-
-
-def level_one_body(tab, *refs):
-    inv_refs, low_refs = refs[:16], refs[16:24]
-    own_ref, up_ref = refs[24:26]
-    diag_refs = refs[26:34]
-    inv_s, low_s, acc, diag, inv_sem, low_sem = refs[34:]
-    copies = load(tab, inv_refs, low_refs, 0, 16, inv_s, low_s, inv_sem, low_sem)
+def level_one_body(group, tab, *refs):
+    rows_ref = refs[9]
+    if group == 0:
+        ups, diag_out = refs[10:12]
+        inv_s, low_s, acc, diag, inv_sem, low_sem = refs[12:]
+    else:
+        first_ups, ups, diag_out, up_spread = refs[10:14]
+        inv_s, low_s, acc, diag, inv_sem, low_sem = refs[14:]
+    copies = load(refs, 1, inv_s, low_s, inv_sem, low_sem)
     acc[...] = jnp.zeros_like(acc)
     diag[...] = jnp.zeros_like(diag)
     for copy in copies:
         copy.wait()
 
-    def own_step(n, carry):
-        acc[...] += product(tab, inv_s, low_s, 0, 4 * n)
+    def step(n, carry):
+        acc[...] += product(tab, inv_s, low_s, 16 * group, 4 * n)
         return carry
 
-    lax.fori_loop(0, 4, own_step, 0)
-    for rb in range(4):
-        rows = pl.ds(rb * B, B)
-        up_ref[rows, :] = jnp.zeros((B, B), BF)
-
-        @pl.when(tab[ROW_AT + rb] > 0)
+    lax.fori_loop(0, 4, step, 0)
+    for i in range(2):
+        rows = pl.ds(i * B, B)
+        ups[rows, :] = jnp.zeros((B, B), BF)
+
+        @pl.when(tab[ROW_AT + 4 * group + 2 * tab[CORE_AT] + i] > 0)
         def _():
             up = (-acc[rows, :]).astype(BF)
-            up_ref[rows, :] = up
-            diag[...] += dot_t(own_ref[rows, :], up)
-
+            ups[rows, :] = up
+            diag[...] += dot_t(rows_ref[rows, :], up)
+
+    if group == 1:
+        for j in range(16):
+            up_spread[j, 0] = first_ups[j * 32 : j * 32 + 32, :]
+            up_spread[j, 1] = ups[j * 32 : j * 32 + 32, :]
     for k in range(8):
         at = pl.ds(pl.multiple_of(tab[SLICE_AT + k] * 32, 32), 32)
-        diag_refs[k][...] = diag[at, :]
-
-
-def level_one(tab, inv_pieces, low_pieces, factor_one):
+        diag_out[k] = diag[at, :]
+
+
+def level_one(group, tab, pieces, low, rows, first_ups=None):
+    shapes = [jax.ShapeDtypeStruct((HALF, B), BF), jax.ShapeDtypeStruct((8, 32, B), F32)]
+    more = []
+    if group == 1:
+        shapes.append(jax.ShapeDtypeStruct((16, 2, 32, B), BF))
+        more = [first_ups]
+
+    def body(tab_ref, *refs):
+        level_one_body(group, tab_ref, *refs)
+
     return call(
-        level_one_body,
+        body,
+        shapes,
+        [SMEM] + [HBM] * 9 + [VMEM] * (1 + len(more)),
         [
-            jax.ShapeDtypeStruct((LOC, B), BF),
-        ]
-        + [jax.ShapeDtypeStruct((32, B), F32)] * 8,
-        [SMEM] + [HBM] * 24 + [VMEM],
-        [
-            pltpu.VMEM((32, LOC, B), BF),
+            pltpu.VMEM((32, HALF, B), BF),
             pltpu.VMEM((16, B, B), BF),
-            pltpu.VMEM((LOC, B), F32),
+            pltpu.VMEM((HALF, B), F32),
             pltpu.VMEM((B, B), F32),
             pltpu.SemaphoreType.DMA((32,)),
-            pltpu.SemaphoreType.DMA((8,)),
+            pltpu.SemaphoreType.DMA((1,)),
         ],
         limit=30,
-    )(tab, *inv_pieces, *low_pieces, factor_one)
-
-
-def kids(tab, inv_pieces, low_pieces):
+        flops=2 * HALF * 16 * B * B,
+        moved=12 * 2**20,
+    )(tab, *pieces, low, rows, *more)
+
+
+def kids_body(tab, *refs):
+    part_own, part_sib, inv_s, low_s, inv_sem, low_sem = refs[10:]
+    copies = load(refs, 2, inv_s, low_s, inv_sem, low_sem)
+    part_own[...] = jnp.zeros_like(part_own)
+    part_sib[...] = jnp.zeros_like(part_sib)
+    for copy in copies:
+        copy.wait()
+
+    for g, part in enumerate((part_own, part_sib)):
+
+        def step(n, carry):
+            cols = pl.ds(pl.multiple_of((n // 2) * B, B), B)
+            part[:, cols] += product(tab, inv_s, low_s.at[pl.ds(16 * g, 16)], 32 + 16 * g, 4 * n)
+            return carry
+
+        lax.fori_loop(0, 4, step, 0)
+
+
+def kids(tab, pieces):
     return call(
         kids_body,
-        jax.ShapeDtypeStruct((LOC, 2 * B), F32),
-        [SMEM] + [HBM] * 24,
+        [jax.ShapeDtypeStruct((HALF, 2 * B), F32)] * 2,
+        [SMEM] + [HBM] * 10,
         [
-            pltpu.VMEM((32, LOC, B), BF),
-            pltpu.VMEM((16, B, B), BF),
+            pltpu.VMEM((32, HALF, B), BF),
+            pltpu.VMEM((32, B, B), BF),
             pltpu.SemaphoreType.DMA((32,)),
-            pltpu.SemaphoreType.DMA((8,)),
+            pltpu.SemaphoreType.DMA((2,)),
         ],
         limit=56,
         flops=2 * LOC * 16 * B * B,
-        moved=24 * 2**20,
-    )(tab, *inv_pieces, *low_pieces)
+        moved=16 * 2**20,
+    )(tab, *pieces)
 
 
 def pack_body(parent, spread, dinv, *refs):
@@ -233,18 +293,22 @@
     diag[...] = value
     half = value.astype(BF)
     for j in range(16):
-        out[j, 0:64, :] = spread[parent[2 * j]]
-        out[j, 64:128, :] = spread[parent[2 * j + 1]]
+        for e in range(2):
+            home = parent[2 * j + e]
+            even, odd = (home // 2) * 2, home % 2
+            out[j, e * 64 : e * 64 + 32, :] = spread[even, odd]
+            out[j, e * 64 + 32 : e * 64 + 64, :] = spread[even + 1, 1 - odd]
         out[j, 128:160, :] = half
 
 
-def level_zero_body(tab, got, part, factor, link, up_ref, sums, both):
+def level_zero_body(tab, got, part_own, part_sib, factor, link, up_ref, sums, both):
     both[...] = jnp.zeros_like(both)
     for e in range(2):
         cols = pl.ds(e * B, B)
         for rb in range(4):
             rows = pl.ds(rb * B, B)
-            present = tab[ROW_AT + 4 * (e + 1) + rb] > 0
+            part_rows = pl.ds((rb % 2) * B, B)
+            present = tab[ROW_AT + 4 * (e + 2) + rb] > 0
 
             @pl.when(jnp.logical_not(present))
             def _():
@@ -252,9 +316,13 @@
 
             @pl.when(present)
             def _():
-                above = got[4 * rb : 4 * rb + 4, e * 64 : e * 64 + 64, :].reshape(B, B)
+                start, at = 8 * (rb % 2), e * 64 + 32 * (rb // 2)
+                above = got[start : start + 8, at : at + 32, :].reshape(B, B)
+                part = jnp.where(
+                    tab[CORE_AT] == rb // 2, part_own[part_rows, cols], part_sib[part_rows, cols]
+                )
                 low = factor[rows, cols]
-                total = part[rows, cols] + dot(above, link[:, cols])
+                total = part + dot(above, link[:, cols])
                 up = (-total).astype(BF)
                 up_ref[rows, cols] = up
                 both[0, :, cols] += dot_t(above, low)
@@ -323,46 +391,61 @@
     dinv_rows = lax.dynamic_slice_in_dim(dinv_one, row * 32, 32, 0)
 
     barrier = lax.optimization_barrier
-    below, above = send(inverse_anc, Z_UP), send(inverse_anc, Z_DOWN)
-    other = send(inverse_anc, X_HI)
+    core = col % 2
+    keep, give = core * HALF, (1 - core) * HALF
     spread_low = call(
         build_body, jax.ShapeDtypeStruct((8, 3, 4, 32, B), BF), [VMEM, VMEM]
     )(factor_one, factor_zero)
     spread_low = lax.all_to_all(spread_low, "prow", 0, 0)
 
-    own, below, above = barrier((inverse_anc, below, above))
+    own_rows = lax.dynamic_slice_in_dim(factor_one, keep, HALF, 0)
+    sib_rows = send(lax.dynamic_slice_in_dim(factor_one, give, HALF, 0), SIBLING)
+    own = jnp.stack(
+        [
+            lax.dynamic_slice_in_dim(inverse_anc, keep, HALF, 0),
+            send(lax.dynamic_slice_in_dim(inverse_anc, give, HALF, 0), SIBLING),
+        ]
+    )
+    own, tab = barrier((own, tab))
+    below, above = send(own, Z_UP), send(own, Z_DOWN)
+    other = send(own, X_HI)
+    own, spread_low, below, above, sib_rows = barrier((own, spread_low, below, above, sib_rows))
     far = send(below, Z_UP)
-    sib_own, sib_below, sib_above = send(own, SIBLING), send(below, SIBLING), send(above, SIBLING)
-
-    spread_low, other, sib_own, sib_below, sib_above = barrier(
-        (spread_low, other, sib_own, sib_below, sib_above)
-    )
-    other_above, other_below = send(other, Z_DOWN), send(other, Z_UP)
     mine = call(pick_body, jax.ShapeDtypeStruct((32, 32, B), BF), [SMEM, VMEM])(
         tab, spread_low.reshape(96, 32, B)
     )
     low_below, low_above = send(mine, Y_UP), send(mine, Y_DOWN)
     low_other = send(mine, X_LO)
+    low_far = send(low_below, Y_UP)
+    low_other_above = send(low_other, Y_DOWN)
+    low_other_below = send(low_other, Y_UP)
+    low_other_far = send(low_other_above, Y_DOWN)
+    other_above, other_below = send(other, Z_DOWN), send(other, Z_UP)
     other_far = send(far, X_HI)
-    sib_far, sib_other = send(far, SIBLING), send(other, SIBLING)
-    low_far = send(low_below, Y_UP)
-    low_other_above, low_other_below = send(low_other, Y_DOWN), send(low_other, Y_UP)
-    low_other_far = send(low_other_above, Y_DOWN)
-    sib_other_below, sib_other_above = send(other_below, SIBLING), send(other_above, SIBLING)
-    sib_other_far = send(other_far, SIBLING)
-    pieces = [own, above, far, below, other, other_above, other_far, other_below]
-    pieces += [sib_own, sib_above, sib_far, sib_below]
-    pieces += [sib_other, sib_other_above, sib_other_far, sib_other_below]
     low_pieces = [mine, low_above, low_far, low_below]
     low_pieces += [low_other, low_other_above, low_other_far, low_other_below]
-
-    upper_one, *diag_parts = level_one(tab, pieces, low_pieces, factor_one)
-    part = kids(tab, pieces, low_pieces)
-
-    spread = lax.all_to_all(upper_one.reshape(16, 64, B), "pcol", 0, 0)
+    low_one, low_zero = collect(tab, low_pieces)
+    low_one, low_zero, other_above, other_below, other_far = barrier(
+        (low_one, low_zero, other_above, other_below, other_far)
+    )
+    low_one_sib = send(low_one, SIBLING)
+    pieces = [own, above, far, below, other, other_above, other_far, other_below]
+
+    up_own, diag_own = level_one(0, tab, pieces, low_one, own_rows)
+    up_sib, diag_sib, up_spread = level_one(1, tab, pieces, low_one_sib, sib_rows, up_own)
+    spread = lax.all_to_all(up_spread, "pcol", 0, 0)
+    low_zero, up_spread2 = barrier((low_zero, up_spread))
+    low_zero_sib = send(low_zero, SIBLING)
+    diag_parts = diag_own + send(diag_sib, SIBLING)
     terms = [diag_parts[0]]
     for k in range(1, 8):
         terms.append(send(diag_parts[k], moves(dy=k % 4, dxl=k // 4)))
+    part_own, part_sib = kids(tab, pieces + [low_zero, low_zero_sib])
+    part_sib = send(part_sib, SIBLING)
+    up_sib = send(up_sib, SIBLING)
+    upper_one = jnp.zeros((LOC, B), BF)
+    upper_one = lax.dynamic_update_slice_in_dim(upper_one, up_own, keep, 0)
+    upper_one = lax.dynamic_update_slice_in_dim(upper_one, up_sib, give, 0)
     packed, diag_rows = call(
         pack_body,
         [jax.ShapeDtypeStruct((16, 160, B), BF), jax.ShapeDtypeStruct((32, B), F32)],
@@ -372,9 +455,9 @@
     upper_zero, sums = call(
         level_zero_body,
         [jax.ShapeDtypeStruct((LOC, 2 * B), BF), jax.ShapeDtypeStruct((8, 64, 2 * B), F32)],
-        [SMEM, VMEM, VMEM, VMEM, VMEM],
+        [SMEM] + [VMEM] * 5,
         [pltpu.VMEM((2, B, 2 * B), F32)],
-    )(tab, got, part, factor_zero, link)
+    )(tab, got, part_own, part_sib, factor_zero, link)
     sums = lax.all_to_all(sums, "prow", 0, 0)
     rows_out = call(
         parent_body,

time: 215 us -> 204 us (0.949)
  blocking collectives: 37.4 us -> 19.3 us
  starting transfers between devices: 50.8 us -> 60 us
  waiting for transfers between devices: 86.3 us -> 80.6 us
  Pallas kernels: 30.3 us -> 35.2 us
  local copies, waits for them, and re-layouts: 7.7 us -> 5.38 us
    ppermute x29 -> x28, waiting for transfers between devices: 78.2 us -> 46.5 us  [send(): return lax.ppermute(block, MESH_AXES, pairs)]
    all_to_all x1 -> x0, blocking collectives: 17.2 us -> none  [shards(): rows_in = lax.all_to_all(rows_out, 'prow', 0, 0)]
    all_to_all x1 -> x2, waiting for transfers between devices: 0.01 us -> 12.9 us  [the longest x1 12.8 us: shards(): rows_in = lax.all_to_all(rows_out, 'prow', 0, 0)]
    all_to_all x1, waiting for transfers between devices: 0.01 us -> 12.2 us  [shards(): spread_low = lax.all_to_all(spread_low, 'prow', 0, 0)]
    all_to_all x1 -> x2, starting transfers between devices: 3.59 us -> 10.6 us  [the longest x1 6.87 us: shards(): spread = lax.all_to_all(up_spread, 'pcol', 0, 0)]
    unnamed x59 -> x41, local copies, waits for them, and re-layouts: 6.73 us -> 2.87 us
    pallas_call x2 -> x4, Pallas kernels: 19.9 us -> 22.7 us  [the longest x1 10.3 us: kids(): call(kids_body, [jax.ShapeDtypeStruct((HALF, 2 * B), F32)] * 2, [SMEM] +...]
    ppermute x29 -> x28, starting transfers between devices: 34.4 us -> 36 us  [send(): return lax.ppermute(block, MESH_AXES, pairs)]
  transfers between devices with their start and end apart: 32 -> 32, of which waited for: 11 -> 14; matrix products, arithmetic and copies ran while one was open for 1% -> 2% of each run, Pallas kernels for 8% -> 12%
where the time goes in v3:
time: 204 us; the launch traced here: 203 us
  waiting for transfers between devices  80.6 us (40%)
  starting transfers between devices  60 us (29%)
  Pallas kernels  35.2 us (17%)
  blocking collectives  19.3 us (9%)
  local copies, waits for them, and re-layouts  5.38 us (3%)
    ppermute x28, waiting for transfers between devices, send(): return lax.ppermute(block, MESH_AXES, pairs)  46.5 us
    ppermute x28, starting transfers between devices, send(): return lax.ppermute(block, MESH_AXES, pairs)  36 us
    all_to_all x1, blocking collectives, shards(): sums = lax.all_to_all(sums, 'prow', 0, 0)  19.3 us
    all_to_all x1, waiting for transfers between devices, shards(): rows_in = lax.all_to_all(rows_out, 'prow', 0, 0)  12.8 us
    all_to_all x1, waiting for transfers between devices, shards(): spread_low = lax.all_to_all(spread_low, 'prow', 0, 0)  12.2 us
    pallas_call x1, Pallas kernels, kids(): call(kids_body, [jax.ShapeDtypeStruct((HALF, 2 * B), F32)] * 2, [SMEM] +...  10.3 us
    pallas_call x2, Pallas kernels, level_one(): call(body, shapes, [SMEM] + [HBM] * 9 + [VMEM] * (1 + len(more)), [pltpu....  10.1 us
    all_to_all x1, waiting for transfers between devices, shards(): got = lax.all_to_all(packed, 'pcol', 0, 0)  9.08 us
  transfers between devices with their start and end apart: 32, of which 14 were waited for; matrix products, arithmetic and copies ran while one was open for 2% of the time, Pallas kernels for 12%

profile of v3, /device:TPU:0, one launch (start us, length us, event | category | flops | bytes accessed | tf_op | source)
XLA Modules:
  0.0 203.2 jit_solution(10153989166267391081)
XLA Ops:
  0.6 0.0 copy-start
  0.7 1.4 dynamic-slice_bitcast_fusion
  2.1 0.1 collective-permute-start
  2.2 0.2 copy-done.7
  2.4 1.2 shard_map.129
  3.6 5.6 %all-to-all-start = ((bf16[8,3,4,32,256]{4,3,2,1,0:T(8,128)(2,1)}), bf16[8,3,4,32,256]{4,3,2,1,0:T(8,128)(2,1)}, u32[]{:S(2)}, u32[]{:S(2)}) async-start(bf16[8,3,4,32,256]{4,3,2,1,0:T(8,128)(2,1)} %shard_map.129), calls=%async_computation | async-start | bytes 3145728 | tf_op jit(solution)/shard_map/all_to_all | solution.py:399
  9.2 0.7 copy.14.select
  9.9 0.6 pad_add_fusion.place
  10.5 2.2 %shard_map.128.tab.tab_ref = s32[123]{0:T(128)} custom-call(s32[2]{0:T(128)} %pad_add_fusion.place, s32[16,16]{1,0:T(8,128)} %struct.1, s32[32,8]{1,0:T(8,128)} %copy.14.select, s32[32]{0:T(128)} %parent.3), custom_call_target="tpu_custom_call" | custom-call | tf_op jit(solution)/shard_map/pallas_call | solution.py:384
  12.7 0.1 pad_maximum_fusion.refs_0_
  12.8 2.0 collective-permute-start.1
  14.8 2.2 %collective-permute-start.2 = (bf16[2,512,512]{2,1,0:T(8,128)(2,1)S(1)}, bf16[2,512,512]{2,1,0:T(8,128)(2,1)}, u32[]{:S(2)}, u32[]{:S(2)}) collective-permute-start(bf16[2,512,512]{2,1,0:T(8,128)(2,1)S(1)} %pad_maximum_fusion.refs_0_), channel_id=1, source_target_pairs={{0,12},{1,13},{2,14},{3,15},{4,0},{5,1},{6,2},{7,3},{8,4},{9,5},{1... | collective-permute-start | bytes 3145736 | tf_op jit(solution)/shard_map/ppermute | solution.py:37
  17.0 0.1 collective-permute-start.3
  17.1 2.8 %collective-permute-start.5 = (bf16[2,512,512]{2,1,0:T(8,128)(2,1)S(1)}, bf16[2,512,512]{2,1,0:T(8,128)(2,1)}, u32[]{:S(2)}, u32[]{:S(2)}) collective-permute-start(bf16[2,512,512]{2,1,0:T(8,128)(2,1)S(1)} %pad_maximum_fusion.refs_0_), channel_id=1, source_target_pairs={{0,2},{1,3},{2,0},{3,1},{4,6},{5,7},{6,4},{7,5},{8,10},{9,11},{10,... | collective-permute-start | bytes 3145736 | tf_op jit(solution)/shard_map/ppermute | solution.py:37
  19.9 12.2 %all-to-all-done = bf16[8,3,4,32,256]{4,3,2,1,0:T(8,128)(2,1)} async-done(((bf16[8,3,4,32,256]{4,3,2,1,0:T(8,128)(2,1)}), bf16[8,3,4,32,256]{4,3,2,1,0:T(8,128)(2,1)}, u32[]{:S(2)}, u32[]{:S(2)}) %all-to-all-start) | async-done | bytes 1572896 | tf_op jit(solution)/shard_map/all_to_all | solution.py:399
  32.1 8.2 %collective-permute-done.1.refs_3_ = bf16[2,512,512]{2,1,0:T(8,128)(2,1)S(1)} collective-permute-done((bf16[2,512,512]{2,1,0:T(8,128)(2,1)S(1)}, bf16[2,512,512]{2,1,0:T(8,128)(2,1)S(1)}, u32[]{:S(2)}, u32[]{:S(2)}) %collective-permute-start.1) | collective-permute-done | bytes 1048608 | tf_op jit(solution)/shard_map/ppermute | solution.py:37
  40.3 1.4 collective-permute-start.4
  41.6 1.5 shard_map.130.refs_0_
  43.1 1.8 collective-permute-start.9
  44.9 1.5 collective-permute-start.7
  46.4 1.8 collective-permute-start.6
  48.1 15.4 %collective-permute-done.9.refs_4_ = bf16[32,32,256]{2,1,0:T(8,128)(2,1)S(1)} collective-permute-done((bf16[32,32,256]{2,1,0:T(8,128)(2,1)S(1)}, bf16[32,32,256]{2,1,0:T(8,128)(2,1)S(1)}, u32[]{:S(2)}, u32[]{:S(2)}) %collective-permute-start.9) | collective-permute-done | bytes 524320 | tf_op jit(solution)/shard_map/ppermute | solution.py:37
  63.6 1.8 collective-permute-start.10
  65.3 0.2 collective-permute-start.12
  65.6 4.0 %collective-permute-start.13 = (bf16[2,512,512]{2,1,0:T(8,128)(2,1)}, bf16[2,512,512]{2,1,0:T(8,128)(2,1)S(1)}, u32[]{:S(2)}, u32[]{:S(2)}) collective-permute-start(bf16[2,512,512]{2,1,0:T(8,128)(2,1)} %collective-permute-done.5.refs_4_), channel_id=1, source_target_pairs={{0,12},{1,13},{2,14},{3,15},{4,0},{5,1},{6,2},{7,3},{8,4},{9,5},{1... | collective-permute-start | bytes 3145736 | tf_op jit(solution)/shard_map/ppermute | solution.py:37
  69.7 2.8 %collective-permute-start.15 = (bf16[2,512,512]{2,1,0:T(8,128)(2,1)S(1)}, bf16[2,512,512]{2,1,0:T(8,128)(2,1)S(1)}, u32[]{:S(2)}, u32[]{:S(2)}) collective-permute-start(bf16[2,512,512]{2,1,0:T(8,128)(2,1)S(1)} %collective-permute-done.4.refs_2_), channel_id=1, source_target_pairs={{0,2},{1,3},{2,0},{3,1},{4,6},{5,7},{6,4},{7,5},{8,10},{9,11},{10,... | collective-permute-start | bytes 3145736 | tf_op jit(solution)/shard_map/ppermute | solution.py:37
  72.5 4.1 %collective-permute-done.10.refs_5_ = bf16[32,32,256]{2,1,0:T(8,128)(2,1)S(1)} collective-permute-done((bf16[32,32,256]{2,1,0:T(8,128)(2,1)S(1)}, bf16[32,32,256]{2,1,0:T(8,128)(2,1)S(1)}, u32[]{:S(2)}, u32[]{:S(2)}) %collective-permute-start.10) | collective-permute-done | bytes 524320 | tf_op jit(solution)/shard_map/ppermute | solution.py:37
  76.6 0.9 collective-permute-start.8
  77.5 2.4 %collective-permute-done.12.refs_7_ = bf16[32,32,256]{2,1,0:T(8,128)(2,1)S(1)} collective-permute-done((bf16[32,32,256]{2,1,0:T(8,128)(2,1)S(1)}, bf16[32,32,256]{2,1,0:T(8,128)(2,1)S(1)}, u32[]{:S(2)}, u32[]{:S(2)}) %collective-permute-start.12) | collective-permute-done | bytes 524320 | tf_op jit(solution)/shard_map/ppermute | solution.py:37
  79.8 10.7 %collective-permute-done.8.refs_2_ = bf16[32,32,256]{2,1,0:T(8,128)(2,1)S(1)} collective-permute-done((bf16[32,32,256]{2,1,0:T(8,128)(2,1)S(1)}, bf16[32,32,256]{2,1,0:T(8,128)(2,1)S(1)}, u32[]{:S(2)}, u32[]{:S(2)}) %collective-permute-start.8) | collective-permute-done | bytes 524320 | tf_op jit(solution)/shard_map/ppermute | solution.py:37
  90.5 0.6 collective-permute-done.11.refs_6_
  91.1 2.4 %shard_map.131 = (bf16[16,256,256]{2,1,0:T(8,128)(2,1)S(1)}, bf16[16,256,256]{2,1,0:T(8,128)(2,1)}) custom-call(s32[123]{0:T(128)S(1)} %copy-done.13, bf16[32,32,256]{2,1,0:T(8,128)(2,1)S(1)} %shard_map.130.refs_0_, bf16[32,32,256]{2,1,0:T(8,128)(2,1)S(1)} %collective-permute-done.6.refs_1_, bf16[32,32,256]{2,1,0:T(8,128)(2,1)S(1)} %collective-permute-done.8.refs_2_, ...), custom_call_target="tpu_custom_call" | custom-call | tf_op jit(solution)/shard_map/pallas_call | solution.py:151
  93.5 1.1 collective-permute-done.14.refs_7_
  94.6 0.2 collective-permute-done.15.refs_6_
  94.8 4.6 %shard_map.132 = (bf16[512,256]{1,0:T(8,128)(2,1)S(1)}, f32[8,32,256]{2,1,0:T(8,128)S(1)}) custom-call(s32[123]{0:T(128)S(1)} %copy-done.13, bf16[2,512,512]{2,1,0:T(8,128)(2,1)S(1)} %pad_maximum_fusion.refs_0_, bf16[2,512,512]{2,1,0:T(8,128)(2,1)} %collective-permute-done.2.refs_1_, bf16[2,512,512]{2,1,0:T(8,128)(2,1)S(1)} %collective-permute-done.4.refs_2_, ...), custom_call_target="tpu_custom_call" | custom-call | flops 1073741824 | bytes 12582912 | tf_op jit(solution)/shard_map/pallas_call | solution.py:234
  99.5 5.5 %shard_map.133 = (bf16[512,256]{1,0:T(8,128)(2,1)S(1)}, f32[8,32,256]{2,1,0:T(8,128)S(1)}, bf16[16,2,32,256]{3,2,1,0:T(8,128)(2,1)}) custom-call(s32[123]{0:T(128)S(1)} %copy-done.13, bf16[2,512,512]{2,1,0:T(8,128)(2,1)S(1)} %pad_maximum_fusion.refs_0_, bf16[2,512,512]{2,1,0:T(8,128)(2,1)} %collective-permute-done.2.refs_1_, ...), custom_call_target="tpu_custom_call" | custom-call | flops 1073741824 | bytes 12582912 | tf_op jit(solution)/shard_map/pallas_call | solution.py:234
  105.0 0.7 copy-done.16
  105.7 0.5 collective-permute-start.26
  106.2 6.9 %all-to-all-start.1 = ((bf16[16,2,32,256]{3,2,1,0:T(8,128)(2,1)}), bf16[16,2,32,256]{3,2,1,0:T(8,128)(2,1)S(1)}, u32[]{:S(2)}, u32[]{:S(2)}) async-start(bf16[16,2,32,256]{3,2,1,0:T(8,128)(2,1)} %get-tuple-element.49), calls=%async_computation.1 | async-start | bytes 1048576 | tf_op jit(solution)/shard_map/all_to_all | solution.py:436
  113.1 1.0 add.27
  114.1 0.5 collective-permute-start.19
  114.6 3.7 %collective-permute-start.20 = (f32[32,256]{1,0:T(8,128)S(1)}, f32[32,256]{1,0:T(8,128)S(1)}, u32[]{:S(2)}, u32[]{:S(2)}) collective-permute-start(f32[32,256]{1,0:T(8,128)S(1)} %get-tuple-element.72), channel_id=1, source_target_pairs={{0,64},{1,65},{2,66},{3,67},{4,68},{5,69},{6,70},{7,71},{8,72},{9,... | collective-permute-start | bytes 98312 | tf_op jit(solution)/shard_map/ppermute | solution.py:37
  118.3 1.1 collective-permute-start.21
  119.4 2.4 %collective-permute-start.23 = (f32[32,256]{1,0:T(8,128)S(1)}, f32[32,256]{1,0:T(8,128)S(1)}, u32[]{:S(2)}, u32[]{:S(2)}) collective-permute-start(f32[32,256]{1,0:T(8,128)S(1)} %get-tuple-element.69), channel_id=1, source_target_pairs={{0,48},{1,49},{2,50},{3,51},{4,52},{5,53},{6,54},{7,55},{8,56},{9,... | collective-permute-start | bytes 98312 | tf_op jit(solution)/shard_map/ppermute | solution.py:37
  121.8 1.6 collective-permute-start.24
  123.3 2.4 %collective-permute-start.25 = (f32[32,256]{1,0:T(8,128)S(1)}, f32[32,256]{1,0:T(8,128)S(1)}, u32[]{:S(2)}, u32[]{:S(2)}) collective-permute-start(f32[32,256]{1,0:T(8,128)S(1)} %get-tuple-element.67), channel_id=1, source_target_pairs={{0,112},{1,113},{2,114},{3,115},{4,116},{5,117},{6,118},{7,119},{8... | collective-permute-start | bytes 98312 | tf_op jit(solution)/shard_map/ppermute | solution.py:37
  125.7 2.4 %collective-permute-done.24.refs_6_ = f32[32,256]{1,0:T(8,128)S(1)} collective-permute-done((f32[32,256]{1,0:T(8,128)S(1)}, f32[32,256]{1,0:T(8,128)S(1)}, u32[]{:S(2)}, u32[]{:S(2)}) %collective-permute-start.24) | collective-permute-done | bytes 32800 | tf_op jit(solution)/shard_map/ppermute | solution.py:37
  128.1 0.1 collective-permute-done.25.refs_7_
  128.1 1.9 shard_map.134
  130.0 7.8 %all-to-all-start.2 = ((bf16[16,160,256]{2,1,0:T(8,128)(2,1)}), bf16[16,160,256]{2,1,0:T(8,128)(2,1)S(1)}, u32[]{:S(2)}, u32[]{:S(2)}) async-start(bf16[16,160,256]{2,1,0:T(8,128)(2,1)} %get-tuple-element.52), calls=%async_computation.2 | async-start | bytes 2621440 | tf_op jit(solution)/shard_map/all_to_all | solution.py:454
  137.9 10.3 %shard_map.135 = (f32[512,512]{1,0:T(8,128)}, f32[512,512]{1,0:T(8,128)}) custom-call(s32[123]{0:T(128)} %shard_map.128.tab.tab_ref, bf16[2,512,512]{2,1,0:T(8,128)(2,1)} %copy-done.1, bf16[2,512,512]{2,1,0:T(8,128)(2,1)} %collective-permute-done.2.refs_1_, bf16[2,512,512]{2,1,0:T(8,128)(2,1)} %copy-done.3, bf16[2,512,512]{2,1,0:T(8,128)(2,1)} %copy-done.2, ...), custom_call_target="tpu_custom_call" | custom-call | flops 2147483648 | bytes 16777216 | tf_op jit(solution)/shard_map/pallas_call | solution.py:271
  148.2 0.5 collective-permute-start.27
  148.7 1.0 constant_dynamic-slice_fusion.link
  149.7 9.1 %all-to-all-done.2.got = bf16[16,160,256]{2,1,0:T(8,128)(2,1)S(1)} async-done(((bf16[16,160,256]{2,1,0:T(8,128)(2,1)}), bf16[16,160,256]{2,1,0:T(8,128)(2,1)S(1)}, u32[]{:S(2)}, u32[]{:S(2)}) %all-to-all-start.2) | async-done | bytes 1310752 | tf_op jit(solution)/shard_map/all_to_all | solution.py:454
  158.8 1.2 copy-done.10
  160.0 2.8 %shard_map.136 = (bf16[1024,512]{1,0:T(8,128)(2,1)}, f32[8,64,512]{2,1,0:T(8,128)S(1)}) custom-call(s32[123]{0:T(128)S(1)} %copy-done.14, bf16[16,160,256]{2,1,0:T(8,128)(2,1)S(1)} %all-to-all-done.2.got, f32[512,512]{1,0:T(8,128)S(1)} %copy-done.10, f32[512,512]{1,0:T(8,128)} %collective-permute-done.27.part_sib, bf16[1024,512]{1,0:T(8,128)(2,1)S(1)} %copy-done.8, ...), custom_call_target="tpu_custom_call" | custom-call | tf_op jit(solution)/shard_map/pallas_call | solution.py:455
  162.8 19.3 %all_to_all.25.sums = f32[8,64,512]{2,1,0:T(8,128)S(1)} all-to-all(f32[8,64,512]{2,1,0:T(8,128)S(1)} %get-tuple-element.57), channel_id=1, replica_groups=mesh['prow'=8,'pcol'=16] {'prow'}, dimensions={0} | all-to-all | bytes 2097152 | tf_op jit(solution)/shard_map/all_to_all | solution.py:461
  182.1 1.7 shard_map.137
  183.8 3.7 %all-to-all-start.4 = ((bf16[8,128,512]{2,1,0:T(8,128)(2,1)}), bf16[8,128,512]{2,1,0:T(8,128)(2,1)S(1)}, u32[]{:S(2)}, u32[]{:S(2)}) async-start(bf16[8,128,512]{2,1,0:T(8,128)(2,1)} %shard_map.137), calls=%async_computation.4 | async-start | bytes 2097152 | tf_op jit(solution)/shard_map/all_to_all | solution.py:467
  187.5 0.1 collective-permute-start.17
  187.7 1.4 collective-permute-done.17
  189.2 0.0 copy-start.18
  189.2 12.8 %all-to-all-done.4.got = bf16[8,128,512]{2,1,0:T(8,128)(2,1)S(1)} async-done(((bf16[8,128,512]{2,1,0:T(8,128)(2,1)}), bf16[8,128,512]{2,1,0:T(8,128)(2,1)S(1)}, u32[]{:S(2)}, u32[]{:S(2)}) %all-to-all-start.4) | async-done | bytes 1048608 | tf_op jit(solution)/shard_map/all_to_all | solution.py:467
  202.0 1.2 shard_map.138
  (64 shorter events, 0.3 us)
Async XLA Ops:
  0.6 125.1 %copy-start = (f32[256,256]{1,0:T(8,128)S(1)}, f32[256,256]{1,0:T(8,128)}, u32[]{:S(2)}) copy-start(f32[256,256]{1,0:T(8,128)} %param.13) | copy-start | bytes 786436
  0.6 1.5 copy-start.9
  0.7 1.7 copy-start.7
  2.1 10.6 %collective-permute-start = (bf16[512,512]{1,0:T(8,128)(2,1)S(1)}, bf16[512,512]{1,0:T(8,128)(2,1)S(1)}, u32[]{:S(2)}, u32[]{:S(2)}) collective-permute-start(bf16[512,512]{1,0:T(8,128)(2,1)S(1)} %get-tuple-element.64), channel_id=1, source_target_pairs={{0,1},{1,0},{2,3},{3,2},{4,5},{5,4},{6,7},{7,6},{8,9},{9,8},{10,11... | collective-permute-start | bytes 1572872 | tf_op jit(solution)/shard_map/ppermute | solution.py:37
  3.6 5.6 %copy-start.19 = (s32[32,8]{0,1:T(8,128)S(1)}, s32[32,8]{0,1:T(8,128)}, u32[]{:S(2)}) copy-start(s32[32,8]{0,1:T(8,128)} %param.16) | copy-start | bytes 3076
  3.6 28.5 %all-to-all-start = ((bf16[8,3,4,32,256]{4,3,2,1,0:T(8,128)(2,1)}), bf16[8,3,4,32,256]{4,3,2,1,0:T(8,128)(2,1)}, u32[]{:S(2)}, u32[]{:S(2)}) async-start(bf16[8,3,4,32,256]{4,3,2,1,0:T(8,128)(2,1)} %shard_map.129), calls=%async_computation | async-start | bytes 3145728 | tf_op jit(solution)/shard_map/all_to_all | solution.py:399
  12.7 29.0 %copy-start.13 = (s32[123]{0:T(128)S(1)}, s32[123]{0:T(128)}, u32[]{:S(2)}) copy-start(s32[123]{0:T(128)} %shard_map.128.tab.tab_ref) | copy-start | bytes 1480
  12.8 86.6 %copy-start.1 = (bf16[2,512,512]{2,1,0:T(8,128)(2,1)}, bf16[2,512,512]{2,1,0:T(8,128)(2,1)S(1)}, u32[]{:S(2)}) copy-start(bf16[2,512,512]{2,1,0:T(8,128)(2,1)S(1)} %pad_maximum_fusion.refs_0_) | copy-start | bytes 3145732
  12.8 27.5 %collective-permute-start.1 = (bf16[2,512,512]{2,1,0:T(8,128)(2,1)S(1)}, bf16[2,512,512]{2,1,0:T(8,128)(2,1)S(1)}, u32[]{:S(2)}, u32[]{:S(2)}) collective-permute-start(bf16[2,512,512]{2,1,0:T(8,128)(2,1)S(1)} %pad_maximum_fusion.refs_0_), channel_id=1, source_target_pairs={{0,4},{1,5},{2,6},{3,7},{4,8},{5,9},{6,10},{7,11},{8,12},{9,13},{1... | collective-permute-start | bytes 3145736 | tf_op jit(solution)/shard_map/ppermute | solution.py:37
  14.8 25.5 %collective-permute-start.2 = (bf16[2,512,512]{2,1,0:T(8,128)(2,1)S(1)}, bf16[2,512,512]{2,1,0:T(8,128)(2,1)}, u32[]{:S(2)}, u32[]{:S(2)}) collective-permute-start(bf16[2,512,512]{2,1,0:T(8,128)(2,1)S(1)} %pad_maximum_fusion.refs_0_), channel_id=1, source_target_pairs={{0,12},{1,13},{2,14},{3,15},{4,0},{5,1},{6,2},{7,3},{8,4},{9,5},{1... | collective-permute-start | bytes 3145736 | tf_op jit(solution)/shard_map/ppermute | solution.py:37
  17.0 2.9 %collective-permute-start.3 = (bf16[512,256]{1,0:T(8,128)(2,1)S(1)}, bf16[512,256]{1,0:T(8,128)(2,1)S(1)}, u32[]{:S(2)}, u32[]{:S(2)}) collective-permute-start(bf16[512,256]{1,0:T(8,128)(2,1)S(1)} %get-tuple-element.66), channel_id=1, source_target_pairs={{0,1},{1,0},{2,3},{3,2},{4,5},{5,4},{6,7},{7,6},{8,9},{9,8},{10,11... | collective-permute-start | bytes 786440 | tf_op jit(solution)/shard_map/ppermute | solution.py:37
  17.1 48.2 %collective-permute-start.5 = (bf16[2,512,512]{2,1,0:T(8,128)(2,1)S(1)}, bf16[2,512,512]{2,1,0:T(8,128)(2,1)}, u32[]{:S(2)}, u32[]{:S(2)}) collective-permute-start(bf16[2,512,512]{2,1,0:T(8,128)(2,1)S(1)} %pad_maximum_fusion.refs_0_), channel_id=1, source_target_pairs={{0,2},{1,3},{2,0},{3,1},{4,6},{5,7},{6,4},{7,5},{8,10},{9,11},{10,... | collective-permute-start | bytes 3145736 | tf_op jit(solution)/shard_map/ppermute | solution.py:37
  40.3 59.2 %copy-start.2 = (bf16[2,512,512]{2,1,0:T(8,128)(2,1)}, bf16[2,512,512]{2,1,0:T(8,128)(2,1)S(1)}, u32[]{:S(2)}) copy-start(bf16[2,512,512]{2,1,0:T(8,128)(2,1)S(1)} %collective-permute-done.1.refs_3_) | copy-start | bytes 3145732
  40.3 29.4 %collective-permute-start.4 = (bf16[2,512,512]{2,1,0:T(8,128)(2,1)S(1)}, bf16[2,512,512]{2,1,0:T(8,128)(2,1)S(1)}, u32[]{:S(2)}, u32[]{:S(2)}) collective-permute-start(bf16[2,512,512]{2,1,0:T(8,128)(2,1)S(1)} %collective-permute-done.1.refs_3_), channel_id=1, source_target_pairs={{0,4},{1,5},{2,6},{3,7},{4,8},{5,9},{6,10},{7,11},{8,12},{9,13},{1... | collective-permute-start | bytes 3145736 | tf_op jit(solution)/shard_map/ppermute | solution.py:37
  43.1 20.5 %collective-permute-start.9 = (bf16[32,32,256]{2,1,0:T(8,128)(2,1)S(1)}, bf16[32,32,256]{2,1,0:T(8,128)(2,1)S(1)}, u32[]{:S(2)}, u32[]{:S(2)}) collective-permute-start(bf16[32,32,256]{2,1,0:T(8,128)(2,1)S(1)} %shard_map.130.refs_0_), channel_id=1, source_target_pairs={{0,16},{1,17},{2,18},{3,19},{4,20},{5,21},{6,22},{7,23},{8,24},{9,... | collective-permute-start | bytes 1572872 | tf_op jit(solution)/shard_map/ppermute | solution.py:37
  44.9 20.7 %collective-permute-start.7 = (bf16[32,32,256]{2,1,0:T(8,128)(2,1)S(1)}, bf16[32,32,256]{2,1,0:T(8,128)(2,1)S(1)}, u32[]{:S(2)}, u32[]{:S(2)}) collective-permute-start(bf16[32,32,256]{2,1,0:T(8,128)(2,1)S(1)} %shard_map.130.refs_0_), channel_id=1, source_target_pairs={{0,32},{1,33},{2,34},{3,35},{4,36},{5,37},{6,38},{7,39},{8,40},{9,... | collective-permute-start | bytes 1572872 | tf_op jit(solution)/shard_map/ppermute | solution.py:37
  46.4 23.3 %collective-permute-start.6 = (bf16[32,32,256]{2,1,0:T(8,128)(2,1)S(1)}, bf16[32,32,256]{2,1,0:T(8,128)(2,1)S(1)}, u32[]{:S(2)}, u32[]{:S(2)}) collective-permute-start(bf16[32,32,256]{2,1,0:T(8,128)(2,1)S(1)} %shard_map.130.refs_0_), channel_id=1, source_target_pairs={{0,96},{1,97},{2,98},{3,99},{4,100},{5,101},{6,102},{7,103},{8,104... | collective-permute-start | bytes 1572872 | tf_op jit(solution)/shard_map/ppermute | solution.py:37
  63.6 13.0 %collective-permute-start.10 = (bf16[32,32,256]{2,1,0:T(8,128)(2,1)S(1)}, bf16[32,32,256]{2,1,0:T(8,128)(2,1)S(1)}, u32[]{:S(2)}, u32[]{:S(2)}) collective-permute-start(bf16[32,32,256]{2,1,0:T(8,128)(2,1)S(1)} %collective-permute-done.9.refs_4_), channel_id=1, source_target_pairs={{0,96},{1,97},{2,98},{3,99},{4,100},{5,101},{6,102},{7,103},{8,104... | collective-permute-start | bytes 1572872 | tf_op jit(solution)/shard_map/ppermute | solution.py:37
  65.3 14.5 %collective-permute-start.12 = (bf16[32,32,256]{2,1,0:T(8,128)(2,1)S(1)}, bf16[32,32,256]{2,1,0:T(8,128)(2,1)S(1)}, u32[]{:S(2)}, u32[]{:S(2)}) collective-permute-start(bf16[32,32,256]{2,1,0:T(8,128)(2,1)S(1)} %collective-permute-done.9.refs_4_), channel_id=1, source_target_pairs={{0,32},{1,33},{2,34},{3,35},{4,36},{5,37},{6,38},{7,39},{8,40},{9,... | collective-permute-start | bytes 1572872 | tf_op jit(solution)/shard_map/ppermute | solution.py:37
  65.6 27.9 %collective-permute-start.13 = (bf16[2,512,512]{2,1,0:T(8,128)(2,1)}, bf16[2,512,512]{2,1,0:T(8,128)(2,1)S(1)}, u32[]{:S(2)}, u32[]{:S(2)}) collective-permute-start(bf16[2,512,512]{2,1,0:T(8,128)(2,1)} %collective-permute-done.5.refs_4_), channel_id=1, source_target_pairs={{0,12},{1,13},{2,14},{3,15},{4,0},{5,1},{6,2},{7,3},{8,4},{9,5},{1... | collective-permute-start | bytes 3145736 | tf_op jit(solution)/shard_map/ppermute | solution.py:37
  69.6 24.9 %collective-permute-start.14 = (bf16[2,512,512]{2,1,0:T(8,128)(2,1)}, bf16[2,512,512]{2,1,0:T(8,128)(2,1)S(1)}, u32[]{:S(2)}, u32[]{:S(2)}) collective-permute-start(bf16[2,512,512]{2,1,0:T(8,128)(2,1)} %collective-permute-done.5.refs_4_), channel_id=1, source_target_pairs={{0,4},{1,5},{2,6},{3,7},{4,8},{5,9},{6,10},{7,11},{8,12},{9,13},{1... | collective-permute-start | bytes 3145736 | tf_op jit(solution)/shard_map/ppermute | solution.py:37
  69.6 29.8 %copy-start.3 = (bf16[2,512,512]{2,1,0:T(8,128)(2,1)}, bf16[2,512,512]{2,1,0:T(8,128)(2,1)S(1)}, u32[]{:S(2)}) copy-start(bf16[2,512,512]{2,1,0:T(8,128)(2,1)S(1)} %collective-permute-done.4.refs_2_) | copy-start | bytes 3145732
  69.7 25.1 %collective-permute-start.15 = (bf16[2,512,512]{2,1,0:T(8,128)(2,1)S(1)}, bf16[2,512,512]{2,1,0:T(8,128)(2,1)S(1)}, u32[]{:S(2)}, u32[]{:S(2)}) collective-permute-start(bf16[2,512,512]{2,1,0:T(8,128)(2,1)S(1)} %collective-permute-done.4.refs_2_), channel_id=1, source_target_pairs={{0,2},{1,3},{2,0},{3,1},{4,6},{5,7},{6,4},{7,5},{8,10},{9,11},{10,... | collective-permute-start | bytes 3145736 | tf_op jit(solution)/shard_map/ppermute | solution.py:37
  76.6 13.9 %collective-permute-start.8 = (bf16[32,32,256]{2,1,0:T(8,128)(2,1)S(1)}, bf16[32,32,256]{2,1,0:T(8,128)(2,1)S(1)}, u32[]{:S(2)}, u32[]{:S(2)}) collective-permute-start(bf16[32,32,256]{2,1,0:T(8,128)(2,1)S(1)} %collective-permute-done.7.refs_3_), channel_id=1, source_target_pairs={{0,32},{1,33},{2,34},{3,35},{4,36},{5,37},{6,38},{7,39},{8,40},{9,... | collective-permute-start | bytes 1572872 | tf_op jit(solution)/shard_map/ppermute | solution.py:37
  79.8 11.3 %collective-permute-start.11 = (bf16[32,32,256]{2,1,0:T(8,128)(2,1)S(1)}, bf16[32,32,256]{2,1,0:T(8,128)(2,1)S(1)}, u32[]{:S(2)}, u32[]{:S(2)}) collective-permute-start(bf16[32,32,256]{2,1,0:T(8,128)(2,1)S(1)} %collective-permute-done.10.refs_5_), channel_id=1, source_target_pairs={{0,96},{1,97},{2,98},{3,99},{4,100},{5,101},{6,102},{7,103},{8,104... | collective-permute-start | bytes 1572872 | tf_op jit(solution)/shard_map/ppermute | solution.py:37
  93.5 6.0 %copy-start.4 = (bf16[2,512,512]{2,1,0:T(8,128)(2,1)}, bf16[2,512,512]{2,1,0:T(8,128)(2,1)S(1)}, u32[]{:S(2)}) copy-start(bf16[2,512,512]{2,1,0:T(8,128)(2,1)S(1)} %collective-permute-done.13.refs_5_) | copy-start | bytes 3145732
  94.6 4.9 %copy-start.5 = (bf16[2,512,512]{2,1,0:T(8,128)(2,1)}, bf16[2,512,512]{2,1,0:T(8,128)(2,1)S(1)}, u32[]{:S(2)}) copy-start(bf16[2,512,512]{2,1,0:T(8,128)(2,1)S(1)} %collective-permute-done.14.refs_7_) | copy-start | bytes 3145732
  94.7 4.7 %copy-start.6 = (bf16[2,512,512]{2,1,0:T(8,128)(2,1)}, bf16[2,512,512]{2,1,0:T(8,128)(2,1)S(1)}, u32[]{:S(2)}) copy-start(bf16[2,512,512]{2,1,0:T(8,128)(2,1)S(1)} %collective-permute-done.15.refs_6_) | copy-start | bytes 3145732
  94.7 4.7 %collective-permute-start.16 = (bf16[16,256,256]{2,1,0:T(8,128)(2,1)S(1)}, bf16[16,256,256]{2,1,0:T(8,128)(2,1)S(1)}, u32[]{:S(2)}, u32[]{:S(2)}) collective-permute-start(bf16[16,256,256]{2,1,0:T(8,128)(2,1)S(1)} %get-tuple-element.45.refs_8_), channel_id=1, source_target_pairs={{0,1},{1,0},{2,3},{3,2},{4,5},{5,4},{6,7},{7,6},{8,9},{9,8},{10,11... | collective-permute-start | bytes 6291464 | tf_op jit(solution)/shard_map/ppermute | solution.py:37
  99.4 5.5 %copy-start.12 = (f32[8,32,256]{2,1,0:T(8,128)}, f32[8,32,256]{2,1,0:T(8,128)S(1)}, u32[]{:S(2)}) copy-start(f32[8,32,256]{2,1,0:T(8,128)S(1)} %get-tuple-element.50) | copy-start | bytes 786436
  104.9 0.7 copy-start.16
  105.7 22.5 %copy-start.15 = (s32[32]{0:T(128)S(1)}, s32[32]{0:T(128)}, u32[]{:S(2)}) copy-start(s32[32]{0:T(128)} %parent.3) | copy-start | bytes 388
  105.7 32.2 %collective-permute-start.26 = (bf16[16,256,256]{2,1,0:T(8,128)(2,1)}, bf16[16,256,256]{2,1,0:T(8,128)(2,1)}, u32[]{:S(2)}, u32[]{:S(2)}) collective-permute-start(bf16[16,256,256]{2,1,0:T(8,128)(2,1)} %get-tuple-element.54.refs_8_), channel_id=1, source_target_pairs={{0,1},{1,0},{2,3},{3,2},{4,5},{5,4},{6,7},{7,6},{8,9},{9,8},{10,11... | collective-permute-start | bytes 6291464 | tf_op jit(solution)/shard_map/ppermute | solution.py:37
  106.2 6.9 %collective-permute-start.18 = (f32[8,32,256]{2,1,0:T(8,128)S(1)}, f32[8,32,256]{2,1,0:T(8,128)S(1)}, u32[]{:S(2)}, u32[]{:S(2)}) collective-permute-start(f32[8,32,256]{2,1,0:T(8,128)S(1)} %get-tuple-element.51), channel_id=1, source_target_pairs={{0,1},{1,0},{2,3},{3,2},{4,5},{5,4},{6,7},{7,6},{8,9},{9,8},{10,11... | collective-permute-start | bytes 786440 | tf_op jit(solution)/shard_map/ppermute | solution.py:37
  106.2 22.0 %all-to-all-start.1 = ((bf16[16,2,32,256]{3,2,1,0:T(8,128)(2,1)}), bf16[16,2,32,256]{3,2,1,0:T(8,128)(2,1)S(1)}, u32[]{:S(2)}, u32[]{:S(2)}) async-start(bf16[16,2,32,256]{3,2,1,0:T(8,128)(2,1)} %get-tuple-element.49), calls=%async_computation.1 | async-start | bytes 1048576 | tf_op jit(solution)/shard_map/all_to_all | solution.py:436
  114.1 5.3 %collective-permute-start.19 = (f32[32,256]{1,0:T(8,128)S(1)}, f32[32,256]{1,0:T(8,128)S(1)}, u32[]{:S(2)}, u32[]{:S(2)}) collective-permute-start(f32[32,256]{1,0:T(8,128)S(1)} %get-tuple-element.73), channel_id=1, source_target_pairs={{0,32},{1,33},{2,34},{3,35},{4,36},{5,37},{6,38},{7,39},{8,40},{9,... | collective-permute-start | bytes 98312 | tf_op jit(solution)/shard_map/ppermute | solution.py:37
  114.6 7.2 %collective-permute-start.20 = (f32[32,256]{1,0:T(8,128)S(1)}, f32[32,256]{1,0:T(8,128)S(1)}, u32[]{:S(2)}, u32[]{:S(2)}) collective-permute-start(f32[32,256]{1,0:T(8,128)S(1)} %get-tuple-element.72), channel_id=1, source_target_pairs={{0,64},{1,65},{2,66},{3,67},{4,68},{5,69},{6,70},{7,71},{8,72},{9,... | collective-permute-start | bytes 98312 | tf_op jit(solution)/shard_map/ppermute | solution.py:37
  118.3 5.1 %collective-permute-start.21 = (f32[32,256]{1,0:T(8,128)S(1)}, f32[32,256]{1,0:T(8,128)S(1)}, u32[]{:S(2)}, u32[]{:S(2)}) collective-permute-start(f32[32,256]{1,0:T(8,128)S(1)} %get-tuple-element.71), channel_id=1, source_target_pairs={{0,96},{1,97},{2,98},{3,99},{4,100},{5,101},{6,102},{7,103},{8,104... | collective-permute-start | bytes 98312 | tf_op jit(solution)/shard_map/ppermute | solution.py:37
  119.3 6.4 %collective-permute-start.22 = (f32[32,256]{1,0:T(8,128)S(1)}, f32[32,256]{1,0:T(8,128)S(1)}, u32[]{:S(2)}, u32[]{:S(2)}) collective-permute-start(f32[32,256]{1,0:T(8,128)S(1)} %get-tuple-element.70), channel_id=1, source_target_pairs={{0,16},{1,17},{2,18},{3,19},{4,20},{5,21},{6,22},{7,23},{8,24},{9,... | collective-permute-start | bytes 98312 | tf_op jit(solution)/shard_map/ppermute | solution.py:37
  119.4 6.4 %collective-permute-start.23 = (f32[32,256]{1,0:T(8,128)S(1)}, f32[32,256]{1,0:T(8,128)S(1)}, u32[]{:S(2)}, u32[]{:S(2)}) collective-permute-start(f32[32,256]{1,0:T(8,128)S(1)} %get-tuple-element.69), channel_id=1, source_target_pairs={{0,48},{1,49},{2,50},{3,51},{4,52},{5,53},{6,54},{7,55},{8,56},{9,... | collective-permute-start | bytes 98312 | tf_op jit(solution)/shard_map/ppermute | solution.py:37
  121.8 6.3 %collective-permute-start.24 = (f32[32,256]{1,0:T(8,128)S(1)}, f32[32,256]{1,0:T(8,128)S(1)}, u32[]{:S(2)}, u32[]{:S(2)}) collective-permute-start(f32[32,256]{1,0:T(8,128)S(1)} %get-tuple-element.68), channel_id=1, source_target_pairs={{0,80},{1,81},{2,82},{3,83},{4,84},{5,85},{6,86},{7,87},{8,88},{9,... | collective-permute-start | bytes 98312 | tf_op jit(solution)/shard_map/ppermute | solution.py:37
  123.3 4.8 %collective-permute-start.25 = (f32[32,256]{1,0:T(8,128)S(1)}, f32[32,256]{1,0:T(8,128)S(1)}, u32[]{:S(2)}, u32[]{:S(2)}) collective-permute-start(f32[32,256]{1,0:T(8,128)S(1)} %get-tuple-element.67), channel_id=1, source_target_pairs={{0,112},{1,113},{2,114},{3,115},{4,116},{5,117},{6,118},{7,119},{8... | collective-permute-start | bytes 98312 | tf_op jit(solution)/shard_map/ppermute | solution.py:37
  130.0 28.7 %all-to-all-start.2 = ((bf16[16,160,256]{2,1,0:T(8,128)(2,1)}), bf16[16,160,256]{2,1,0:T(8,128)(2,1)S(1)}, u32[]{:S(2)}, u32[]{:S(2)}) async-start(bf16[16,160,256]{2,1,0:T(8,128)(2,1)} %get-tuple-element.52), calls=%async_computation.2 | async-start | bytes 2621440 | tf_op jit(solution)/shard_map/all_to_all | solution.py:454
  137.9 20.9 %copy-start.8 = (bf16[1024,512]{1,0:T(8,128)(2,1)S(1)}, bf16[1024,512]{1,0:T(8,128)(2,1)}, u32[]{:S(2)}) copy-start(bf16[1024,512]{1,0:T(8,128)(2,1)} %factor.1) | copy-start | bytes 3145732
  137.9 20.9 %copy-start.14 = (s32[123]{0:T(128)S(1)}, s32[123]{0:T(128)}, u32[]{:S(2)}) copy-start(s32[123]{0:T(128)} %shard_map.128.tab.tab_ref) | copy-start | bytes 1480
  148.2 10.5 %collective-permute-start.27 = (f32[512,512]{1,0:T(8,128)}, f32[512,512]{1,0:T(8,128)}, u32[]{:S(2)}, u32[]{:S(2)}) collective-permute-start(f32[512,512]{1,0:T(8,128)} %get-tuple-element.56), channel_id=1, source_target_pairs={{0,1},{1,0},{2,3},{3,2},{4,5},{5,4},{6,7},{7,6},{8,9},{9,8},{10,11... | collective-permute-start | bytes 3145736 | tf_op jit(solution)/shard_map/ppermute | solution.py:37
  158.8 1.2 copy-start.10
  182.1 5.4 %copy-start.17 = (bf16[512,256]{1,0:T(8,128)(2,1)S(1)}, bf16[512,256]{1,0:T(8,128)(2,1)}, u32[]{:S(2)}) copy-start(bf16[512,256]{1,0:T(8,128)(2,1)} %copy-done.16) | copy-start | bytes 786436
  183.8 18.2 %copy-start.11 = (f32[256,512]{1,0:T(8,128)S(1)}, f32[256,512]{1,0:T(8,128)}, u32[]{:S(2)}) copy-start(f32[256,512]{1,0:T(8,128)} %dinv.1) | copy-start | bytes 1572868
  183.8 18.2 %all-to-all-start.4 = ((bf16[8,128,512]{2,1,0:T(8,128)(2,1)}), bf16[8,128,512]{2,1,0:T(8,128)(2,1)S(1)}, u32[]{:S(2)}, u32[]{:S(2)}) async-start(bf16[8,128,512]{2,1,0:T(8,128)(2,1)} %shard_map.137), calls=%async_computation.4 | async-start | bytes 2097152 | tf_op jit(solution)/shard_map/all_to_all | solution.py:467
  187.5 1.6 collective-permute-start.17
  189.2 14.0 %copy-start.18 = (bf16[1024,256]{1,0:T(8,128)(2,1)}, bf16[1024,256]{1,0:T(8,128)(2,1)S(1)}, u32[]{:S(2)}) copy-start(bf16[1024,256]{1,0:T(8,128)(2,1)S(1)} %constant_dynamic-update-slice_fusion) | copy-start | bytes 1572868

commit v4 on v3

--- a/solution.py
+++ b/solution.py
@@ -186,11 +186,11 @@
 def level_one_body(group, tab, *refs):
     rows_ref = refs[9]
     if group == 0:
-        ups, diag_out = refs[10:12]
-        inv_s, low_s, acc, diag, inv_sem, low_sem = refs[12:]
+        ups, near, away = refs[10:13]
+        inv_s, low_s, acc, diag, inv_sem, low_sem = refs[13:]
     else:
-        first_ups, ups, diag_out, up_spread = refs[10:14]
-        inv_s, low_s, acc, diag, inv_sem, low_sem = refs[14:]
+        first_ups, ups, near, away, up_spread = refs[10:15]
+        inv_s, low_s, acc, diag, inv_sem, low_sem = refs[15:]
     copies = load(refs, 1, inv_s, low_s, inv_sem, low_sem)
     acc[...] = jnp.zeros_like(acc)
     diag[...] = jnp.zeros_like(diag)
@@ -218,11 +218,12 @@
             up_spread[j, 1] = ups[j * 32 : j * 32 + 32, :]
     for k in range(8):
         at = pl.ds(pl.multiple_of(tab[SLICE_AT + k] * 32, 32), 32)
-        diag_out[k] = diag[at, :]
+        (near if k < 4 else away)[k % 4] = diag[at, :]
 
 
 def level_one(group, tab, pieces, low, rows, first_ups=None):
-    shapes = [jax.ShapeDtypeStruct((HALF, B), BF), jax.ShapeDtypeStruct((8, 32, B), F32)]
+    shapes = [jax.ShapeDtypeStruct((HALF, B), BF)]
+    shapes += [jax.ShapeDtypeStruct((4, 32, B), F32)] * 2
     more = []
     if group == 1:
         shapes.append(jax.ShapeDtypeStruct((16, 2, 32, B), BF))
@@ -285,9 +286,9 @@
 
 
 def pack_body(parent, spread, dinv, *refs):
-    terms, out, diag = refs[:8], refs[8], refs[9]
+    terms, out, diag = refs[:4], refs[4], refs[5]
     total = terms[0][...]
-    for i in range(1, 8):
+    for i in range(1, 4):
         total = total + terms[i][...]
     value = dinv[...] - total
     diag[...] = value
@@ -431,25 +432,26 @@
     low_one_sib = send(low_one, SIBLING)
     pieces = [own, above, far, below, other, other_above, other_far, other_below]
 
-    up_own, diag_own = level_one(0, tab, pieces, low_one, own_rows)
-    up_sib, diag_sib, up_spread = level_one(1, tab, pieces, low_one_sib, sib_rows, up_own)
+    up_own, near_own, away_own = level_one(0, tab, pieces, low_one, own_rows)
+    up_sib, near_sib, away_sib, up_spread = level_one(1, tab, pieces, low_one_sib, sib_rows, up_own)
     spread = lax.all_to_all(up_spread, "pcol", 0, 0)
     low_zero, up_spread2 = barrier((low_zero, up_spread))
     low_zero_sib = send(low_zero, SIBLING)
-    diag_parts = diag_own + send(diag_sib, SIBLING)
-    terms = [diag_parts[0]]
-    for k in range(1, 8):
-        terms.append(send(diag_parts[k], moves(dy=k % 4, dxl=k // 4)))
+    near = near_own + send(near_sib, SIBLING)
+    near = near + send(away_own, X_LO) + send(away_sib, moves(dxl=1, dcore=1))
+    terms = [near[0]]
+    for k in range(1, 4):
+        terms.append(send(near[k], moves(dy=k)))
     part_own, part_sib = kids(tab, pieces + [low_zero, low_zero_sib])
     part_sib = send(part_sib, SIBLING)
-    up_sib = send(up_sib, SIBLING)
+    up_sib, part_sib = lax.optimization_barrier((send(up_sib, SIBLING), part_sib))
     upper_one = jnp.zeros((LOC, B), BF)
     upper_one = lax.dynamic_update_slice_in_dim(upper_one, up_own, keep, 0)
     upper_one = lax.dynamic_update_slice_in_dim(upper_one, up_sib, give, 0)
     packed, diag_rows = call(
         pack_body,
         [jax.ShapeDtypeStruct((16, 160, B), BF), jax.ShapeDtypeStruct((32, B), F32)],
-        [SMEM] + [VMEM] * 10,
+        [SMEM] + [VMEM] * 6,
     )(parent, spread, dinv_rows, *terms)
     got = lax.all_to_all(packed, "pcol", 0, 0)
     upper_zero, sums = call(

time: 204 us -> 199 us (0.975)
  starting transfers between devices: 60 us -> 51.8 us
  waiting for transfers between devices: 80.6 us -> 83.5 us
    all_to_all x1, waiting for transfers between devices: 0.01 us -> 4.88 us  [shards(): spread = lax.all_to_all(up_spread, 'pcol', 0, 0)]
    all_to_all x1, starting transfers between devices: 7.82 us -> 3.7 us  [shards(): got = lax.all_to_all(packed, 'pcol', 0, 0)]
    ppermute x28 -> x26, starting transfers between devices: 36 us -> 32.2 us  [send(): return lax.ppermute(block, MESH_AXES, pairs)]
    ppermute x28 -> x26, waiting for transfers between devices: 46.5 us -> 45.7 us  [send(): return lax.ppermute(block, MESH_AXES, pairs)]
  transfers between devices with their start and end apart: 32 -> 30, of which waited for: 14 -> 16; matrix products, arithmetic and copies ran while one was open for 2% -> 2% of each run, Pallas kernels for 12% -> 12%
where the time goes in v4:
time: 199 us; the launch traced here: 198 us
  waiting for transfers between devices  83.5 us (42%)
  starting transfers between devices  51.8 us (26%)
  Pallas kernels  36.3 us (18%)
  blocking collectives  18.5 us (9%)
  local copies, waits for them, and re-layouts  6.33 us (3%)
    ppermute x26, waiting for transfers between devices, send(): return lax.ppermute(block, MESH_AXES, pairs)  45.7 us
    ppermute x26, starting transfers between devices, send(): return lax.ppermute(block, MESH_AXES, pairs)  32.2 us
    all_to_all x1, blocking collectives, shards(): sums = lax.all_to_all(sums, 'prow', 0, 0)  18.5 us
    all_to_all x1, waiting for transfers between devices, shards(): rows_in = lax.all_to_all(rows_out, 'prow', 0, 0)  13.5 us
    all_to_all x1, waiting for transfers between devices, shards(): spread_low = lax.all_to_all(spread_low, 'prow', 0, 0)  12.2 us
    pallas_call x2, Pallas kernels, level_one(): call(body, shapes, [SMEM] + [HBM] * 9 + [VMEM] * (1 + len(more)), [pltpu....  10.8 us
    pallas_call x1, Pallas kernels, kids(): call(kids_body, [jax.ShapeDtypeStruct((HALF, 2 * B), F32)] * 2, [SMEM] +...  10.3 us
    all_to_all x1, waiting for transfers between devices, shards(): got = lax.all_to_all(packed, 'pcol', 0, 0)  7.22 us
  transfers between devices with their start and end apart: 30, of which 16 were waited for; matrix products, arithmetic and copies ran while one was open for 2% of the time, Pallas kernels for 12%

profile of v4, /device:TPU:0, one launch (start us, length us, event | category | flops | bytes accessed | tf_op | source)
XLA Modules:
  0.0 198.3 jit_solution(15661367741658750166)
XLA Ops:
  0.7 1.4 dynamic-slice_bitcast_fusion
  2.1 0.1 collective-permute-start
  2.2 0.2 copy-done.7
  2.4 1.2 shard_map.129
  3.6 5.6 %all-to-all-start = ((bf16[8,3,4,32,256]{4,3,2,1,0:T(8,128)(2,1)}), bf16[8,3,4,32,256]{4,3,2,1,0:T(8,128)(2,1)}, u32[]{:S(2)}, u32[]{:S(2)}) async-start(bf16[8,3,4,32,256]{4,3,2,1,0:T(8,128)(2,1)} %shard_map.129), calls=%async_computation | async-start | bytes 3145728 | tf_op jit(solution)/shard_map/all_to_all | solution.py:400
  9.2 0.7 copy.14.select
  9.9 0.6 pad_add_fusion.place
  10.5 2.2 %shard_map.128.tab.tab_ref = s32[123]{0:T(128)} custom-call(s32[2]{0:T(128)} %pad_add_fusion.place, s32[16,16]{1,0:T(8,128)} %struct.1, s32[32,8]{1,0:T(8,128)} %copy.14.select, s32[32]{0:T(128)} %parent.3), custom_call_target="tpu_custom_call" | custom-call | tf_op jit(solution)/shard_map/pallas_call | solution.py:385
  12.7 0.1 pad_maximum_fusion.refs_0_
  12.8 2.0 %collective-permute-start.1 = (bf16[2,512,512]{2,1,0:T(8,128)(2,1)S(1)}, bf16[2,512,512]{2,1,0:T(8,128)(2,1)S(1)}, u32[]{:S(2)}, u32[]{:S(2)}) collective-permute-start(bf16[2,512,512]{2,1,0:T(8,128)(2,1)S(1)} %pad_maximum_fusion.refs_0_), channel_id=1, source_target_pairs={{0,4},{1,5},{2,6},{3,7},{4,8},{5,9},{6,10},{7,11},{8,12},{9,13},{1... | collective-permute-start | bytes 3145736 | tf_op jit(solution)/shard_map/ppermute | solution.py:37
  14.8 2.2 %collective-permute-start.2 = (bf16[2,512,512]{2,1,0:T(8,128)(2,1)S(1)}, bf16[2,512,512]{2,1,0:T(8,128)(2,1)}, u32[]{:S(2)}, u32[]{:S(2)}) collective-permute-start(bf16[2,512,512]{2,1,0:T(8,128)(2,1)S(1)} %pad_maximum_fusion.refs_0_), channel_id=1, source_target_pairs={{0,12},{1,13},{2,14},{3,15},{4,0},{5,1},{6,2},{7,3},{8,4},{9,5},{1... | collective-permute-start | bytes 3145736 | tf_op jit(solution)/shard_map/ppermute | solution.py:37
  17.0 0.1 collective-permute-start.3
  17.1 2.8 %collective-permute-start.5 = (bf16[2,512,512]{2,1,0:T(8,128)(2,1)S(1)}, bf16[2,512,512]{2,1,0:T(8,128)(2,1)}, u32[]{:S(2)}, u32[]{:S(2)}) collective-permute-start(bf16[2,512,512]{2,1,0:T(8,128)(2,1)S(1)} %pad_maximum_fusion.refs_0_), channel_id=1, source_target_pairs={{0,2},{1,3},{2,0},{3,1},{4,6},{5,7},{6,4},{7,5},{8,10},{9,11},{10,... | collective-permute-start | bytes 3145736 | tf_op jit(solution)/shard_map/ppermute | solution.py:37
  19.9 12.2 %all-to-all-done = bf16[8,3,4,32,256]{4,3,2,1,0:T(8,128)(2,1)} async-done(((bf16[8,3,4,32,256]{4,3,2,1,0:T(8,128)(2,1)}), bf16[8,3,4,32,256]{4,3,2,1,0:T(8,128)(2,1)}, u32[]{:S(2)}, u32[]{:S(2)}) %all-to-all-start) | async-done | bytes 1572896 | tf_op jit(solution)/shard_map/all_to_all | solution.py:400
  32.1 8.2 %collective-permute-done.1.refs_3_ = bf16[2,512,512]{2,1,0:T(8,128)(2,1)S(1)} collective-permute-done((bf16[2,512,512]{2,1,0:T(8,128)(2,1)S(1)}, bf16[2,512,512]{2,1,0:T(8,128)(2,1)S(1)}, u32[]{:S(2)}, u32[]{:S(2)}) %collective-permute-start.1) | collective-permute-done | bytes 1048608 | tf_op jit(solution)/shard_map/ppermute | solution.py:37
  40.3 1.4 collective-permute-start.4
  41.6 1.5 shard_map.130.refs_0_
  43.1 1.8 collective-permute-start.7
  44.9 1.5 collective-permute-start.9
  46.4 1.8 collective-permute-start.6
  48.1 8.7 %collective-permute-done.7.refs_3_ = bf16[32,32,256]{2,1,0:T(8,128)(2,1)S(1)} collective-permute-done((bf16[32,32,256]{2,1,0:T(8,128)(2,1)S(1)}, bf16[32,32,256]{2,1,0:T(8,128)(2,1)S(1)}, u32[]{:S(2)}, u32[]{:S(2)}) %collective-permute-start.7) | collective-permute-done | bytes 524320 | tf_op jit(solution)/shard_map/ppermute | solution.py:37
  56.8 0.2 collective-permute-start.8
  57.0 6.5 %collective-permute-done.9.refs_4_ = bf16[32,32,256]{2,1,0:T(8,128)(2,1)S(1)} collective-permute-done((bf16[32,32,256]{2,1,0:T(8,128)(2,1)S(1)}, bf16[32,32,256]{2,1,0:T(8,128)(2,1)S(1)}, u32[]{:S(2)}, u32[]{:S(2)}) %collective-permute-start.9) | collective-permute-done | bytes 524320 | tf_op jit(solution)/shard_map/ppermute | solution.py:37
  63.6 1.8 collective-permute-start.10
  65.3 4.0 %collective-permute-start.13 = (bf16[2,512,512]{2,1,0:T(8,128)(2,1)}, bf16[2,512,512]{2,1,0:T(8,128)(2,1)S(1)}, u32[]{:S(2)}, u32[]{:S(2)}) collective-permute-start(bf16[2,512,512]{2,1,0:T(8,128)(2,1)} %collective-permute-done.5.refs_4_), channel_id=1, source_target_pairs={{0,12},{1,13},{2,14},{3,15},{4,0},{5,1},{6,2},{7,3},{8,4},{9,5},{1... | collective-permute-start | bytes 3145736 | tf_op jit(solution)/shard_map/ppermute | solution.py:37
  69.4 2.8 %collective-permute-start.15 = (bf16[2,512,512]{2,1,0:T(8,128)(2,1)S(1)}, bf16[2,512,512]{2,1,0:T(8,128)(2,1)S(1)}, u32[]{:S(2)}, u32[]{:S(2)}) collective-permute-start(bf16[2,512,512]{2,1,0:T(8,128)(2,1)S(1)} %collective-permute-done.4.refs_2_), channel_id=1, source_target_pairs={{0,2},{1,3},{2,0},{3,1},{4,6},{5,7},{6,4},{7,5},{8,10},{9,11},{10,... | collective-permute-start | bytes 3145736 | tf_op jit(solution)/shard_map/ppermute | solution.py:37
  72.2 0.2 collective-permute-start.12
  72.5 4.1 %collective-permute-done.10.refs_5_ = bf16[32,32,256]{2,1,0:T(8,128)(2,1)S(1)} collective-permute-done((bf16[32,32,256]{2,1,0:T(8,128)(2,1)S(1)}, bf16[32,32,256]{2,1,0:T(8,128)(2,1)S(1)}, u32[]{:S(2)}, u32[]{:S(2)}) %collective-permute-start.10) | collective-permute-done | bytes 524320 | tf_op jit(solution)/shard_map/ppermute | solution.py:37
  76.6 3.0 %collective-permute-start.11 = (bf16[32,32,256]{2,1,0:T(8,128)(2,1)S(1)}, bf16[32,32,256]{2,1,0:T(8,128)(2,1)S(1)}, u32[]{:S(2)}, u32[]{:S(2)}) collective-permute-start(bf16[32,32,256]{2,1,0:T(8,128)(2,1)S(1)} %collective-permute-done.10.refs_5_), channel_id=1, source_target_pairs={{0,96},{1,97},{2,98},{3,99},{4,100},{5,101},{6,102},{7,103},{8,104... | collective-permute-start | bytes 1572872 | tf_op jit(solution)/shard_map/ppermute | solution.py:37
  79.6 6.0 %collective-permute-done.12.refs_7_ = bf16[32,32,256]{2,1,0:T(8,128)(2,1)S(1)} collective-permute-done((bf16[32,32,256]{2,1,0:T(8,128)(2,1)S(1)}, bf16[32,32,256]{2,1,0:T(8,128)(2,1)S(1)}, u32[]{:S(2)}, u32[]{:S(2)}) %collective-permute-start.12) | collective-permute-done | bytes 524320 | tf_op jit(solution)/shard_map/ppermute | solution.py:37
  85.6 3.6 %collective-permute-done.11.refs_6_ = bf16[32,32,256]{2,1,0:T(8,128)(2,1)S(1)} collective-permute-done((bf16[32,32,256]{2,1,0:T(8,128)(2,1)S(1)}, bf16[32,32,256]{2,1,0:T(8,128)(2,1)S(1)}, u32[]{:S(2)}, u32[]{:S(2)}) %collective-permute-start.11) | collective-permute-done | bytes 524320 | tf_op jit(solution)/shard_map/ppermute | solution.py:37
  89.2 2.4 %shard_map.131 = (bf16[16,256,256]{2,1,0:T(8,128)(2,1)S(1)}, bf16[16,256,256]{2,1,0:T(8,128)(2,1)}) custom-call(s32[123]{0:T(128)S(1)} %copy-done.12, bf16[32,32,256]{2,1,0:T(8,128)(2,1)S(1)} %shard_map.130.refs_0_, bf16[32,32,256]{2,1,0:T(8,128)(2,1)S(1)} %collective-permute-done.6.refs_1_, bf16[32,32,256]{2,1,0:T(8,128)(2,1)S(1)} %collective-permute-done.8.refs_2_, ...), custom_call_target="tpu_custom_call" | custom-call | tf_op jit(solution)/shard_map/pallas_call | solution.py:151
  91.6 2.9 %collective-permute-done.14.refs_7_ = bf16[2,512,512]{2,1,0:T(8,128)(2,1)S(1)} collective-permute-done((bf16[2,512,512]{2,1,0:T(8,128)(2,1)}, bf16[2,512,512]{2,1,0:T(8,128)(2,1)S(1)}, u32[]{:S(2)}, u32[]{:S(2)}) %collective-permute-start.14) | collective-permute-done | bytes 1048608 | tf_op jit(solution)/shard_map/ppermute | solution.py:37
  94.5 0.2 collective-permute-done.15.refs_6_
  94.7 5.3 %shard_map.132 = (bf16[512,256]{1,0:T(8,128)(2,1)S(1)}, f32[4,32,256]{2,1,0:T(8,128)S(1)}, f32[4,32,256]{2,1,0:T(8,128)}) custom-call(s32[123]{0:T(128)S(1)} %copy-done.12, bf16[2,512,512]{2,1,0:T(8,128)(2,1)S(1)} %pad_maximum_fusion.refs_0_, bf16[2,512,512]{2,1,0:T(8,128)(2,1)} %collective-permute-done.2.refs_1_, ...), custom_call_target="tpu_custom_call" | custom-call | flops 1073741824 | bytes 12582912 | tf_op jit(solution)/shard_map/pallas_call | solution.py:235
  100.0 5.5 %shard_map.133 = (bf16[512,256]{1,0:T(8,128)(2,1)S(1)}, f32[4,32,256]{2,1,0:T(8,128)S(1)}, f32[4,32,256]{2,1,0:T(8,128)}, bf16[16,2,32,256]{3,2,1,0:T(8,128)(2,1)}) custom-call(s32[123]{0:T(128)S(1)} %copy-done.12, bf16[2,512,512]{2,1,0:T(8,128)(2,1)S(1)} %pad_maximum_fusion.refs_0_, bf16[2,512,512]{2,1,0:T(8,128)(2,1)} %collective-permute-done.2.refs_1_, ...), custom_call_target="tpu_custom_call" | custom-call | flops 1073741824 | bytes 12582912 | tf_op jit(solution)/shard_map/pallas_call | solution.py:235
  105.6 0.7 copy-done.15
  106.3 0.3 collective-permute-start.18
  106.5 1.1 collective-permute-start.21
  107.7 0.4 collective-permute-start.22
  108.1 0.6 collective-permute-start.20
  108.7 6.6 %all-to-all-start.1 = ((bf16[16,2,32,256]{3,2,1,0:T(8,128)(2,1)}), bf16[16,2,32,256]{3,2,1,0:T(8,128)(2,1)S(1)}, u32[]{:S(2)}, u32[]{:S(2)}) async-start(bf16[16,2,32,256]{3,2,1,0:T(8,128)(2,1)} %get-tuple-element.54), calls=%async_computation.1 | async-start | bytes 1048576 | tf_op jit(solution)/shard_map/all_to_all | solution.py:437
  115.4 0.3 collective-permute-start.23
  115.7 3.2 %collective-permute-start.24 = (f32[32,256]{1,0:T(8,128)S(1)}, f32[32,256]{1,0:T(8,128)S(1)}, u32[]{:S(2)}, u32[]{:S(2)}) collective-permute-start(f32[32,256]{1,0:T(8,128)S(1)} %get-tuple-element.76), channel_id=1, source_target_pairs={{0,64},{1,65},{2,66},{3,67},{4,68},{5,69},{6,70},{7,71},{8,72},{9,... | collective-permute-start | bytes 98312 | tf_op jit(solution)/shard_map/ppermute | solution.py:37
  119.0 2.0 %collective-permute-done.23.refs_1_ = f32[32,256]{1,0:T(8,128)S(1)} collective-permute-done((f32[32,256]{1,0:T(8,128)S(1)}, f32[32,256]{1,0:T(8,128)S(1)}, u32[]{:S(2)}, u32[]{:S(2)}) %collective-permute-start.23) | collective-permute-done | bytes 32800 | tf_op jit(solution)/shard_map/ppermute | solution.py:37
  121.0 0.4 collective-permute-done.24.refs_2_
  121.3 1.5 collective-permute-done.25.refs_3_
  122.8 4.9 %all-to-all-done.1.spread = bf16[16,2,32,256]{3,2,1,0:T(8,128)(2,1)S(1)} async-done(((bf16[16,2,32,256]{3,2,1,0:T(8,128)(2,1)}), bf16[16,2,32,256]{3,2,1,0:T(8,128)(2,1)S(1)}, u32[]{:S(2)}, u32[]{:S(2)}) %all-to-all-start.1) | async-done | bytes 524320 | tf_op jit(solution)/shard_map/all_to_all | solution.py:437
  127.7 1.9 shard_map.135
  129.6 3.7 %all-to-all-start.2 = ((bf16[16,160,256]{2,1,0:T(8,128)(2,1)}), bf16[16,160,256]{2,1,0:T(8,128)(2,1)S(1)}, u32[]{:S(2)}, u32[]{:S(2)}) async-start(bf16[16,160,256]{2,1,0:T(8,128)(2,1)} %get-tuple-element.62), calls=%async_computation.2 | async-start | bytes 2621440 | tf_op jit(solution)/shard_map/all_to_all | solution.py:456
  133.4 10.3 %shard_map.134 = (f32[512,512]{1,0:T(8,128)}, f32[512,512]{1,0:T(8,128)}) custom-call(s32[123]{0:T(128)} %shard_map.128.tab.tab_ref, bf16[2,512,512]{2,1,0:T(8,128)(2,1)} %copy-done.1, bf16[2,512,512]{2,1,0:T(8,128)(2,1)} %collective-permute-done.2.refs_1_, bf16[2,512,512]{2,1,0:T(8,128)(2,1)} %copy-done.3, bf16[2,512,512]{2,1,0:T(8,128)(2,1)} %copy-done.2, ...), custom_call_target="tpu_custom_call" | custom-call | flops 2147483648 | bytes 16777216 | tf_op jit(solution)/shard_map/pallas_call | solution.py:272
  143.7 0.4 collective-permute-start.19
  144.0 0.2 collective-permute-start.17
  144.3 1.0 constant_dynamic-slice_fusion.link
  145.2 1.7 collective-permute-done.17
  146.9 7.2 %all-to-all-done.2.got = bf16[16,160,256]{2,1,0:T(8,128)(2,1)S(1)} async-done(((bf16[16,160,256]{2,1,0:T(8,128)(2,1)}), bf16[16,160,256]{2,1,0:T(8,128)(2,1)S(1)}, u32[]{:S(2)}, u32[]{:S(2)}) %all-to-all-start.2) | async-done | bytes 1310752 | tf_op jit(solution)/shard_map/all_to_all | solution.py:456
  154.2 1.2 copy-done.10
  155.4 3.2 %shard_map.136 = (bf16[1024,512]{1,0:T(8,128)(2,1)}, f32[8,64,512]{2,1,0:T(8,128)S(1)}) custom-call(s32[123]{0:T(128)S(1)} %copy-done.13, bf16[16,160,256]{2,1,0:T(8,128)(2,1)S(1)} %all-to-all-done.2.got, f32[512,512]{1,0:T(8,128)S(1)} %copy-done.10, f32[512,512]{1,0:T(8,128)} %collective-permute-done.19.part_sib, bf16[1024,512]{1,0:T(8,128)(2,1)S(1)} %copy-done.8, ...), custom_call_target="tpu_custom_call" | custom-call | tf_op jit(solution)/shard_map/pallas_call | solution.py:457
  158.6 18.5 %all_to_all.25.sums = f32[8,64,512]{2,1,0:T(8,128)S(1)} all-to-all(f32[8,64,512]{2,1,0:T(8,128)S(1)} %get-tuple-element.65), channel_id=1, replica_groups=mesh['prow'=8,'pcol'=16] {'prow'}, dimensions={0} | all-to-all | bytes 2097152 | tf_op jit(solution)/shard_map/all_to_all | solution.py:463
  177.1 1.7 shard_map.137
  178.8 3.7 %all-to-all-start.4 = ((bf16[8,128,512]{2,1,0:T(8,128)(2,1)}), bf16[8,128,512]{2,1,0:T(8,128)(2,1)S(1)}, u32[]{:S(2)}, u32[]{:S(2)}) async-start(bf16[8,128,512]{2,1,0:T(8,128)(2,1)} %shard_map.137), calls=%async_computation.4 | async-start | bytes 2097152 | tf_op jit(solution)/shard_map/all_to_all | solution.py:469
  182.6 1.0 constant_dynamic-update-slice_fusion
  183.6 13.5 %all-to-all-done.4.got = bf16[8,128,512]{2,1,0:T(8,128)(2,1)S(1)} async-done(((bf16[8,128,512]{2,1,0:T(8,128)(2,1)}), bf16[8,128,512]{2,1,0:T(8,128)(2,1)S(1)}, u32[]{:S(2)}, u32[]{:S(2)}) %all-to-all-start.4) | async-done | bytes 1048608 | tf_op jit(solution)/shard_map/all_to_all | solution.py:469
  197.1 1.2 shard_map.138
  (58 shorter events, 0.4 us)
Async XLA Ops:
  0.6 118.3 %copy-start = (f32[256,256]{1,0:T(8,128)S(1)}, f32[256,256]{1,0:T(8,128)}, u32[]{:S(2)}) copy-start(f32[256,256]{1,0:T(8,128)} %param.13) | copy-start | bytes 786436
  0.6 1.5 copy-start.9
  0.7 1.7 copy-start.7
  2.1 10.6 %collective-permute-start = (bf16[512,512]{1,0:T(8,128)(2,1)S(1)}, bf16[512,512]{1,0:T(8,128)(2,1)S(1)}, u32[]{:S(2)}, u32[]{:S(2)}) collective-permute-start(bf16[512,512]{1,0:T(8,128)(2,1)S(1)} %get-tuple-element.72), channel_id=1, source_target_pairs={{0,1},{1,0},{2,3},{3,2},{4,5},{5,4},{6,7},{7,6},{8,9},{9,8},{10,11... | collective-permute-start | bytes 1572872 | tf_op jit(solution)/shard_map/ppermute | solution.py:37
  3.6 5.6 %copy-start.18 = (s32[32,8]{0,1:T(8,128)S(1)}, s32[32,8]{0,1:T(8,128)}, u32[]{:S(2)}) copy-start(s32[32,8]{0,1:T(8,128)} %param.16) | copy-start | bytes 3076
  3.6 28.5 %all-to-all-start = ((bf16[8,3,4,32,256]{4,3,2,1,0:T(8,128)(2,1)}), bf16[8,3,4,32,256]{4,3,2,1,0:T(8,128)(2,1)}, u32[]{:S(2)}, u32[]{:S(2)}) async-start(bf16[8,3,4,32,256]{4,3,2,1,0:T(8,128)(2,1)} %shard_map.129), calls=%async_computation | async-start | bytes 3145728 | tf_op jit(solution)/shard_map/all_to_all | solution.py:400
  12.7 29.0 %copy-start.12 = (s32[123]{0:T(128)S(1)}, s32[123]{0:T(128)}, u32[]{:S(2)}) copy-start(s32[123]{0:T(128)} %shard_map.128.tab.tab_ref) | copy-start | bytes 1480
  12.8 87.2 %copy-start.1 = (bf16[2,512,512]{2,1,0:T(8,128)(2,1)}, bf16[2,512,512]{2,1,0:T(8,128)(2,1)S(1)}, u32[]{:S(2)}) copy-start(bf16[2,512,512]{2,1,0:T(8,128)(2,1)S(1)} %pad_maximum_fusion.refs_0_) | copy-start | bytes 3145732
  12.8 27.5 %collective-permute-start.1 = (bf16[2,512,512]{2,1,0:T(8,128)(2,1)S(1)}, bf16[2,512,512]{2,1,0:T(8,128)(2,1)S(1)}, u32[]{:S(2)}, u32[]{:S(2)}) collective-permute-start(bf16[2,512,512]{2,1,0:T(8,128)(2,1)S(1)} %pad_maximum_fusion.refs_0_), channel_id=1, source_target_pairs={{0,4},{1,5},{2,6},{3,7},{4,8},{5,9},{6,10},{7,11},{8,12},{9,13},{1... | collective-permute-start | bytes 3145736 | tf_op jit(solution)/shard_map/ppermute | solution.py:37
  14.8 25.5 %collective-permute-start.2 = (bf16[2,512,512]{2,1,0:T(8,128)(2,1)S(1)}, bf16[2,512,512]{2,1,0:T(8,128)(2,1)}, u32[]{:S(2)}, u32[]{:S(2)}) collective-permute-start(bf16[2,512,512]{2,1,0:T(8,128)(2,1)S(1)} %pad_maximum_fusion.refs_0_), channel_id=1, source_target_pairs={{0,12},{1,13},{2,14},{3,15},{4,0},{5,1},{6,2},{7,3},{8,4},{9,5},{1... | collective-permute-start | bytes 3145736 | tf_op jit(solution)/shard_map/ppermute | solution.py:37
  17.0 2.9 %collective-permute-start.3 = (bf16[512,256]{1,0:T(8,128)(2,1)S(1)}, bf16[512,256]{1,0:T(8,128)(2,1)S(1)}, u32[]{:S(2)}, u32[]{:S(2)}) collective-permute-start(bf16[512,256]{1,0:T(8,128)(2,1)S(1)} %get-tuple-element.74), channel_id=1, source_target_pairs={{0,1},{1,0},{2,3},{3,2},{4,5},{5,4},{6,7},{7,6},{8,9},{9,8},{10,11... | collective-permute-start | bytes 786440 | tf_op jit(solution)/shard_map/ppermute | solution.py:37
  17.1 48.2 %collective-permute-start.5 = (bf16[2,512,512]{2,1,0:T(8,128)(2,1)S(1)}, bf16[2,512,512]{2,1,0:T(8,128)(2,1)}, u32[]{:S(2)}, u32[]{:S(2)}) collective-permute-start(bf16[2,512,512]{2,1,0:T(8,128)(2,1)S(1)} %pad_maximum_fusion.refs_0_), channel_id=1, source_target_pairs={{0,2},{1,3},{2,0},{3,1},{4,6},{5,7},{6,4},{7,5},{8,10},{9,11},{10,... | collective-permute-start | bytes 3145736 | tf_op jit(solution)/shard_map/ppermute | solution.py:37
  40.3 59.7 %copy-start.2 = (bf16[2,512,512]{2,1,0:T(8,128)(2,1)}, bf16[2,512,512]{2,1,0:T(8,128)(2,1)S(1)}, u32[]{:S(2)}) copy-start(bf16[2,512,512]{2,1,0:T(8,128)(2,1)S(1)} %collective-permute-done.1.refs_3_) | copy-start | bytes 3145732
  40.3 29.1 %collective-permute-start.4 = (bf16[2,512,512]{2,1,0:T(8,128)(2,1)S(1)}, bf16[2,512,512]{2,1,0:T(8,128)(2,1)S(1)}, u32[]{:S(2)}, u32[]{:S(2)}) collective-permute-start(bf16[2,512,512]{2,1,0:T(8,128)(2,1)S(1)} %collective-permute-done.1.refs_3_), channel_id=1, source_target_pairs={{0,4},{1,5},{2,6},{3,7},{4,8},{5,9},{6,10},{7,11},{8,12},{9,13},{1... | collective-permute-start | bytes 3145736 | tf_op jit(solution)/shard_map/ppermute | solution.py:37
  43.1 13.7 %collective-permute-start.7 = (bf16[32,32,256]{2,1,0:T(8,128)(2,1)S(1)}, bf16[32,32,256]{2,1,0:T(8,128)(2,1)S(1)}, u32[]{:S(2)}, u32[]{:S(2)}) collective-permute-start(bf16[32,32,256]{2,1,0:T(8,128)(2,1)S(1)} %shard_map.130.refs_0_), channel_id=1, source_target_pairs={{0,32},{1,33},{2,34},{3,35},{4,36},{5,37},{6,38},{7,39},{8,40},{9,... | collective-permute-start | bytes 1572872 | tf_op jit(solution)/shard_map/ppermute | solution.py:37
  44.9 18.7 %collective-permute-start.9 = (bf16[32,32,256]{2,1,0:T(8,128)(2,1)S(1)}, bf16[32,32,256]{2,1,0:T(8,128)(2,1)S(1)}, u32[]{:S(2)}, u32[]{:S(2)}) collective-permute-start(bf16[32,32,256]{2,1,0:T(8,128)(2,1)S(1)} %shard_map.130.refs_0_), channel_id=1, source_target_pairs={{0,16},{1,17},{2,18},{3,19},{4,20},{5,21},{6,22},{7,23},{8,24},{9,... | collective-permute-start | bytes 1572872 | tf_op jit(solution)/shard_map/ppermute | solution.py:37
  46.4 23.0 %collective-permute-start.6 = (bf16[32,32,256]{2,1,0:T(8,128)(2,1)S(1)}, bf16[32,32,256]{2,1,0:T(8,128)(2,1)S(1)}, u32[]{:S(2)}, u32[]{:S(2)}) collective-permute-start(bf16[32,32,256]{2,1,0:T(8,128)(2,1)S(1)} %shard_map.130.refs_0_), channel_id=1, source_target_pairs={{0,96},{1,97},{2,98},{3,99},{4,100},{5,101},{6,102},{7,103},{8,104... | collective-permute-start | bytes 1572872 | tf_op jit(solution)/shard_map/ppermute | solution.py:37
  56.8 15.4 %collective-permute-start.8 = (bf16[32,32,256]{2,1,0:T(8,128)(2,1)S(1)}, bf16[32,32,256]{2,1,0:T(8,128)(2,1)S(1)}, u32[]{:S(2)}, u32[]{:S(2)}) collective-permute-start(bf16[32,32,256]{2,1,0:T(8,128)(2,1)S(1)} %collective-permute-done.7.refs_3_), channel_id=1, source_target_pairs={{0,32},{1,33},{2,34},{3,35},{4,36},{5,37},{6,38},{7,39},{8,40},{9,... | collective-permute-start | bytes 1572872 | tf_op jit(solution)/shard_map/ppermute | solution.py:37
  63.6 13.0 %collective-permute-start.10 = (bf16[32,32,256]{2,1,0:T(8,128)(2,1)S(1)}, bf16[32,32,256]{2,1,0:T(8,128)(2,1)S(1)}, u32[]{:S(2)}, u32[]{:S(2)}) collective-permute-start(bf16[32,32,256]{2,1,0:T(8,128)(2,1)S(1)} %collective-permute-done.9.refs_4_), channel_id=1, source_target_pairs={{0,96},{1,97},{2,98},{3,99},{4,100},{5,101},{6,102},{7,103},{8,104... | collective-permute-start | bytes 1572872 | tf_op jit(solution)/shard_map/ppermute | solution.py:37
  65.3 26.2 %collective-permute-start.13 = (bf16[2,512,512]{2,1,0:T(8,128)(2,1)}, bf16[2,512,512]{2,1,0:T(8,128)(2,1)S(1)}, u32[]{:S(2)}, u32[]{:S(2)}) collective-permute-start(bf16[2,512,512]{2,1,0:T(8,128)(2,1)} %collective-permute-done.5.refs_4_), channel_id=1, source_target_pairs={{0,12},{1,13},{2,14},{3,15},{4,0},{5,1},{6,2},{7,3},{8,4},{9,5},{1... | collective-permute-start | bytes 3145736 | tf_op jit(solution)/shard_map/ppermute | solution.py:37
  69.4 25.1 %collective-permute-start.14 = (bf16[2,512,512]{2,1,0:T(8,128)(2,1)}, bf16[2,512,512]{2,1,0:T(8,128)(2,1)S(1)}, u32[]{:S(2)}, u32[]{:S(2)}) collective-permute-start(bf16[2,512,512]{2,1,0:T(8,128)(2,1)} %collective-permute-done.5.refs_4_), channel_id=1, source_target_pairs={{0,4},{1,5},{2,6},{3,7},{4,8},{5,9},{6,10},{7,11},{8,12},{9,13},{1... | collective-permute-start | bytes 3145736 | tf_op jit(solution)/shard_map/ppermute | solution.py:37
  69.4 30.6 %copy-start.3 = (bf16[2,512,512]{2,1,0:T(8,128)(2,1)}, bf16[2,512,512]{2,1,0:T(8,128)(2,1)S(1)}, u32[]{:S(2)}) copy-start(bf16[2,512,512]{2,1,0:T(8,128)(2,1)S(1)} %collective-permute-done.4.refs_2_) | copy-start | bytes 3145732
  69.4 25.3 %collective-permute-start.15 = (bf16[2,512,512]{2,1,0:T(8,128)(2,1)S(1)}, bf16[2,512,512]{2,1,0:T(8,128)(2,1)S(1)}, u32[]{:S(2)}, u32[]{:S(2)}) collective-permute-start(bf16[2,512,512]{2,1,0:T(8,128)(2,1)S(1)} %collective-permute-done.4.refs_2_), channel_id=1, source_target_pairs={{0,2},{1,3},{2,0},{3,1},{4,6},{5,7},{6,4},{7,5},{8,10},{9,11},{10,... | collective-permute-start | bytes 3145736 | tf_op jit(solution)/shard_map/ppermute | solution.py:37
  72.2 13.4 %collective-permute-start.12 = (bf16[32,32,256]{2,1,0:T(8,128)(2,1)S(1)}, bf16[32,32,256]{2,1,0:T(8,128)(2,1)S(1)}, u32[]{:S(2)}, u32[]{:S(2)}) collective-permute-start(bf16[32,32,256]{2,1,0:T(8,128)(2,1)S(1)} %collective-permute-done.9.refs_4_), channel_id=1, source_target_pairs={{0,32},{1,33},{2,34},{3,35},{4,36},{5,37},{6,38},{7,39},{8,40},{9,... | collective-permute-start | bytes 1572872 | tf_op jit(solution)/shard_map/ppermute | solution.py:37
  76.6 12.6 %collective-permute-start.11 = (bf16[32,32,256]{2,1,0:T(8,128)(2,1)S(1)}, bf16[32,32,256]{2,1,0:T(8,128)(2,1)S(1)}, u32[]{:S(2)}, u32[]{:S(2)}) collective-permute-start(bf16[32,32,256]{2,1,0:T(8,128)(2,1)S(1)} %collective-permute-done.10.refs_5_), channel_id=1, source_target_pairs={{0,96},{1,97},{2,98},{3,99},{4,100},{5,101},{6,102},{7,103},{8,104... | collective-permute-start | bytes 1572872 | tf_op jit(solution)/shard_map/ppermute | solution.py:37
  91.5 8.5 %copy-start.4 = (bf16[2,512,512]{2,1,0:T(8,128)(2,1)}, bf16[2,512,512]{2,1,0:T(8,128)(2,1)S(1)}, u32[]{:S(2)}) copy-start(bf16[2,512,512]{2,1,0:T(8,128)(2,1)S(1)} %collective-permute-done.13.refs_5_) | copy-start | bytes 3145732
  94.5 5.5 %copy-start.5 = (bf16[2,512,512]{2,1,0:T(8,128)(2,1)}, bf16[2,512,512]{2,1,0:T(8,128)(2,1)S(1)}, u32[]{:S(2)}) copy-start(bf16[2,512,512]{2,1,0:T(8,128)(2,1)S(1)} %collective-permute-done.14.refs_7_) | copy-start | bytes 3145732
  94.7 5.4 %copy-start.6 = (bf16[2,512,512]{2,1,0:T(8,128)(2,1)}, bf16[2,512,512]{2,1,0:T(8,128)(2,1)S(1)}, u32[]{:S(2)}) copy-start(bf16[2,512,512]{2,1,0:T(8,128)(2,1)S(1)} %collective-permute-done.15.refs_6_) | copy-start | bytes 3145732
  94.7 5.3 %collective-permute-start.16 = (bf16[16,256,256]{2,1,0:T(8,128)(2,1)S(1)}, bf16[16,256,256]{2,1,0:T(8,128)(2,1)S(1)}, u32[]{:S(2)}, u32[]{:S(2)}) collective-permute-start(bf16[16,256,256]{2,1,0:T(8,128)(2,1)S(1)} %get-tuple-element.49.refs_8_), channel_id=1, source_target_pairs={{0,1},{1,0},{2,3},{3,2},{4,5},{5,4},{6,7},{7,6},{8,9},{9,8},{10,11... | collective-permute-start | bytes 6291464 | tf_op jit(solution)/shard_map/ppermute | solution.py:37
  100.0 27.7 %copy-start.14 = (s32[32]{0:T(128)S(1)}, s32[32]{0:T(128)}, u32[]{:S(2)}) copy-start(s32[32]{0:T(128)} %parent.3) | copy-start | bytes 388
  105.6 0.7 copy-start.15
  106.3 27.1 %collective-permute-start.18 = (bf16[16,256,256]{2,1,0:T(8,128)(2,1)}, bf16[16,256,256]{2,1,0:T(8,128)(2,1)}, u32[]{:S(2)}, u32[]{:S(2)}) collective-permute-start(bf16[16,256,256]{2,1,0:T(8,128)(2,1)} %get-tuple-element.55.refs_8_), channel_id=1, source_target_pairs={{0,1},{1,0},{2,3},{3,2},{4,5},{5,4},{6,7},{7,6},{8,9},{9,8},{10,11... | collective-permute-start | bytes 6291464 | tf_op jit(solution)/shard_map/ppermute | solution.py:37
  106.5 8.8 %collective-permute-start.21 = (f32[4,32,256]{2,1,0:T(8,128)}, f32[4,32,256]{2,1,0:T(8,128)S(1)}, u32[]{:S(2)}, u32[]{:S(2)}) collective-permute-start(f32[4,32,256]{2,1,0:T(8,128)} %get-tuple-element.60), channel_id=1, source_target_pairs={{0,16},{1,17},{2,18},{3,19},{4,20},{5,21},{6,22},{7,23},{8,24},{9,... | collective-permute-start | bytes 393224 | tf_op jit(solution)/shard_map/ppermute | solution.py:37
  107.7 7.7 %collective-permute-start.22 = (f32[4,32,256]{2,1,0:T(8,128)}, f32[4,32,256]{2,1,0:T(8,128)S(1)}, u32[]{:S(2)}, u32[]{:S(2)}) collective-permute-start(f32[4,32,256]{2,1,0:T(8,128)} %get-tuple-element.61), channel_id=1, source_target_pairs={{0,17},{1,16},{2,19},{3,18},{4,21},{5,20},{6,23},{7,22},{8,25},{9,... | collective-permute-start | bytes 393224 | tf_op jit(solution)/shard_map/ppermute | solution.py:37
  108.1 7.2 %collective-permute-start.20 = (f32[4,32,256]{2,1,0:T(8,128)S(1)}, f32[4,32,256]{2,1,0:T(8,128)S(1)}, u32[]{:S(2)}, u32[]{:S(2)}) collective-permute-start(f32[4,32,256]{2,1,0:T(8,128)S(1)} %get-tuple-element.59), channel_id=1, source_target_pairs={{0,1},{1,0},{2,3},{3,2},{4,5},{5,4},{6,7},{7,6},{8,9},{9,8},{10,11... | collective-permute-start | bytes 393224 | tf_op jit(solution)/shard_map/ppermute | solution.py:37
  108.7 19.0 %all-to-all-start.1 = ((bf16[16,2,32,256]{3,2,1,0:T(8,128)(2,1)}), bf16[16,2,32,256]{3,2,1,0:T(8,128)(2,1)S(1)}, u32[]{:S(2)}, u32[]{:S(2)}) async-start(bf16[16,2,32,256]{3,2,1,0:T(8,128)(2,1)} %get-tuple-element.54), calls=%async_computation.1 | async-start | bytes 1048576 | tf_op jit(solution)/shard_map/all_to_all | solution.py:437
  115.4 5.5 %collective-permute-start.23 = (f32[32,256]{1,0:T(8,128)S(1)}, f32[32,256]{1,0:T(8,128)S(1)}, u32[]{:S(2)}, u32[]{:S(2)}) collective-permute-start(f32[32,256]{1,0:T(8,128)S(1)} %get-tuple-element.77), channel_id=1, source_target_pairs={{0,32},{1,33},{2,34},{3,35},{4,36},{5,37},{6,38},{7,39},{8,40},{9,... | collective-permute-start | bytes 98312 | tf_op jit(solution)/shard_map/ppermute | solution.py:37
  115.7 5.6 %collective-permute-start.24 = (f32[32,256]{1,0:T(8,128)S(1)}, f32[32,256]{1,0:T(8,128)S(1)}, u32[]{:S(2)}, u32[]{:S(2)}) collective-permute-start(f32[32,256]{1,0:T(8,128)S(1)} %get-tuple-element.76), channel_id=1, source_target_pairs={{0,64},{1,65},{2,66},{3,67},{4,68},{5,69},{6,70},{7,71},{8,72},{9,... | collective-permute-start | bytes 98312 | tf_op jit(solution)/shard_map/ppermute | solution.py:37
  118.9 3.9 %collective-permute-start.25 = (f32[32,256]{1,0:T(8,128)S(1)}, f32[32,256]{1,0:T(8,128)S(1)}, u32[]{:S(2)}, u32[]{:S(2)}) collective-permute-start(f32[32,256]{1,0:T(8,128)S(1)} %get-tuple-element.75), channel_id=1, source_target_pairs={{0,96},{1,97},{2,98},{3,99},{4,100},{5,101},{6,102},{7,103},{8,104... | collective-permute-start | bytes 98312 | tf_op jit(solution)/shard_map/ppermute | solution.py:37
  129.6 24.5 %all-to-all-start.2 = ((bf16[16,160,256]{2,1,0:T(8,128)(2,1)}), bf16[16,160,256]{2,1,0:T(8,128)(2,1)S(1)}, u32[]{:S(2)}, u32[]{:S(2)}) async-start(bf16[16,160,256]{2,1,0:T(8,128)(2,1)} %get-tuple-element.62), calls=%async_computation.2 | async-start | bytes 2621440 | tf_op jit(solution)/shard_map/all_to_all | solution.py:456
  133.3 10.7 %copy-start.16 = (bf16[512,256]{1,0:T(8,128)(2,1)S(1)}, bf16[512,256]{1,0:T(8,128)(2,1)}, u32[]{:S(2)}) copy-start(bf16[512,256]{1,0:T(8,128)(2,1)} %copy-done.15) | copy-start | bytes 786436
  133.3 20.8 %copy-start.8 = (bf16[1024,512]{1,0:T(8,128)(2,1)S(1)}, bf16[1024,512]{1,0:T(8,128)(2,1)}, u32[]{:S(2)}) copy-start(bf16[1024,512]{1,0:T(8,128)(2,1)} %factor.1) | copy-start | bytes 3145732
  133.3 20.8 %copy-start.13 = (s32[123]{0:T(128)S(1)}, s32[123]{0:T(128)}, u32[]{:S(2)}) copy-start(s32[123]{0:T(128)} %shard_map.128.tab.tab_ref) | copy-start | bytes 1480
  143.7 3.2 %collective-permute-start.19 = (f32[512,512]{1,0:T(8,128)}, f32[512,512]{1,0:T(8,128)}, u32[]{:S(2)}, u32[]{:S(2)}) collective-permute-start(f32[512,512]{1,0:T(8,128)} %get-tuple-element.56), channel_id=1, source_target_pairs={{0,1},{1,0},{2,3},{3,2},{4,5},{5,4},{6,7},{7,6},{8,9},{9,8},{10,11... | collective-permute-start | bytes 3145736 | tf_op jit(solution)/shard_map/ppermute | solution.py:37
  144.0 2.9 %collective-permute-start.17 = (bf16[512,256]{1,0:T(8,128)(2,1)S(1)}, bf16[512,256]{1,0:T(8,128)(2,1)}, u32[]{:S(2)}, u32[]{:S(2)}) collective-permute-start(bf16[512,256]{1,0:T(8,128)(2,1)S(1)} %copy-done.16), channel_id=1, source_target_pairs={{0,1},{1,0},{2,3},{3,2},{4,5},{5,4},{6,7},{7,6},{8,9},{9,8},{10,11... | collective-permute-start | bytes 786440 | tf_op jit(solution)/shard_map/ppermute | solution.py:37
  154.2 1.2 copy-start.10
  178.8 18.3 %copy-start.11 = (f32[256,512]{1,0:T(8,128)S(1)}, f32[256,512]{1,0:T(8,128)}, u32[]{:S(2)}) copy-start(f32[256,512]{1,0:T(8,128)} %dinv.1) | copy-start | bytes 1572868
  178.8 18.3 %all-to-all-start.4 = ((bf16[8,128,512]{2,1,0:T(8,128)(2,1)}), bf16[8,128,512]{2,1,0:T(8,128)(2,1)S(1)}, u32[]{:S(2)}, u32[]{:S(2)}) async-start(bf16[8,128,512]{2,1,0:T(8,128)(2,1)} %shard_map.137), calls=%async_computation.4 | async-start | bytes 2097152 | tf_op jit(solution)/shard_map/all_to_all | solution.py:469
  183.6 14.7 %copy-start.17 = (bf16[1024,256]{1,0:T(8,128)(2,1)}, bf16[1024,256]{1,0:T(8,128)(2,1)S(1)}, u32[]{:S(2)}) copy-start(bf16[1024,256]{1,0:T(8,128)(2,1)S(1)} %constant_dynamic-update-slice_fusion) | copy-start | bytes 1572868

commit v5 on v4

--- a/solution.py
+++ b/solution.py
@@ -50,7 +50,7 @@
 HBM = pl.BlockSpec(memory_space=pltpu.HBM)
 
 
-def call(body, out_shape, in_specs, scratch=(), limit=32, flops=0, moved=0):
+def call(body, out_shape, in_specs, scratch=(), limit=16, flops=0, moved=0):
     outs = [VMEM] * len(out_shape) if isinstance(out_shape, list) else VMEM
     cost = pl.CostEstimate(flops=flops, bytes_accessed=moved, transcendentals=0)
     return pl.pallas_call(

time: 199 us -> 198 us (level)
  transfers between devices with their start and end apart: 30 -> 30, of which waited for: 16 -> 16; matrix products, arithmetic and copies ran while one was open for 2% -> 2% of each run, Pallas kernels for 12% -> 13%
where the time goes in v5:
time: 198 us; the launch traced here: 197 us
  waiting for transfers between devices  82.6 us (42%)
  starting transfers between devices  52 us (26%)
  Pallas kernels  36.7 us (19%)
  blocking collectives  17.7 us (9%)
  local copies, waits for them, and re-layouts  6.33 us (3%)
    ppermute x26, waiting for transfers between devices, send(): return lax.ppermute(block, MESH_AXES, pairs)  45.6 us
    ppermute x26, starting transfers between devices, send(): return lax.ppermute(block, MESH_AXES, pairs)  32.3 us
    all_to_all x1, blocking collectives, shards(): sums = lax.all_to_all(sums, 'prow', 0, 0)  17.7 us
    all_to_all x1, waiting for transfers between devices, shards(): rows_in = lax.all_to_all(rows_out, 'prow', 0, 0)  12.7 us
    all_to_all x1, waiting for transfers between devices, shards(): spread_low = lax.all_to_all(spread_low, 'prow', 0, 0)  12.2 us
    pallas_call x2, Pallas kernels, level_one(): call(body, shapes, [SMEM] + [HBM] * 9 + [VMEM] * (1 + len(more)), [pltpu....  10.8 us
    pallas_call x1, Pallas kernels, kids(): call(kids_body, [jax.ShapeDtypeStruct((HALF, 2 * B), F32)] * 2, [SMEM] +...  10.3 us
    all_to_all x1, waiting for transfers between devices, shards(): got = lax.all_to_all(packed, 'pcol', 0, 0)  7.22 us
  transfers between devices with their start and end apart: 30, of which 16 were waited for; matrix products, arithmetic and copies ran while one was open for 2% of the time, Pallas kernels for 13%

profile of v5, /device:TPU:0, one launch (start us, length us, event | category | flops | bytes accessed | tf_op | source)
XLA Modules:
  0.0 197.0 jit_solution(9878219550875438908)
XLA Ops:
  0.7 1.4 dynamic-slice_bitcast_fusion
  2.1 0.1 collective-permute-start
  2.2 0.2 copy-done.7
  2.4 1.2 shard_map.129
  3.6 5.6 %all-to-all-start = ((bf16[8,3,4,32,256]{4,3,2,1,0:T(8,128)(2,1)}), bf16[8,3,4,32,256]{4,3,2,1,0:T(8,128)(2,1)}, u32[]{:S(2)}, u32[]{:S(2)}) async-start(bf16[8,3,4,32,256]{4,3,2,1,0:T(8,128)(2,1)} %shard_map.129), calls=%async_computation | async-start | bytes 3145728 | tf_op jit(solution)/shard_map/all_to_all | solution.py:400
  9.2 0.7 copy.14.select
  9.9 0.6 pad_add_fusion.place
  10.5 2.2 %shard_map.128.tab.tab_ref = s32[123]{0:T(128)} custom-call(s32[2]{0:T(128)} %pad_add_fusion.place, s32[16,16]{1,0:T(8,128)} %struct.1, s32[32,8]{1,0:T(8,128)} %copy.14.select, s32[32]{0:T(128)} %parent.3), custom_call_target="tpu_custom_call" | custom-call | tf_op jit(solution)/shard_map/pallas_call | solution.py:385
  12.7 0.1 pad_maximum_fusion.refs_0_
  12.8 2.0 %collective-permute-start.1 = (bf16[2,512,512]{2,1,0:T(8,128)(2,1)S(1)}, bf16[2,512,512]{2,1,0:T(8,128)(2,1)S(1)}, u32[]{:S(2)}, u32[]{:S(2)}) collective-permute-start(bf16[2,512,512]{2,1,0:T(8,128)(2,1)S(1)} %pad_maximum_fusion.refs_0_), channel_id=1, source_target_pairs={{0,4},{1,5},{2,6},{3,7},{4,8},{5,9},{6,10},{7,11},{8,12},{9,13},{1... | collective-permute-start | bytes 3145736 | tf_op jit(solution)/shard_map/ppermute | solution.py:37
  14.8 2.2 %collective-permute-start.2 = (bf16[2,512,512]{2,1,0:T(8,128)(2,1)S(1)}, bf16[2,512,512]{2,1,0:T(8,128)(2,1)}, u32[]{:S(2)}, u32[]{:S(2)}) collective-permute-start(bf16[2,512,512]{2,1,0:T(8,128)(2,1)S(1)} %pad_maximum_fusion.refs_0_), channel_id=1, source_target_pairs={{0,12},{1,13},{2,14},{3,15},{4,0},{5,1},{6,2},{7,3},{8,4},{9,5},{1... | collective-permute-start | bytes 3145736 | tf_op jit(solution)/shard_map/ppermute | solution.py:37
  17.1 2.8 %collective-permute-start.5 = (bf16[2,512,512]{2,1,0:T(8,128)(2,1)S(1)}, bf16[2,512,512]{2,1,0:T(8,128)(2,1)}, u32[]{:S(2)}, u32[]{:S(2)}) collective-permute-start(bf16[2,512,512]{2,1,0:T(8,128)(2,1)S(1)} %pad_maximum_fusion.refs_0_), channel_id=1, source_target_pairs={{0,2},{1,3},{2,0},{3,1},{4,6},{5,7},{6,4},{7,5},{8,10},{9,11},{10,... | collective-permute-start | bytes 3145736 | tf_op jit(solution)/shard_map/ppermute | solution.py:37
  19.9 12.2 %all-to-all-done = bf16[8,3,4,32,256]{4,3,2,1,0:T(8,128)(2,1)} async-done(((bf16[8,3,4,32,256]{4,3,2,1,0:T(8,128)(2,1)}), bf16[8,3,4,32,256]{4,3,2,1,0:T(8,128)(2,1)}, u32[]{:S(2)}, u32[]{:S(2)}) %all-to-all-start) | async-done | bytes 1572896 | tf_op jit(solution)/shard_map/all_to_all | solution.py:400
  32.1 8.2 %collective-permute-done.1.refs_3_ = bf16[2,512,512]{2,1,0:T(8,128)(2,1)S(1)} collective-permute-done((bf16[2,512,512]{2,1,0:T(8,128)(2,1)S(1)}, bf16[2,512,512]{2,1,0:T(8,128)(2,1)S(1)}, u32[]{:S(2)}, u32[]{:S(2)}) %collective-permute-start.1) | collective-permute-done | bytes 1048608 | tf_op jit(solution)/shard_map/ppermute | solution.py:37
  40.3 1.4 collective-permute-start.4
  41.6 1.5 shard_map.130.refs_0_
  43.1 1.8 collective-permute-start.7
  44.9 1.5 collective-permute-start.9
  46.4 1.8 collective-permute-start.6
  48.1 8.7 %collective-permute-done.7.refs_3_ = bf16[32,32,256]{2,1,0:T(8,128)(2,1)S(1)} collective-permute-done((bf16[32,32,256]{2,1,0:T(8,128)(2,1)S(1)}, bf16[32,32,256]{2,1,0:T(8,128)(2,1)S(1)}, u32[]{:S(2)}, u32[]{:S(2)}) %collective-permute-start.7) | collective-permute-done | bytes 524320 | tf_op jit(solution)/shard_map/ppermute | solution.py:37
  56.8 0.2 collective-permute-start.8
  57.0 6.5 %collective-permute-done.9.refs_4_ = bf16[32,32,256]{2,1,0:T(8,128)(2,1)S(1)} collective-permute-done((bf16[32,32,256]{2,1,0:T(8,128)(2,1)S(1)}, bf16[32,32,256]{2,1,0:T(8,128)(2,1)S(1)}, u32[]{:S(2)}, u32[]{:S(2)}) %collective-permute-start.9) | collective-permute-done | bytes 524320 | tf_op jit(solution)/shard_map/ppermute | solution.py:37
  63.6 1.8 collective-permute-start.10
  65.3 4.0 %collective-permute-start.13 = (bf16[2,512,512]{2,1,0:T(8,128)(2,1)}, bf16[2,512,512]{2,1,0:T(8,128)(2,1)S(1)}, u32[]{:S(2)}, u32[]{:S(2)}) collective-permute-start(bf16[2,512,512]{2,1,0:T(8,128)(2,1)} %collective-permute-done.5.refs_4_), channel_id=1, source_target_pairs={{0,12},{1,13},{2,14},{3,15},{4,0},{5,1},{6,2},{7,3},{8,4},{9,5},{1... | collective-permute-start | bytes 3145736 | tf_op jit(solution)/shard_map/ppermute | solution.py:37
  69.4 2.8 %collective-permute-start.15 = (bf16[2,512,512]{2,1,0:T(8,128)(2,1)S(1)}, bf16[2,512,512]{2,1,0:T(8,128)(2,1)S(1)}, u32[]{:S(2)}, u32[]{:S(2)}) collective-permute-start(bf16[2,512,512]{2,1,0:T(8,128)(2,1)S(1)} %collective-permute-done.4.refs_2_), channel_id=1, source_target_pairs={{0,2},{1,3},{2,0},{3,1},{4,6},{5,7},{6,4},{7,5},{8,10},{9,11},{10,... | collective-permute-start | bytes 3145736 | tf_op jit(solution)/shard_map/ppermute | solution.py:37
  72.2 0.2 collective-permute-start.12
  72.5 4.1 %collective-permute-done.10.refs_5_ = bf16[32,32,256]{2,1,0:T(8,128)(2,1)S(1)} collective-permute-done((bf16[32,32,256]{2,1,0:T(8,128)(2,1)S(1)}, bf16[32,32,256]{2,1,0:T(8,128)(2,1)S(1)}, u32[]{:S(2)}, u32[]{:S(2)}) %collective-permute-start.10) | collective-permute-done | bytes 524320 | tf_op jit(solution)/shard_map/ppermute | solution.py:37
  76.6 3.0 %collective-permute-start.11 = (bf16[32,32,256]{2,1,0:T(8,128)(2,1)S(1)}, bf16[32,32,256]{2,1,0:T(8,128)(2,1)S(1)}, u32[]{:S(2)}, u32[]{:S(2)}) collective-permute-start(bf16[32,32,256]{2,1,0:T(8,128)(2,1)S(1)} %collective-permute-done.10.refs_5_), channel_id=1, source_target_pairs={{0,96},{1,97},{2,98},{3,99},{4,100},{5,101},{6,102},{7,103},{8,104... | collective-permute-start | bytes 1572872 | tf_op jit(solution)/shard_map/ppermute | solution.py:37
  79.6 6.0 %collective-permute-done.12.refs_7_ = bf16[32,32,256]{2,1,0:T(8,128)(2,1)S(1)} collective-permute-done((bf16[32,32,256]{2,1,0:T(8,128)(2,1)S(1)}, bf16[32,32,256]{2,1,0:T(8,128)(2,1)S(1)}, u32[]{:S(2)}, u32[]{:S(2)}) %collective-permute-start.12) | collective-permute-done | bytes 524320 | tf_op jit(solution)/shard_map/ppermute | solution.py:37
  85.6 3.6 %collective-permute-done.11.refs_6_ = bf16[32,32,256]{2,1,0:T(8,128)(2,1)S(1)} collective-permute-done((bf16[32,32,256]{2,1,0:T(8,128)(2,1)S(1)}, bf16[32,32,256]{2,1,0:T(8,128)(2,1)S(1)}, u32[]{:S(2)}, u32[]{:S(2)}) %collective-permute-start.11) | collective-permute-done | bytes 524320 | tf_op jit(solution)/shard_map/ppermute | solution.py:37
  89.2 2.4 %shard_map.131 = (bf16[16,256,256]{2,1,0:T(8,128)(2,1)S(1)}, bf16[16,256,256]{2,1,0:T(8,128)(2,1)}) custom-call(s32[123]{0:T(128)S(1)} %copy-done.12, bf16[32,32,256]{2,1,0:T(8,128)(2,1)S(1)} %shard_map.130.refs_0_, bf16[32,32,256]{2,1,0:T(8,128)(2,1)S(1)} %collective-permute-done.6.refs_1_, bf16[32,32,256]{2,1,0:T(8,128)(2,1)S(1)} %collective-permute-done.8.refs_2_, ...), custom_call_target="tpu_custom_call" | custom-call | tf_op jit(solution)/shard_map/pallas_call | solution.py:151
  91.6 2.9 %collective-permute-done.14.refs_7_ = bf16[2,512,512]{2,1,0:T(8,128)(2,1)S(1)} collective-permute-done((bf16[2,512,512]{2,1,0:T(8,128)(2,1)}, bf16[2,512,512]{2,1,0:T(8,128)(2,1)S(1)}, u32[]{:S(2)}, u32[]{:S(2)}) %collective-permute-start.14) | collective-permute-done | bytes 1048608 | tf_op jit(solution)/shard_map/ppermute | solution.py:37
  94.5 0.2 collective-permute-done.15.refs_6_
  94.7 5.3 %shard_map.132 = (bf16[512,256]{1,0:T(8,128)(2,1)S(1)}, f32[4,32,256]{2,1,0:T(8,128)S(1)}, f32[4,32,256]{2,1,0:T(8,128)}) custom-call(s32[123]{0:T(128)S(1)} %copy-done.12, bf16[2,512,512]{2,1,0:T(8,128)(2,1)S(1)} %pad_maximum_fusion.refs_0_, bf16[2,512,512]{2,1,0:T(8,128)(2,1)} %collective-permute-done.2.refs_1_, ...), custom_call_target="tpu_custom_call" | custom-call | flops 1073741824 | bytes 12582912 | tf_op jit(solution)/shard_map/pallas_call | solution.py:235
  100.0 5.5 %shard_map.133 = (bf16[512,256]{1,0:T(8,128)(2,1)S(1)}, f32[4,32,256]{2,1,0:T(8,128)S(1)}, f32[4,32,256]{2,1,0:T(8,128)}, bf16[16,2,32,256]{3,2,1,0:T(8,128)(2,1)}) custom-call(s32[123]{0:T(128)S(1)} %copy-done.12, bf16[2,512,512]{2,1,0:T(8,128)(2,1)S(1)} %pad_maximum_fusion.refs_0_, bf16[2,512,512]{2,1,0:T(8,128)(2,1)} %collective-permute-done.2.refs_1_, ...), custom_call_target="tpu_custom_call" | custom-call | flops 1073741824 | bytes 12582912 | tf_op jit(solution)/shard_map/pallas_call | solution.py:235
  105.6 0.7 copy-done.15
  106.3 0.3 collective-permute-start.18
  106.5 0.9 collective-permute-start.21
  107.5 0.7 collective-permute-start.22
  108.1 0.6 collective-permute-start.20
  108.7 6.6 %all-to-all-start.1 = ((bf16[16,2,32,256]{3,2,1,0:T(8,128)(2,1)}), bf16[16,2,32,256]{3,2,1,0:T(8,128)(2,1)S(1)}, u32[]{:S(2)}, u32[]{:S(2)}) async-start(bf16[16,2,32,256]{3,2,1,0:T(8,128)(2,1)} %get-tuple-element.54), calls=%async_computation.1 | async-start | bytes 1048576 | tf_op jit(solution)/shard_map/all_to_all | solution.py:437
  115.4 0.3 collective-permute-start.23
  115.7 3.2 %collective-permute-start.24 = (f32[32,256]{1,0:T(8,128)S(1)}, f32[32,256]{1,0:T(8,128)S(1)}, u32[]{:S(2)}, u32[]{:S(2)}) collective-permute-start(f32[32,256]{1,0:T(8,128)S(1)} %get-tuple-element.76), channel_id=1, source_target_pairs={{0,64},{1,65},{2,66},{3,67},{4,68},{5,69},{6,70},{7,71},{8,72},{9,... | collective-permute-start | bytes 98312 | tf_op jit(solution)/shard_map/ppermute | solution.py:37
  118.9 0.2 collective-permute-start.25
  119.1 1.9 collective-permute-done.23.refs_1_
  121.0 0.4 collective-permute-done.24.refs_2_
  121.3 1.5 collective-permute-done.25.refs_3_
  122.8 4.9 %all-to-all-done.1.spread = bf16[16,2,32,256]{3,2,1,0:T(8,128)(2,1)S(1)} async-done(((bf16[16,2,32,256]{3,2,1,0:T(8,128)(2,1)}), bf16[16,2,32,256]{3,2,1,0:T(8,128)(2,1)S(1)}, u32[]{:S(2)}, u32[]{:S(2)}) %all-to-all-start.1) | async-done | bytes 524320 | tf_op jit(solution)/shard_map/all_to_all | solution.py:437
  127.7 1.9 shard_map.135
  129.6 3.7 %all-to-all-start.2 = ((bf16[16,160,256]{2,1,0:T(8,128)(2,1)}), bf16[16,160,256]{2,1,0:T(8,128)(2,1)S(1)}, u32[]{:S(2)}, u32[]{:S(2)}) async-start(bf16[16,160,256]{2,1,0:T(8,128)(2,1)} %get-tuple-element.62), calls=%async_computation.2 | async-start | bytes 2621440 | tf_op jit(solution)/shard_map/all_to_all | solution.py:456
  133.4 10.3 %shard_map.134 = (f32[512,512]{1,0:T(8,128)}, f32[512,512]{1,0:T(8,128)}) custom-call(s32[123]{0:T(128)} %shard_map.128.tab.tab_ref, bf16[2,512,512]{2,1,0:T(8,128)(2,1)} %copy-done.1, bf16[2,512,512]{2,1,0:T(8,128)(2,1)} %collective-permute-done.2.refs_1_, bf16[2,512,512]{2,1,0:T(8,128)(2,1)} %copy-done.3, bf16[2,512,512]{2,1,0:T(8,128)(2,1)} %copy-done.2, ...), custom_call_target="tpu_custom_call" | custom-call | flops 2147483648 | bytes 16777216 | tf_op jit(solution)/shard_map/pallas_call | solution.py:272
  143.7 0.4 collective-permute-start.19
  144.0 0.2 collective-permute-start.17
  144.3 1.0 constant_dynamic-slice_fusion.link
  145.2 1.7 collective-permute-done.17
  146.9 7.2 %all-to-all-done.2.got = bf16[16,160,256]{2,1,0:T(8,128)(2,1)S(1)} async-done(((bf16[16,160,256]{2,1,0:T(8,128)(2,1)}), bf16[16,160,256]{2,1,0:T(8,128)(2,1)S(1)}, u32[]{:S(2)}, u32[]{:S(2)}) %all-to-all-start.2) | async-done | bytes 1310752 | tf_op jit(solution)/shard_map/all_to_all | solution.py:456
  154.2 1.2 copy-done.10
  155.4 3.6 %shard_map.136 = (bf16[1024,512]{1,0:T(8,128)(2,1)}, f32[8,64,512]{2,1,0:T(8,128)S(1)}) custom-call(s32[123]{0:T(128)S(1)} %copy-done.13, bf16[16,160,256]{2,1,0:T(8,128)(2,1)S(1)} %all-to-all-done.2.got, f32[512,512]{1,0:T(8,128)S(1)} %copy-done.10, f32[512,512]{1,0:T(8,128)} %collective-permute-done.19.part_sib, bf16[1024,512]{1,0:T(8,128)(2,1)S(1)} %copy-done.8, ...), custom_call_target="tpu_custom_call" | custom-call | tf_op jit(solution)/shard_map/pallas_call | solution.py:457
  159.0 17.7 %all_to_all.25.sums = f32[8,64,512]{2,1,0:T(8,128)S(1)} all-to-all(f32[8,64,512]{2,1,0:T(8,128)S(1)} %get-tuple-element.65), channel_id=1, replica_groups=mesh['prow'=8,'pcol'=16] {'prow'}, dimensions={0} | all-to-all | bytes 2097152 | tf_op jit(solution)/shard_map/all_to_all | solution.py:463
  176.6 1.7 shard_map.137
  178.4 3.7 %all-to-all-start.4 = ((bf16[8,128,512]{2,1,0:T(8,128)(2,1)}), bf16[8,128,512]{2,1,0:T(8,128)(2,1)S(1)}, u32[]{:S(2)}, u32[]{:S(2)}) async-start(bf16[8,128,512]{2,1,0:T(8,128)(2,1)} %shard_map.137), calls=%async_computation.4 | async-start | bytes 2097152 | tf_op jit(solution)/shard_map/all_to_all | solution.py:469
  182.1 1.0 constant_dynamic-update-slice_fusion
  183.1 12.7 %all-to-all-done.4.got = bf16[8,128,512]{2,1,0:T(8,128)(2,1)S(1)} async-done(((bf16[8,128,512]{2,1,0:T(8,128)(2,1)}), bf16[8,128,512]{2,1,0:T(8,128)(2,1)S(1)}, u32[]{:S(2)}, u32[]{:S(2)}) %all-to-all-start.4) | async-done | bytes 1048608 | tf_op jit(solution)/shard_map/all_to_all | solution.py:469
  195.8 1.2 shard_map.138
  (58 shorter events, 0.4 us)
Async XLA Ops:
  0.6 118.5 %copy-start = (f32[256,256]{1,0:T(8,128)S(1)}, f32[256,256]{1,0:T(8,128)}, u32[]{:S(2)}) copy-start(f32[256,256]{1,0:T(8,128)} %param.13) | copy-start | bytes 786436
  0.6 1.5 copy-start.9
  0.7 1.7 copy-start.7
  2.1 10.6 %collective-permute-start = (bf16[512,512]{1,0:T(8,128)(2,1)S(1)}, bf16[512,512]{1,0:T(8,128)(2,1)S(1)}, u32[]{:S(2)}, u32[]{:S(2)}) collective-permute-start(bf16[512,512]{1,0:T(8,128)(2,1)S(1)} %get-tuple-element.72), channel_id=1, source_target_pairs={{0,1},{1,0},{2,3},{3,2},{4,5},{5,4},{6,7},{7,6},{8,9},{9,8},{10,11... | collective-permute-start | bytes 1572872 | tf_op jit(solution)/shard_map/ppermute | solution.py:37
  3.6 5.6 %copy-start.18 = (s32[32,8]{0,1:T(8,128)S(1)}, s32[32,8]{0,1:T(8,128)}, u32[]{:S(2)}) copy-start(s32[32,8]{0,1:T(8,128)} %param.16) | copy-start | bytes 3076
  3.6 28.5 %all-to-all-start = ((bf16[8,3,4,32,256]{4,3,2,1,0:T(8,128)(2,1)}), bf16[8,3,4,32,256]{4,3,2,1,0:T(8,128)(2,1)}, u32[]{:S(2)}, u32[]{:S(2)}) async-start(bf16[8,3,4,32,256]{4,3,2,1,0:T(8,128)(2,1)} %shard_map.129), calls=%async_computation | async-start | bytes 3145728 | tf_op jit(solution)/shard_map/all_to_all | solution.py:400
  12.7 29.0 %copy-start.12 = (s32[123]{0:T(128)S(1)}, s32[123]{0:T(128)}, u32[]{:S(2)}) copy-start(s32[123]{0:T(128)} %shard_map.128.tab.tab_ref) | copy-start | bytes 1480
  12.8 87.2 %copy-start.1 = (bf16[2,512,512]{2,1,0:T(8,128)(2,1)}, bf16[2,512,512]{2,1,0:T(8,128)(2,1)S(1)}, u32[]{:S(2)}) copy-start(bf16[2,512,512]{2,1,0:T(8,128)(2,1)S(1)} %pad_maximum_fusion.refs_0_) | copy-start | bytes 3145732
  12.8 27.5 %collective-permute-start.1 = (bf16[2,512,512]{2,1,0:T(8,128)(2,1)S(1)}, bf16[2,512,512]{2,1,0:T(8,128)(2,1)S(1)}, u32[]{:S(2)}, u32[]{:S(2)}) collective-permute-start(bf16[2,512,512]{2,1,0:T(8,128)(2,1)S(1)} %pad_maximum_fusion.refs_0_), channel_id=1, source_target_pairs={{0,4},{1,5},{2,6},{3,7},{4,8},{5,9},{6,10},{7,11},{8,12},{9,13},{1... | collective-permute-start | bytes 3145736 | tf_op jit(solution)/shard_map/ppermute | solution.py:37
  14.8 25.5 %collective-permute-start.2 = (bf16[2,512,512]{2,1,0:T(8,128)(2,1)S(1)}, bf16[2,512,512]{2,1,0:T(8,128)(2,1)}, u32[]{:S(2)}, u32[]{:S(2)}) collective-permute-start(bf16[2,512,512]{2,1,0:T(8,128)(2,1)S(1)} %pad_maximum_fusion.refs_0_), channel_id=1, source_target_pairs={{0,12},{1,13},{2,14},{3,15},{4,0},{5,1},{6,2},{7,3},{8,4},{9,5},{1... | collective-permute-start | bytes 3145736 | tf_op jit(solution)/shard_map/ppermute | solution.py:37
  17.0 2.9 %collective-permute-start.3 = (bf16[512,256]{1,0:T(8,128)(2,1)S(1)}, bf16[512,256]{1,0:T(8,128)(2,1)S(1)}, u32[]{:S(2)}, u32[]{:S(2)}) collective-permute-start(bf16[512,256]{1,0:T(8,128)(2,1)S(1)} %get-tuple-element.74), channel_id=1, source_target_pairs={{0,1},{1,0},{2,3},{3,2},{4,5},{5,4},{6,7},{7,6},{8,9},{9,8},{10,11... | collective-permute-start | bytes 786440 | tf_op jit(solution)/shard_map/ppermute | solution.py:37
  17.1 48.2 %collective-permute-start.5 = (bf16[2,512,512]{2,1,0:T(8,128)(2,1)S(1)}, bf16[2,512,512]{2,1,0:T(8,128)(2,1)}, u32[]{:S(2)}, u32[]{:S(2)}) collective-permute-start(bf16[2,512,512]{2,1,0:T(8,128)(2,1)S(1)} %pad_maximum_fusion.refs_0_), channel_id=1, source_target_pairs={{0,2},{1,3},{2,0},{3,1},{4,6},{5,7},{6,4},{7,5},{8,10},{9,11},{10,... | collective-permute-start | bytes 3145736 | tf_op jit(solution)/shard_map/ppermute | solution.py:37
  40.3 59.7 %copy-start.2 = (bf16[2,512,512]{2,1,0:T(8,128)(2,1)}, bf16[2,512,512]{2,1,0:T(8,128)(2,1)S(1)}, u32[]{:S(2)}) copy-start(bf16[2,512,512]{2,1,0:T(8,128)(2,1)S(1)} %collective-permute-done.1.refs_3_) | copy-start | bytes 3145732
  40.3 29.1 %collective-permute-start.4 = (bf16[2,512,512]{2,1,0:T(8,128)(2,1)S(1)}, bf16[2,512,512]{2,1,0:T(8,128)(2,1)S(1)}, u32[]{:S(2)}, u32[]{:S(2)}) collective-permute-start(bf16[2,512,512]{2,1,0:T(8,128)(2,1)S(1)} %collective-permute-done.1.refs_3_), channel_id=1, source_target_pairs={{0,4},{1,5},{2,6},{3,7},{4,8},{5,9},{6,10},{7,11},{8,12},{9,13},{1... | collective-permute-start | bytes 3145736 | tf_op jit(solution)/shard_map/ppermute | solution.py:37
  43.1 13.7 %collective-permute-start.7 = (bf16[32,32,256]{2,1,0:T(8,128)(2,1)S(1)}, bf16[32,32,256]{2,1,0:T(8,128)(2,1)S(1)}, u32[]{:S(2)}, u32[]{:S(2)}) collective-permute-start(bf16[32,32,256]{2,1,0:T(8,128)(2,1)S(1)} %shard_map.130.refs_0_), channel_id=1, source_target_pairs={{0,32},{1,33},{2,34},{3,35},{4,36},{5,37},{6,38},{7,39},{8,40},{9,... | collective-permute-start | bytes 1572872 | tf_op jit(solution)/shard_map/ppermute | solution.py:37
  44.9 18.7 %collective-permute-start.9 = (bf16[32,32,256]{2,1,0:T(8,128)(2,1)S(1)}, bf16[32,32,256]{2,1,0:T(8,128)(2,1)S(1)}, u32[]{:S(2)}, u32[]{:S(2)}) collective-permute-start(bf16[32,32,256]{2,1,0:T(8,128)(2,1)S(1)} %shard_map.130.refs_0_), channel_id=1, source_target_pairs={{0,16},{1,17},{2,18},{3,19},{4,20},{5,21},{6,22},{7,23},{8,24},{9,... | collective-permute-start | bytes 1572872 | tf_op jit(solution)/shard_map/ppermute | solution.py:37
  46.4 23.0 %collective-permute-start.6 = (bf16[32,32,256]{2,1,0:T(8,128)(2,1)S(1)}, bf16[32,32,256]{2,1,0:T(8,128)(2,1)S(1)}, u32[]{:S(2)}, u32[]{:S(2)}) collective-permute-start(bf16[32,32,256]{2,1,0:T(8,128)(2,1)S(1)} %shard_map.130.refs_0_), channel_id=1, source_target_pairs={{0,96},{1,97},{2,98},{3,99},{4,100},{5,101},{6,102},{7,103},{8,104... | collective-permute-start | bytes 1572872 | tf_op jit(solution)/shard_map/ppermute | solution.py:37
  56.8 15.4 %collective-permute-start.8 = (bf16[32,32,256]{2,1,0:T(8,128)(2,1)S(1)}, bf16[32,32,256]{2,1,0:T(8,128)(2,1)S(1)}, u32[]{:S(2)}, u32[]{:S(2)}) collective-permute-start(bf16[32,32,256]{2,1,0:T(8,128)(2,1)S(1)} %collective-permute-done.7.refs_3_), channel_id=1, source_target_pairs={{0,32},{1,33},{2,34},{3,35},{4,36},{5,37},{6,38},{7,39},{8,40},{9,... | collective-permute-start | bytes 1572872 | tf_op jit(solution)/shard_map/ppermute | solution.py:37
  63.6 13.0 %collective-permute-start.10 = (bf16[32,32,256]{2,1,0:T(8,128)(2,1)S(1)}, bf16[32,32,256]{2,1,0:T(8,128)(2,1)S(1)}, u32[]{:S(2)}, u32[]{:S(2)}) collective-permute-start(bf16[32,32,256]{2,1,0:T(8,128)(2,1)S(1)} %collective-permute-done.9.refs_4_), channel_id=1, source_target_pairs={{0,96},{1,97},{2,98},{3,99},{4,100},{5,101},{6,102},{7,103},{8,104... | collective-permute-start | bytes 1572872 | tf_op jit(solution)/shard_map/ppermute | solution.py:37
  65.3 26.2 %collective-permute-start.13 = (bf16[2,512,512]{2,1,0:T(8,128)(2,1)}, bf16[2,512,512]{2,1,0:T(8,128)(2,1)S(1)}, u32[]{:S(2)}, u32[]{:S(2)}) collective-permute-start(bf16[2,512,512]{2,1,0:T(8,128)(2,1)} %collective-permute-done.5.refs_4_), channel_id=1, source_target_pairs={{0,12},{1,13},{2,14},{3,15},{4,0},{5,1},{6,2},{7,3},{8,4},{9,5},{1... | collective-permute-start | bytes 3145736 | tf_op jit(solution)/shard_map/ppermute | solution.py:37
  69.4 25.1 %collective-permute-start.14 = (bf16[2,512,512]{2,1,0:T(8,128)(2,1)}, bf16[2,512,512]{2,1,0:T(8,128)(2,1)S(1)}, u32[]{:S(2)}, u32[]{:S(2)}) collective-permute-start(bf16[2,512,512]{2,1,0:T(8,128)(2,1)} %collective-permute-done.5.refs_4_), channel_id=1, source_target_pairs={{0,4},{1,5},{2,6},{3,7},{4,8},{5,9},{6,10},{7,11},{8,12},{9,13},{1... | collective-permute-start | bytes 3145736 | tf_op jit(solution)/shard_map/ppermute | solution.py:37
  69.4 30.6 %copy-start.3 = (bf16[2,512,512]{2,1,0:T(8,128)(2,1)}, bf16[2,512,512]{2,1,0:T(8,128)(2,1)S(1)}, u32[]{:S(2)}) copy-start(bf16[2,512,512]{2,1,0:T(8,128)(2,1)S(1)} %collective-permute-done.4.refs_2_) | copy-start | bytes 3145732
  69.4 25.3 %collective-permute-start.15 = (bf16[2,512,512]{2,1,0:T(8,128)(2,1)S(1)}, bf16[2,512,512]{2,1,0:T(8,128)(2,1)S(1)}, u32[]{:S(2)}, u32[]{:S(2)}) collective-permute-start(bf16[2,512,512]{2,1,0:T(8,128)(2,1)S(1)} %collective-permute-done.4.refs_2_), channel_id=1, source_target_pairs={{0,2},{1,3},{2,0},{3,1},{4,6},{5,7},{6,4},{7,5},{8,10},{9,11},{10,... | collective-permute-start | bytes 3145736 | tf_op jit(solution)/shard_map/ppermute | solution.py:37
  72.2 13.4 %collective-permute-start.12 = (bf16[32,32,256]{2,1,0:T(8,128)(2,1)S(1)}, bf16[32,32,256]{2,1,0:T(8,128)(2,1)S(1)}, u32[]{:S(2)}, u32[]{:S(2)}) collective-permute-start(bf16[32,32,256]{2,1,0:T(8,128)(2,1)S(1)} %collective-permute-done.9.refs_4_), channel_id=1, source_target_pairs={{0,32},{1,33},{2,34},{3,35},{4,36},{5,37},{6,38},{7,39},{8,40},{9,... | collective-permute-start | bytes 1572872 | tf_op jit(solution)/shard_map/ppermute | solution.py:37
  76.6 12.6 %collective-permute-start.11 = (bf16[32,32,256]{2,1,0:T(8,128)(2,1)S(1)}, bf16[32,32,256]{2,1,0:T(8,128)(2,1)S(1)}, u32[]{:S(2)}, u32[]{:S(2)}) collective-permute-start(bf16[32,32,256]{2,1,0:T(8,128)(2,1)S(1)} %collective-permute-done.10.refs_5_), channel_id=1, source_target_pairs={{0,96},{1,97},{2,98},{3,99},{4,100},{5,101},{6,102},{7,103},{8,104... | collective-permute-start | bytes 1572872 | tf_op jit(solution)/shard_map/ppermute | solution.py:37
  91.5 8.5 %copy-start.4 = (bf16[2,512,512]{2,1,0:T(8,128)(2,1)}, bf16[2,512,512]{2,1,0:T(8,128)(2,1)S(1)}, u32[]{:S(2)}) copy-start(bf16[2,512,512]{2,1,0:T(8,128)(2,1)S(1)} %collective-permute-done.13.refs_5_) | copy-start | bytes 3145732
  94.5 5.5 %copy-start.5 = (bf16[2,512,512]{2,1,0:T(8,128)(2,1)}, bf16[2,512,512]{2,1,0:T(8,128)(2,1)S(1)}, u32[]{:S(2)}) copy-start(bf16[2,512,512]{2,1,0:T(8,128)(2,1)S(1)} %collective-permute-done.14.refs_7_) | copy-start | bytes 3145732
  94.7 5.4 %copy-start.6 = (bf16[2,512,512]{2,1,0:T(8,128)(2,1)}, bf16[2,512,512]{2,1,0:T(8,128)(2,1)S(1)}, u32[]{:S(2)}) copy-start(bf16[2,512,512]{2,1,0:T(8,128)(2,1)S(1)} %collective-permute-done.15.refs_6_) | copy-start | bytes 3145732
  94.7 5.3 %collective-permute-start.16 = (bf16[16,256,256]{2,1,0:T(8,128)(2,1)S(1)}, bf16[16,256,256]{2,1,0:T(8,128)(2,1)S(1)}, u32[]{:S(2)}, u32[]{:S(2)}) collective-permute-start(bf16[16,256,256]{2,1,0:T(8,128)(2,1)S(1)} %get-tuple-element.49.refs_8_), channel_id=1, source_target_pairs={{0,1},{1,0},{2,3},{3,2},{4,5},{5,4},{6,7},{7,6},{8,9},{9,8},{10,11... | collective-permute-start | bytes 6291464 | tf_op jit(solution)/shard_map/ppermute | solution.py:37
  100.0 27.7 %copy-start.14 = (s32[32]{0:T(128)S(1)}, s32[32]{0:T(128)}, u32[]{:S(2)}) copy-start(s32[32]{0:T(128)} %parent.3) | copy-start | bytes 388
  105.6 0.7 copy-start.15
  106.3 27.1 %collective-permute-start.18 = (bf16[16,256,256]{2,1,0:T(8,128)(2,1)}, bf16[16,256,256]{2,1,0:T(8,128)(2,1)}, u32[]{:S(2)}, u32[]{:S(2)}) collective-permute-start(bf16[16,256,256]{2,1,0:T(8,128)(2,1)} %get-tuple-element.55.refs_8_), channel_id=1, source_target_pairs={{0,1},{1,0},{2,3},{3,2},{4,5},{5,4},{6,7},{7,6},{8,9},{9,8},{10,11... | collective-permute-start | bytes 6291464 | tf_op jit(solution)/shard_map/ppermute | solution.py:37
  106.5 8.8 %collective-permute-start.21 = (f32[4,32,256]{2,1,0:T(8,128)}, f32[4,32,256]{2,1,0:T(8,128)S(1)}, u32[]{:S(2)}, u32[]{:S(2)}) collective-permute-start(f32[4,32,256]{2,1,0:T(8,128)} %get-tuple-element.60), channel_id=1, source_target_pairs={{0,16},{1,17},{2,18},{3,19},{4,20},{5,21},{6,22},{7,23},{8,24},{9,... | collective-permute-start | bytes 393224 | tf_op jit(solution)/shard_map/ppermute | solution.py:37
  107.5 7.9 %collective-permute-start.22 = (f32[4,32,256]{2,1,0:T(8,128)}, f32[4,32,256]{2,1,0:T(8,128)S(1)}, u32[]{:S(2)}, u32[]{:S(2)}) collective-permute-start(f32[4,32,256]{2,1,0:T(8,128)} %get-tuple-element.61), channel_id=1, source_target_pairs={{0,17},{1,16},{2,19},{3,18},{4,21},{5,20},{6,23},{7,22},{8,25},{9,... | collective-permute-start | bytes 393224 | tf_op jit(solution)/shard_map/ppermute | solution.py:37
  108.1 7.2 %collective-permute-start.20 = (f32[4,32,256]{2,1,0:T(8,128)S(1)}, f32[4,32,256]{2,1,0:T(8,128)S(1)}, u32[]{:S(2)}, u32[]{:S(2)}) collective-permute-start(f32[4,32,256]{2,1,0:T(8,128)S(1)} %get-tuple-element.59), channel_id=1, source_target_pairs={{0,1},{1,0},{2,3},{3,2},{4,5},{5,4},{6,7},{7,6},{8,9},{9,8},{10,11... | collective-permute-start | bytes 393224 | tf_op jit(solution)/shard_map/ppermute | solution.py:37
  108.7 19.0 %all-to-all-start.1 = ((bf16[16,2,32,256]{3,2,1,0:T(8,128)(2,1)}), bf16[16,2,32,256]{3,2,1,0:T(8,128)(2,1)S(1)}, u32[]{:S(2)}, u32[]{:S(2)}) async-start(bf16[16,2,32,256]{3,2,1,0:T(8,128)(2,1)} %get-tuple-element.54), calls=%async_computation.1 | async-start | bytes 1048576 | tf_op jit(solution)/shard_map/all_to_all | solution.py:437
  115.4 5.5 %collective-permute-start.23 = (f32[32,256]{1,0:T(8,128)S(1)}, f32[32,256]{1,0:T(8,128)S(1)}, u32[]{:S(2)}, u32[]{:S(2)}) collective-permute-start(f32[32,256]{1,0:T(8,128)S(1)} %get-tuple-element.77), channel_id=1, source_target_pairs={{0,32},{1,33},{2,34},{3,35},{4,36},{5,37},{6,38},{7,39},{8,40},{9,... | collective-permute-start | bytes 98312 | tf_op jit(solution)/shard_map/ppermute | solution.py:37
  115.7 5.6 %collective-permute-start.24 = (f32[32,256]{1,0:T(8,128)S(1)}, f32[32,256]{1,0:T(8,128)S(1)}, u32[]{:S(2)}, u32[]{:S(2)}) collective-permute-start(f32[32,256]{1,0:T(8,128)S(1)} %get-tuple-element.76), channel_id=1, source_target_pairs={{0,64},{1,65},{2,66},{3,67},{4,68},{5,69},{6,70},{7,71},{8,72},{9,... | collective-permute-start | bytes 98312 | tf_op jit(solution)/shard_map/ppermute | solution.py:37
  118.9 3.9 %collective-permute-start.25 = (f32[32,256]{1,0:T(8,128)S(1)}, f32[32,256]{1,0:T(8,128)S(1)}, u32[]{:S(2)}, u32[]{:S(2)}) collective-permute-start(f32[32,256]{1,0:T(8,128)S(1)} %get-tuple-element.75), channel_id=1, source_target_pairs={{0,96},{1,97},{2,98},{3,99},{4,100},{5,101},{6,102},{7,103},{8,104... | collective-permute-start | bytes 98312 | tf_op jit(solution)/shard_map/ppermute | solution.py:37
  129.6 24.5 %all-to-all-start.2 = ((bf16[16,160,256]{2,1,0:T(8,128)(2,1)}), bf16[16,160,256]{2,1,0:T(8,128)(2,1)S(1)}, u32[]{:S(2)}, u32[]{:S(2)}) async-start(bf16[16,160,256]{2,1,0:T(8,128)(2,1)} %get-tuple-element.62), calls=%async_computation.2 | async-start | bytes 2621440 | tf_op jit(solution)/shard_map/all_to_all | solution.py:456
  133.3 10.7 %copy-start.16 = (bf16[512,256]{1,0:T(8,128)(2,1)S(1)}, bf16[512,256]{1,0:T(8,128)(2,1)}, u32[]{:S(2)}) copy-start(bf16[512,256]{1,0:T(8,128)(2,1)} %copy-done.15) | copy-start | bytes 786436
  133.3 20.8 %copy-start.8 = (bf16[1024,512]{1,0:T(8,128)(2,1)S(1)}, bf16[1024,512]{1,0:T(8,128)(2,1)}, u32[]{:S(2)}) copy-start(bf16[1024,512]{1,0:T(8,128)(2,1)} %factor.1) | copy-start | bytes 3145732
  133.3 20.8 %copy-start.13 = (s32[123]{0:T(128)S(1)}, s32[123]{0:T(128)}, u32[]{:S(2)}) copy-start(s32[123]{0:T(128)} %shard_map.128.tab.tab_ref) | copy-start | bytes 1480
  143.7 3.2 %collective-permute-start.19 = (f32[512,512]{1,0:T(8,128)}, f32[512,512]{1,0:T(8,128)}, u32[]{:S(2)}, u32[]{:S(2)}) collective-permute-start(f32[512,512]{1,0:T(8,128)} %get-tuple-element.56), channel_id=1, source_target_pairs={{0,1},{1,0},{2,3},{3,2},{4,5},{5,4},{6,7},{7,6},{8,9},{9,8},{10,11... | collective-permute-start | bytes 3145736 | tf_op jit(solution)/shard_map/ppermute | solution.py:37
  144.0 2.9 %collective-permute-start.17 = (bf16[512,256]{1,0:T(8,128)(2,1)S(1)}, bf16[512,256]{1,0:T(8,128)(2,1)}, u32[]{:S(2)}, u32[]{:S(2)}) collective-permute-start(bf16[512,256]{1,0:T(8,128)(2,1)S(1)} %copy-done.16), channel_id=1, source_target_pairs={{0,1},{1,0},{2,3},{3,2},{4,5},{5,4},{6,7},{7,6},{8,9},{9,8},{10,11... | collective-permute-start | bytes 786440 | tf_op jit(solution)/shard_map/ppermute | solution.py:37
  154.2 1.2 copy-start.10
  178.4 17.5 %copy-start.11 = (f32[256,512]{1,0:T(8,128)S(1)}, f32[256,512]{1,0:T(8,128)}, u32[]{:S(2)}) copy-start(f32[256,512]{1,0:T(8,128)} %dinv.1) | copy-start | bytes 1572868
  178.4 17.5 %all-to-all-start.4 = ((bf16[8,128,512]{2,1,0:T(8,128)(2,1)}), bf16[8,128,512]{2,1,0:T(8,128)(2,1)S(1)}, u32[]{:S(2)}, u32[]{:S(2)}) async-start(bf16[8,128,512]{2,1,0:T(8,128)(2,1)} %shard_map.137), calls=%async_computation.4 | async-start | bytes 2097152 | tf_op jit(solution)/shard_map/all_to_all | solution.py:469
  183.1 13.9 %copy-start.17 = (bf16[1024,256]{1,0:T(8,128)(2,1)}, bf16[1024,256]{1,0:T(8,128)(2,1)S(1)}, u32[]{:S(2)}) copy-start(bf16[1024,256]{1,0:T(8,128)(2,1)S(1)} %constant_dynamic-update-slice_fusion) | copy-start | bytes 1572868
